TPU v7x, 32 devices: a whole 2x2x4 slice. The times are simulated.
32 devices in a mesh: az: 4 (over y, x), ta: 8 (over z, core).
Axes of the slice: x: 2, y: 2, z: 4, core: 2. Of those that a mesh axis runs over, the one named last changes fastest.
Arguments:
- initial_field: float32 [16, 1024, 4096], P(None, 'ta', 'az'), may hold values from -6 to 6
- conductivity: bfloat16 [16, 1024, 4096], P(None, 'ta', 'az'), may hold values from 0.25 to 4
- current_density: bfloat16 [16, 1024, 4096], P(None, 'ta', 'az'), may hold values from -6 to 6
- rotor_cycle: bfloat16 [1024, 4096], P('ta', 'az'), may hold values from -6 to 6
- skew_list: int32 [1024], P('ta'), may hold values from 0 to 31
Outputs:
- relaxed: float32 [16, 1024, 4096], P(None, 'ta', 'az')
Inputs may be any that keep to these rules, and one draw needn't show every extreme that they name: `skew_list`: the rotor's offset in whole panels of 128 azimuth cells at each time step.
All inputs are finite; a program needn't handle non-finite values.
Results may differ from a plain program's by a relative error of at most 0.0003.
Values may be sent and summed in bfloat16 or wider, within the bound.
No kernel may reach another device: no remote copies, remote signals or barrier semaphores. Data moves between devices by JAX's collectives and lax.ppermute only.
A program may use at most 192 MiB of HBM per device.

v0:
```python
import functools

import jax
import jax.numpy as jnp
from jax import lax
from jax.experimental import pallas as pl
from jax.experimental.pallas import tpu as pltpu
from jax.sharding import PartitionSpec as P

LANES = 128
EDGE = 8
LAG = 4
VMEM_BYTES = 60 * 1024 * 1024


def checker(rows):
    sub = lax.broadcasted_iota(jnp.int32, (rows, LANES), 0)
    lane = lax.broadcasted_iota(jnp.int32, (rows, LANES), 1)
    return ((sub + lane) & 1) == 0


def f32(value):
    return value.astype(jnp.float32)


def split_high_low(value):
    high = f32(value.astype(jnp.bfloat16))
    return high, value - high


def edges_kernel(
    u_top, u_bot, s_top, s_bot, j_top, j_bot,
    u_left, u_right, s_left, s_right, j_left, j_right,
    to_prev, to_next, to_left, to_right, *, pairs, tiles, blocks,
):
    even8 = checker(8)
    even16 = checker(16)
    sub = lax.broadcasted_iota(jnp.int32, (8, LANES), 0)
    lane = lax.broadcasted_iota(jnp.int32, (16, LANES), 1)
    field_rows = sub < 5

    def pair_rows(m, _):
        for c in range(tiles):
            cols = slice(c * LANES, (c + 1) * LANES)
            for u_ref, s_ref, j_ref, half, out_ref in (
                (u_top, s_top, j_top, 0, to_prev),
                (u_bot, s_bot, j_bot, 8, to_next),
            ):
                eo = []
                for ref in (u_ref, s_ref, j_ref):
                    first = f32(ref[2 * m, :, cols])
                    second = f32(ref[2 * m + 1, :, cols])
                    if first.shape[0] == 16:
                        first = first[half : half + 8]
                        second = second[half : half + 8]
                    eo.append((first, second))
                for colour in (0, 1):
                    pick = [
                        jnp.where(even8, a, b) if colour == 0 else jnp.where(even8, b, a)
                        for a, b in eo
                    ]
                    high, low = split_high_low(pick[0])
                    sig, cur = pick[1], pick[2]
                    if half == 0:
                        sig = pltpu.roll(sig, 5, 0)
                        cur = pltpu.roll(cur, 5, 0)
                    else:
                        high = pltpu.roll(high, 5, 0)
                        low = pltpu.roll(low, 5, 0)
                    both = jnp.concatenate(
                        [jnp.where(field_rows, high, sig), jnp.where(field_rows, low, cur)], 0
                    )
                    out_ref[colour, m, :, cols] = both.astype(jnp.bfloat16)
        return 0

    lax.fori_loop(0, pairs, pair_rows, 0)

    group_of = lane // 8
    first_half = (lane & 7) < 4

    def block_cols(q, _):
        rows = pl.ds(pl.multiple_of(16 * q, 16), 16)
        for refs, out_ref, red_first in (
            ((u_left, s_left, j_left), to_left, False),
            ((u_right, s_right, j_right), to_right, True),
        ):
            packed = []
            for ref in refs:
                acc = [jnp.zeros((8, LANES), jnp.float32)]
                total = acc[0]
                for m in range(pairs):
                    first = f32(ref[2 * m, rows, :])
                    second = f32(ref[2 * m + 1, rows, :])
                    red = jnp.where(even16, first, second)
                    black = jnp.where(even16, second, first)
                    for w in (0, 1):
                        g = m + pairs * w
                        near = pltpu.roll(red[8 * w : 8 * w + 8], (8 * g + 4) % LANES, 1)
                        far = pltpu.roll(black[8 * w : 8 * w + 8], (8 * g + 8) % LANES, 1)
                        if red_first:
                            near_slot, far_slot = 8 * g, 8 * g + 4
                        else:
                            near_slot, far_slot = 8 * g + 4, (8 * g + 8) % LANES
                        l8 = lane[:8]
                        total = jnp.where((l8 >= near_slot) & (l8 < near_slot + 4), near, total)
                        total = jnp.where((l8 >= far_slot) & (l8 < far_slot + 4), far, total)
                packed.append(total)
            high, low = split_high_low(packed[0])
            out_ref[q, 0] = jnp.concatenate([high, low], 0).astype(jnp.bfloat16)
            out_ref[q, 1] = jnp.concatenate([packed[1], packed[2]], 0).astype(jnp.bfloat16)
        return 0

    lax.fori_loop(0, blocks, block_cols, 0)


def pack_edges(field, sigma, current):
    layers, rows, cols = field.shape
    pairs, tiles, blocks = layers // 2, cols // LANES, rows // 16

    def whole(shape, index):
        return pl.BlockSpec(shape, lambda i: index)

    def row_specs(height):
        return [
            whole((layers, height, cols), (0, 0, 0)),
            whole((layers, height, cols), (0, rows // height - 1, 0)),
        ]

    col_specs = [
        whole((layers, rows, LANES), (0, 0, 0)),
        whole((layers, rows, LANES), (0, 0, tiles - 1)),
    ]
    ta_shape = (2, pairs, 16, cols)
    az_shape = (blocks, 2, 16, LANES)
    return pl.pallas_call(
        functools.partial(edges_kernel, pairs=pairs, tiles=tiles, blocks=blocks),
        grid=(1,),
        in_specs=row_specs(8) + row_specs(16) * 2 + col_specs * 3,
        out_specs=[whole(ta_shape, (0,) * 4)] * 2 + [whole(az_shape, (0,) * 4)] * 2,
        out_shape=[jax.ShapeDtypeStruct(ta_shape, jnp.bfloat16)] * 2
        + [jax.ShapeDtypeStruct(az_shape, jnp.bfloat16)] * 2,
        compiler_params=pltpu.CompilerParams(vmem_limit_bytes=VMEM_BYTES),
        name="edges",
    )(
        field, field, sigma, sigma, current, current,
        field, field, sigma, sigma, current, current,
    )


def relax_kernel(*refs, slots, pairs, rows, tiles):
    rotor = refs[:slots]
    (skew, from_left, from_right, corner_prev, corner_next, from_prev, from_next,
     u_ref, s_ref, j_ref, out_ref,
     red_a, red_b, black_a, black_b, sig_r, sig_b, cur_r, cur_b, side) = refs[slots:]
    g = pl.program_id(0)
    ext = rows + 2 * EDGE
    blocks = rows // 16
    even8 = checker(8)
    even16 = checker(16)
    lane = lax.broadcasted_iota(jnp.int32, (8, LANES), 1)
    lane16 = lax.broadcasted_iota(jnp.int32, (16, LANES), 1)
    lane_first = lane == 0
    lane_last = lane == LANES - 1

    @pl.when(g == 0)
    def prologue():
        panels = slots * tiles
        bits = (panels - 1).bit_length()
        want = [(panels - tiles - 1 + p) % panels for p in range(tiles + 2)]
        needs = [set(want)]
        for bit in range(bits):
            needs.append(needs[-1] | {(q - (1 << bit)) % panels for q in needs[-1]})

        def rotor_rows(b, _):
            at = pl.ds(pl.multiple_of(16 * b, 16), 16)
            turn = skew[at, :]
            cur = {}
            for q in sorted(needs[bits]):
                source = rotor[slots - 1 - q // tiles]
                c = q % tiles
                cur[q] = f32(source[at, c * LANES : (c + 1) * LANES])
            for bit in reversed(range(bits)):
                on = ((turn >> bit) & 1) == 1
                cur = {q: jnp.where(on, cur[(q - (1 << bit)) % panels], cur[q]) for q in sorted(needs[bit])}
            placed = [cur[want[p + 1]] for p in range(tiles)]
            placed.append(jnp.where(lane16 < LANES // 2, cur[want[tiles + 1]], cur[want[0]]))
            zero = jnp.zeros((16, LANES), jnp.float32)
            for buf in (red_a, red_b, black_a, black_b):
                for c in range(tiles + 1):
                    buf[0, c, at, :] = placed[c]
                    buf[pairs + 1, c, at, :] = zero
            return 0

        lax.fori_loop(0, ext // 16, rotor_rows, 0)

        left_slot = (lane & 7) < 4

        def decode(q, left, right):
            left0, left1, right0, right1 = f32(left[0]), f32(left[1]), f32(right[0]), f32(right[1])
            items = (
                (left0[:8] + left0[8:], right0[:8] + right0[8:], 1.0),
                (left1[:8], right1[:8], 1.0 / 48.0),
                (left1[8:], right1[8:], 0.25),
            )
            for item, (a, b, scale) in enumerate(items):
                side[0, item, q] = jnp.where(left_slot, a, b) * scale
                side[1, item, q] = jnp.where(left_slot, b, a) * scale

        for q in range(blocks):
            decode(q, from_left[q], from_right[q])
        decode(blocks, corner_prev[0], corner_prev[1])
        decode(blocks + 1, corner_next[0], corner_next[1])

    @pl.when(g < pairs)
    def load():
        m = g
        fields = ((red_a, sig_r, cur_r), (black_a, sig_b, cur_b))
        for colour in (0, 1):
            u_dst, s_dst, j_dst = fields[colour]
            for c in range(tiles):
                cols = slice(c * LANES, (c + 1) * LANES)
                both = f32(from_prev[colour, 0, :, cols])
                u_dst[m + 1, c, pl.ds(EDGE - 5, 8), :] = both[:8] + both[8:]
                s_dst[m, c, pl.ds(0, 8), :] = both[:8] * (1.0 / 48.0)
                j_dst[m, c, pl.ds(0, 8), :] = both[8:] * 0.25
                both = f32(from_next[colour, 0, :, cols])
                u_dst[m + 1, c, pl.ds(EDGE + rows, 8), :] = both[:8] + both[8:]
                s_dst[m, c, pl.ds(EDGE + rows - 5, 8), :] = both[:8] * (1.0 / 48.0)
                j_dst[m, c, pl.ds(EDGE + rows - 5, 8), :] = both[8:] * 0.25

        def own_rows(q, _):
            at = pl.ds(pl.multiple_of(16 * q, 16), 16)
            to = pl.ds(pl.multiple_of(16 * q + EDGE, 8), 16)
            for c in range(tiles):
                cols = slice(c * LANES, (c + 1) * LANES)
                a, b = u_ref[0, at, cols], u_ref[1, at, cols]
                red_a[m + 1, c, to, :] = jnp.where(even16, a, b)
                black_a[m + 1, c, to, :] = jnp.where(even16, b, a)
                a, b = f32(s_ref[0, at, cols]) * (1.0 / 48.0), f32(s_ref[1, at, cols]) * (1.0 / 48.0)
                sig_r[m, c, to, :] = jnp.where(even16, a, b)
                sig_b[m, c, to, :] = jnp.where(even16, b, a)
                a, b = f32(j_ref[0, at, cols]) * 0.25, f32(j_ref[1, at, cols]) * 0.25
                cur_r[m, c, to, :] = jnp.where(even16, a, b)
                cur_b[m, c, to, :] = jnp.where(even16, b, a)
            return 0

        lax.fori_loop(0, blocks, own_rows, 0)

        for colour in (0, 1):
            u_dst, s_dst, j_dst = fields[colour]
            for item, (dst, plane) in enumerate(((u_dst, m + 1), (s_dst, m), (j_dst, m))):
                for w in (0, 1):
                    turn = lax.rem(2 * LANES + 124 - 4 * colour - 8 * (m + pairs * w), LANES)
                    for q in range(blocks):
                        dst[plane, tiles, pl.ds(EDGE + 16 * q + 8 * w, 8), :] = pltpu.roll(side[colour, item, q], turn, 1)
                    if w == 1:
                        dst[plane, tiles, pl.ds(0, 8), :] = pltpu.roll(side[colour, item, blocks], turn, 1)
                    else:
                        dst[plane, tiles, pl.ds(EDGE + rows, 8), :] = pltpu.roll(side[colour, item, blocks + 1], turn, 1)

    def half_step(m, colour, own, other, sig, cur, start, count, write):
        def body(r, _):
            at = start + 8 * r
            centre = [other[m + 1, c, pl.ds(at, 8), :] for c in range(tiles + 1)]
            ahead = [pltpu.roll(x, 1, 1) for x in centre]
            back = [pltpu.roll(x, LANES - 1, 1) for x in centre]
            outputs = tiles if write is not None and count * 8 == rows else tiles + 1
            for c in range(outputs):
                left = jnp.where(lane_first, ahead[c - 1], ahead[c])
                right = jnp.where(lane_last, back[(c + 1) % (tiles + 1)], back[c])
                below = other[m, c, pl.ds(at, 8), :]
                above = other[m + 2, c, pl.ds(at, 8), :]
                outer = jnp.where(even8, below, above) if colour == 0 else jnp.where(even8, above, below)
                near = other[m + 1, c, pl.ds(at + 1, 8), :] - other[m + 1, c, pl.ds(at - 1, 8), :]
                far = own[m + 1, c, pl.ds(at + 2, 8), :] - own[m + 1, c, pl.ds(at - 2, 8), :]
                total = (left + right) + (centre[c] + outer)
                new = cur[m, c, pl.ds(at, 8), :] + 0.25 * total - sig[m, c, pl.ds(at, 8), :] * (8.0 * near - far)
                write(m, c, at, r, new)
            return 0

        lax.fori_loop(0, count, body, 0)

    def keep(buf):
        def write(m, c, at, r, new):
            buf[m + 1, c, pl.ds(at, 8), :] = new

        return write

    def emit(m, c, at, r, new):
        red = red_a[m + 1, c, pl.ds(at, 8), :]
        cols = slice(c * LANES, (c + 1) * LANES)
        to = pl.ds(pl.multiple_of(8 * r, 8), 8)
        out_ref[0, to, cols] = jnp.where(even8, red, new)
        out_ref[1, to, cols] = jnp.where(even8, new, red)

    wide = (EDGE - 4, rows // 8 + 1)
    plan = (
        (1, 0, red_a, black_a, sig_r, cur_r, wide, keep(red_b)),
        (2, 1, black_a, red_b, sig_b, cur_b, wide, keep(black_b)),
        (3, 0, red_b, black_b, sig_r, cur_r, wide, keep(red_a)),
        (4, 1, black_b, red_a, sig_b, cur_b, (EDGE, rows // 8), emit),
    )
    for lag, colour, own, other, sig, cur, (start, count), write in plan:

        @pl.when((g >= lag) & (g < pairs + lag))
        def phase(lag=lag, colour=colour, own=own, other=other, sig=sig, cur=cur, start=start, count=count, write=write):
            half_step(g - lag, colour, own, other, sig, cur, start, count, write)


def relax(rotor, skew, from_left, from_right, corner_prev, corner_next, from_prev, from_next, field, sigma, current):
    layers, rows, cols = field.shape
    pairs, tiles, slots = layers // 2, cols // LANES, len(rotor)
    ext = rows + 2 * EDGE

    def whole(array):
        zeros = (0,) * array.ndim
        return pl.BlockSpec(array.shape, lambda g: zeros)

    def coming(g):
        return jnp.minimum(g, pairs - 1)

    halo = pl.BlockSpec((2, 1, 16, cols), lambda g: (0, coming(g), 0, 0))
    block = pl.BlockSpec((2, rows, cols), lambda g: (coming(g), 0, 0))
    fixed = list(rotor) + [skew, from_left, from_right, corner_prev, corner_next]
    state = pltpu.VMEM((pairs + 2, tiles + 1, ext, LANES), jnp.float32)
    coef = pltpu.VMEM((pairs, tiles + 1, ext, LANES), jnp.float32)
    return pl.pallas_call(
        functools.partial(relax_kernel, slots=slots, pairs=pairs, rows=rows, tiles=tiles),
        grid=(pairs + LAG,),
        in_specs=[whole(a) for a in fixed] + [halo, halo, block, block, block],
        out_specs=pl.BlockSpec((2, rows, cols), lambda g: (jnp.maximum(g - LAG, 0), 0, 0)),
        out_shape=jax.ShapeDtypeStruct(field.shape, jnp.float32),
        scratch_shapes=[state] * 4 + [coef] * 4 + [pltpu.VMEM((2, 3, rows // 16 + 2, 8, LANES), jnp.float32)],
        compiler_params=pltpu.CompilerParams(vmem_limit_bytes=VMEM_BYTES),
        name="relax",
    )(*fixed, from_prev, from_next, field, sigma, current)


def moved(value, axis, steps):
    count = lax.axis_size(axis)
    return lax.ppermute(value, axis, [(i, (i + steps) % count) for i in range(count)])


def local(field, sigma, current, rotor_cycle, skew_list):
    rows = field.shape[1]
    rotor = jnp.concatenate(
        [moved(rotor_cycle[rows - EDGE :], "ta", 1), rotor_cycle, moved(rotor_cycle[:EDGE], "ta", -1)], 0
    )
    skew = jnp.concatenate(
        [moved(skew_list[rows - EDGE :], "ta", 1), skew_list, moved(skew_list[:EDGE], "ta", -1)], 0
    )
    skew = jnp.broadcast_to(skew[:, None], (rows + 2 * EDGE, LANES))
    to_prev, to_next, to_left, to_right = pack_edges(field, sigma, current)
    from_left = moved(to_right, "az", 1)
    from_right = moved(to_left, "az", -1)
    from_prev = moved(to_next, "ta", 1)
    from_next = moved(to_prev, "ta", -1)
    corner_prev = moved(jnp.stack([from_left[-1], from_right[-1]]), "ta", 1)
    corner_next = moved(jnp.stack([from_left[0], from_right[0]]), "ta", -1)
    slots = [rotor] + [moved(rotor, "az", s) for s in range(1, lax.axis_size("az"))]
    return relax(
        slots, skew, from_left, from_right, corner_prev, corner_next, from_prev, from_next, field, sigma, current
    )


def solution(mesh):
    placed = (P(None, "ta", "az"), P(None, "ta", "az"), P(None, "ta", "az"), P("ta", "az"), P("ta"))
    return jax.shard_map(
        local, mesh=mesh, in_specs=placed, out_specs=P(None, "ta", "az"), check_vma=False
    )
```

profile of v0, /device:TPU:0, one launch (start us, length us, event | category | flops | bytes accessed | tf_op | source)
XLA Modules:
  0.0 108.4 jit_solution(10381138297291337161)
XLA Ops:
  0.0 0.7 fusion
  0.7 0.5 collective-permute-start
  1.2 0.8 fusion.3
  2.0 2.7 %collective-permute-start.5 = (s32[8]{0:T(128)S(1)}, s32[8]{0:T(128)S(1)}, u32[]{:S(2)}, u32[]{:S(2)}) collective-permute-start(s32[8]{0:T(128)S(1)} %get-tuple-element.19), channel_id=1, source_target_pairs={{0,1},{1,2},{2,3},{3,4},{4,5},{5,6},{6,7},{7,0},{8,9},{9,10},{10,1... | collective-permute-start | bytes 104 | tf_op jit(solution)/shard_map/ppermute | solution.py:341
  4.7 0.0 copy-start.2
  4.7 0.0 copy-start.11
  4.7 1.4 %collective-permute-start.1 = (bf16[8,1024]{1,0:T(8,128)(2,1)S(1)}, bf16[8,1024]{1,0:T(8,128)(2,1)S(1)}, u32[]{:S(2)}, u32[]{:S(2)}) collective-permute-start(bf16[8,1024]{1,0:T(8,128)(2,1)S(1)} %get-tuple-element.13), channel_id=1, source_target_pairs={{0,7},{1,0},{2,1},{3,2},{4,3},{5,4},{6,5},{7,6},{8,15},{9,8},{10,9... | collective-permute-start | bytes 49160 | tf_op jit(solution)/shard_map/ppermute | solution.py:341
  6.1 6.2 %edges.1 = (bf16[2,8,16,1024]{3,2,1,0:T(8,128)(2,1)}, bf16[2,8,16,1024]{3,2,1,0:T(8,128)(2,1)}, bf16[8,2,16,128]{3,2,1,0:T(8,128)(2,1)}, bf16[8,2,16,128]{3,2,1,0:T(8,128)(2,1)}) custom-call(f32[16,128,1024]{2,1,0:T(8,128)} %refs_11_.1, f32[16,128,1024]{2,1,0:T(8,128)} %refs_11_.1, bf16[16,128,1024]{2,1,0:T(8,128)(2,1)} %refs_12_.1, ...), custom_call_target="tpu_custom_call" | custom-call | tf_op jit(solution)/shard_map/edges/pallas_call | solution.py:135
  12.3 2.0 %collective-permute-start.7 = (bf16[8,2,16,128]{3,2,1,0:T(8,128)(2,1)}, bf16[8,2,16,128]{3,2,1,0:T(8,128)(2,1)S(1)}, u32[]{:S(2)}, u32[]{:S(2)}) collective-permute-start(bf16[8,2,16,128]{3,2,1,0:T(8,128)(2,1)} %get-tuple-element.9), channel_id=1, source_target_pairs={{0,8},{8,16},{16,24},{24,0},{1,9},{9,17},{17,25},{25,1},{2,10},{10... | collective-permute-start | bytes 196616 | tf_op jit(solution)/shard_map/ppermute | solution.py:341
  14.3 1.0 collective-permute-start.8
  15.3 0.0 collective-permute-done
  15.3 0.0 collective-permute-start.11
  15.3 0.0 copy-done.2
  15.4 2.4 %collective-permute-done.7.refs_5_ = bf16[8,2,16,128]{3,2,1,0:T(8,128)(2,1)S(1)} collective-permute-done((bf16[8,2,16,128]{3,2,1,0:T(8,128)(2,1)}, bf16[8,2,16,128]{3,2,1,0:T(8,128)(2,1)S(1)}, u32[]{:S(2)}, u32[]{:S(2)}) %collective-permute-start.7) | collective-permute-done | bytes 65568 | tf_op jit(solution)/shard_map/ppermute | solution.py:341
  17.8 1.2 %collective-permute-start.12 = (bf16[2,8,16,1024]{3,2,1,0:T(8,128)(2,1)}, bf16[2,8,16,1024]{3,2,1,0:T(8,128)(2,1)S(1)}, u32[]{:S(2)}, u32[]{:S(2)}) collective-permute-start(bf16[2,8,16,1024]{3,2,1,0:T(8,128)(2,1)} %get-tuple-element.12), channel_id=1, source_target_pairs={{0,7},{1,0},{2,1},{3,2},{4,3},{5,4},{6,5},{7,6},{8,15},{9,8},{10,9... | collective-permute-start | bytes 1572872 | tf_op jit(solution)/shard_map/ppermute | solution.py:341
  19.0 0.0 collective-permute-done.8.refs_6_
  19.0 0.1 collective-permute-start.9
  19.1 0.0 collective-permute-done.1
  19.1 3.5 %collective-permute-start.10 = (bf16[2,2,16,128]{3,2,1,0:T(8,128)(2,1)S(1)}, bf16[2,2,16,128]{3,2,1,0:T(8,128)(2,1)S(1)}, u32[]{:S(2)}, u32[]{:S(2)}) collective-permute-start(bf16[2,2,16,128]{3,2,1,0:T(8,128)(2,1)S(1)} %pad_maximum_fusion.1), channel_id=1, source_target_pairs={{0,7},{1,0},{2,1},{3,2},{4,3},{5,4},{6,5},{7,6},{8,15},{9,8},{10,9... | collective-permute-start | bytes 49160 | tf_op jit(solution)/shard_map/ppermute | solution.py:341
  22.6 0.0 collective-permute-done.5
  22.6 0.1 collective-permute-start.6
  22.7 5.2 %collective-permute-done.6 = s32[8]{0:T(128)S(1)} collective-permute-done((s32[8]{0:T(128)S(1)}, s32[8]{0:T(128)S(1)}, u32[]{:S(2)}, u32[]{:S(2)}) %collective-permute-start.6) | collective-permute-done | bytes 64 | tf_op jit(solution)/shard_map/ppermute | solution.py:341
  27.9 1.5 %collective-permute-start.4 = (bf16[144,1024]{1,0:T(8,128)(2,1)S(1)}, bf16[144,1024]{1,0:T(8,128)(2,1)S(1)}, u32[]{:S(2)}, u32[]{:S(2)}) collective-permute-start(bf16[144,1024]{1,0:T(8,128)(2,1)S(1)} %constant_dynamic-update-slice_fusion.refs_0_), channel_id=1, source_target_pairs={{0,24},{8,0},{16,8},{24,16},{1,25},{9,1},{17,9},{25,17},{2,26},{10... | collective-permute-start | bytes 884744 | tf_op jit(solution)/shard_map/ppermute | solution.py:341
  29.5 0.9 collective-permute-done.9.refs_7_
  30.4 2.5 %collective-permute-start.3 = (bf16[144,1024]{1,0:T(8,128)(2,1)S(1)}, bf16[144,1024]{1,0:T(8,128)(2,1)S(1)}, u32[]{:S(2)}, u32[]{:S(2)}) collective-permute-start(bf16[144,1024]{1,0:T(8,128)(2,1)S(1)} %constant_dynamic-update-slice_fusion.refs_0_), channel_id=1, source_target_pairs={{0,16},{8,24},{16,0},{24,8},{1,17},{9,25},{17,1},{25,9},{2,18},{10... | collective-permute-start | bytes 884744 | tf_op jit(solution)/shard_map/ppermute | solution.py:341
  32.8 0.0 collective-permute-done.10.refs_8_
  32.8 0.6 collective-permute-start.2
  33.4 0.0 copy-done.11
  33.4 0.1 pad_add_fusion
  33.5 1.3 %collective-permute-done.4.refs_3_ = bf16[144,1024]{1,0:T(8,128)(2,1)S(1)} collective-permute-done((bf16[144,1024]{1,0:T(8,128)(2,1)S(1)}, bf16[144,1024]{1,0:T(8,128)(2,1)S(1)}, u32[]{:S(2)}, u32[]{:S(2)}) %collective-permute-start.4) | collective-permute-done | bytes 294944 | tf_op jit(solution)/shard_map/ppermute | solution.py:341
  34.9 11.5 %collective-permute-done.3.refs_2_ = bf16[144,1024]{1,0:T(8,128)(2,1)S(1)} collective-permute-done((bf16[144,1024]{1,0:T(8,128)(2,1)S(1)}, bf16[144,1024]{1,0:T(8,128)(2,1)S(1)}, u32[]{:S(2)}, u32[]{:S(2)}) %collective-permute-start.3) | collective-permute-done | bytes 294944 | tf_op jit(solution)/shard_map/ppermute | solution.py:341
  46.4 0.0 collective-permute-done.2.refs_1_
  46.4 0.0 collective-permute-done.11.refs_9_
  46.4 0.0 copy-start
  46.4 0.0 collective-permute-done.12.refs_10_
  46.4 0.0 copy-start.1
  46.4 0.8 broadcast_in_dim.2.refs_4_
  47.3 0.0 copy-done.7
  47.3 0.0 copy-done.8
  47.3 0.0 copy-done.3
  47.3 0.0 copy-done.9
  47.3 0.0 copy-done.10
  47.3 0.0 copy-done.4
  47.3 0.0 copy-done.5
  47.3 0.0 copy-done.6
  47.3 0.1 copy-done
  47.4 0.2 copy-done.1
  47.6 60.8 %relax.1 = f32[16,128,1024]{2,1,0:T(8,128)} custom-call(bf16[144,1024]{1,0:T(8,128)(2,1)} %copy-done.3, bf16[144,1024]{1,0:T(8,128)(2,1)} %copy-done.6, bf16[144,1024]{1,0:T(8,128)(2,1)} %copy-done.5, bf16[144,1024]{1,0:T(8,128)(2,1)} %copy-done.4, s32[144,128]{1,0:T(8,128)} %broadcast_in_dim.2.refs_4_, bf16[8,2,16,128]{3,2,1,0:T(8,128)(2,1)} %copy-done.7, ...), custom_call_target="tpu_custom_call" | custom-call | tf_op jit(solution)/shard_map/relax/pallas_call | solution.py:327
  (15 shorter events, 0.1 us)
Async XLA Ops:
  0.7 14.6 %collective-permute-start = (bf16[8,1024]{1,0:T(8,128)(2,1)S(1)}, bf16[8,1024]{1,0:T(8,128)(2,1)S(1)}, u32[]{:S(2)}, u32[]{:S(2)}) collective-permute-start(bf16[8,1024]{1,0:T(8,128)(2,1)S(1)} %get-tuple-element.14), channel_id=1, source_target_pairs={{0,1},{1,2},{2,3},{3,4},{4,5},{5,6},{6,7},{7,0},{8,9},{9,10},{10,1... | collective-permute-start | bytes 49160 | tf_op jit(solution)/shard_map/ppermute | solution.py:341
  2.0 20.6 %collective-permute-start.5 = (s32[8]{0:T(128)S(1)}, s32[8]{0:T(128)S(1)}, u32[]{:S(2)}, u32[]{:S(2)}) collective-permute-start(s32[8]{0:T(128)S(1)} %get-tuple-element.19), channel_id=1, source_target_pairs={{0,1},{1,2},{2,3},{3,4},{4,5},{5,6},{6,7},{7,0},{8,9},{9,10},{10,1... | collective-permute-start | bytes 104 | tf_op jit(solution)/shard_map/ppermute | solution.py:341
  4.7 10.6 %copy-start.2 = (bf16[128,1024]{1,0:T(8,128)(2,1)S(1)}, bf16[128,1024]{1,0:T(8,128)(2,1)}, u32[]{:S(2)}) copy-start(bf16[128,1024]{1,0:T(8,128)(2,1)} %param.8) | copy-start | bytes 786436
  4.7 28.8 %copy-start.11 = (s32[128]{0:T(128)S(1)}, s32[128]{0:T(128)}, u32[]{:S(2)}) copy-start(s32[128]{0:T(128)} %param.9) | copy-start | bytes 1540
  4.7 14.4 %collective-permute-start.1 = (bf16[8,1024]{1,0:T(8,128)(2,1)S(1)}, bf16[8,1024]{1,0:T(8,128)(2,1)S(1)}, u32[]{:S(2)}, u32[]{:S(2)}) collective-permute-start(bf16[8,1024]{1,0:T(8,128)(2,1)S(1)} %get-tuple-element.13), channel_id=1, source_target_pairs={{0,7},{1,0},{2,1},{3,2},{4,3},{5,4},{6,5},{7,6},{8,15},{9,8},{10,9... | collective-permute-start | bytes 49160 | tf_op jit(solution)/shard_map/ppermute | solution.py:341
  12.3 5.5 %collective-permute-start.7 = (bf16[8,2,16,128]{3,2,1,0:T(8,128)(2,1)}, bf16[8,2,16,128]{3,2,1,0:T(8,128)(2,1)S(1)}, u32[]{:S(2)}, u32[]{:S(2)}) collective-permute-start(bf16[8,2,16,128]{3,2,1,0:T(8,128)(2,1)} %get-tuple-element.9), channel_id=1, source_target_pairs={{0,8},{8,16},{16,24},{24,0},{1,9},{9,17},{17,25},{25,1},{2,10},{10... | collective-permute-start | bytes 196616 | tf_op jit(solution)/shard_map/ppermute | solution.py:341
  14.3 4.7 %collective-permute-start.8 = (bf16[8,2,16,128]{3,2,1,0:T(8,128)(2,1)}, bf16[8,2,16,128]{3,2,1,0:T(8,128)(2,1)S(1)}, u32[]{:S(2)}, u32[]{:S(2)}) collective-permute-start(bf16[8,2,16,128]{3,2,1,0:T(8,128)(2,1)} %get-tuple-element.10), channel_id=1, source_target_pairs={{0,24},{8,0},{16,8},{24,16},{1,25},{9,1},{17,9},{25,17},{2,26},{10... | collective-permute-start | bytes 196616 | tf_op jit(solution)/shard_map/ppermute | solution.py:341
  15.3 31.1 %collective-permute-start.11 = (bf16[2,8,16,1024]{3,2,1,0:T(8,128)(2,1)}, bf16[2,8,16,1024]{3,2,1,0:T(8,128)(2,1)S(1)}, u32[]{:S(2)}, u32[]{:S(2)}) collective-permute-start(bf16[2,8,16,1024]{3,2,1,0:T(8,128)(2,1)} %get-tuple-element.11), channel_id=1, source_target_pairs={{0,1},{1,2},{2,3},{3,4},{4,5},{5,6},{6,7},{7,0},{8,9},{9,10},{10,1... | collective-permute-start | bytes 1572872 | tf_op jit(solution)/shard_map/ppermute | solution.py:341
  17.8 29.5 %copy-start.7 = (bf16[8,2,16,128]{3,2,1,0:T(8,128)(2,1)}, bf16[8,2,16,128]{3,2,1,0:T(8,128)(2,1)S(1)}, u32[]{:S(2)}) copy-start(bf16[8,2,16,128]{3,2,1,0:T(8,128)(2,1)S(1)} %collective-permute-done.7.refs_5_) | copy-start | bytes 196612
  17.8 28.6 %collective-permute-start.12 = (bf16[2,8,16,1024]{3,2,1,0:T(8,128)(2,1)}, bf16[2,8,16,1024]{3,2,1,0:T(8,128)(2,1)S(1)}, u32[]{:S(2)}, u32[]{:S(2)}) collective-permute-start(bf16[2,8,16,1024]{3,2,1,0:T(8,128)(2,1)} %get-tuple-element.12), channel_id=1, source_target_pairs={{0,7},{1,0},{2,1},{3,2},{4,3},{5,4},{6,5},{7,6},{8,15},{9,8},{10,9... | collective-permute-start | bytes 1572872 | tf_op jit(solution)/shard_map/ppermute | solution.py:341
  19.0 28.3 %copy-start.8 = (bf16[8,2,16,128]{3,2,1,0:T(8,128)(2,1)}, bf16[8,2,16,128]{3,2,1,0:T(8,128)(2,1)S(1)}, u32[]{:S(2)}) copy-start(bf16[8,2,16,128]{3,2,1,0:T(8,128)(2,1)S(1)} %collective-permute-done.8.refs_6_) | copy-start | bytes 196612
  19.0 11.4 %collective-permute-start.9 = (bf16[2,2,16,128]{3,2,1,0:T(8,128)(2,1)S(1)}, bf16[2,2,16,128]{3,2,1,0:T(8,128)(2,1)S(1)}, u32[]{:S(2)}, u32[]{:S(2)}) collective-permute-start(bf16[2,2,16,128]{3,2,1,0:T(8,128)(2,1)S(1)} %pad_maximum_fusion), channel_id=1, source_target_pairs={{0,1},{1,2},{2,3},{3,4},{4,5},{5,6},{6,7},{7,0},{8,9},{9,10},{10,1... | collective-permute-start | bytes 49160 | tf_op jit(solution)/shard_map/ppermute | solution.py:341
  19.1 13.8 %collective-permute-start.10 = (bf16[2,2,16,128]{3,2,1,0:T(8,128)(2,1)S(1)}, bf16[2,2,16,128]{3,2,1,0:T(8,128)(2,1)S(1)}, u32[]{:S(2)}, u32[]{:S(2)}) collective-permute-start(bf16[2,2,16,128]{3,2,1,0:T(8,128)(2,1)S(1)} %pad_maximum_fusion.1), channel_id=1, source_target_pairs={{0,7},{1,0},{2,1},{3,2},{4,3},{5,4},{6,5},{7,6},{8,15},{9,8},{10,9... | collective-permute-start | bytes 49160 | tf_op jit(solution)/shard_map/ppermute | solution.py:341
  22.6 24.7 %copy-start.3 = (bf16[144,1024]{1,0:T(8,128)(2,1)}, bf16[144,1024]{1,0:T(8,128)(2,1)S(1)}, u32[]{:S(2)}) copy-start(bf16[144,1024]{1,0:T(8,128)(2,1)S(1)} %constant_dynamic-update-slice_fusion.refs_0_) | copy-start | bytes 884740
  22.6 5.3 %collective-permute-start.6 = (s32[8]{0:T(128)S(1)}, s32[8]{0:T(128)S(1)}, u32[]{:S(2)}, u32[]{:S(2)}) collective-permute-start(s32[8]{0:T(128)S(1)} %get-tuple-element.20), channel_id=1, source_target_pairs={{0,7},{1,0},{2,1},{3,2},{4,3},{5,4},{6,5},{7,6},{8,15},{9,8},{10,9... | collective-permute-start | bytes 104 | tf_op jit(solution)/shard_map/ppermute | solution.py:341
  27.9 6.9 %collective-permute-start.4 = (bf16[144,1024]{1,0:T(8,128)(2,1)S(1)}, bf16[144,1024]{1,0:T(8,128)(2,1)S(1)}, u32[]{:S(2)}, u32[]{:S(2)}) collective-permute-start(bf16[144,1024]{1,0:T(8,128)(2,1)S(1)} %constant_dynamic-update-slice_fusion.refs_0_), channel_id=1, source_target_pairs={{0,24},{8,0},{16,8},{24,16},{1,25},{9,1},{17,9},{25,17},{2,26},{10... | collective-permute-start | bytes 884744 | tf_op jit(solution)/shard_map/ppermute | solution.py:341
  30.3 16.9 %copy-start.9 = (bf16[2,2,16,128]{3,2,1,0:T(8,128)(2,1)}, bf16[2,2,16,128]{3,2,1,0:T(8,128)(2,1)S(1)}, u32[]{:S(2)}) copy-start(bf16[2,2,16,128]{3,2,1,0:T(8,128)(2,1)S(1)} %collective-permute-done.9.refs_7_) | copy-start | bytes 49156
  30.4 16.1 %collective-permute-start.3 = (bf16[144,1024]{1,0:T(8,128)(2,1)S(1)}, bf16[144,1024]{1,0:T(8,128)(2,1)S(1)}, u32[]{:S(2)}, u32[]{:S(2)}) collective-permute-start(bf16[144,1024]{1,0:T(8,128)(2,1)S(1)} %constant_dynamic-update-slice_fusion.refs_0_), channel_id=1, source_target_pairs={{0,16},{8,24},{16,0},{24,8},{1,17},{9,25},{17,1},{25,9},{2,18},{10... | collective-permute-start | bytes 884744 | tf_op jit(solution)/shard_map/ppermute | solution.py:341
  32.8 14.4 %copy-start.10 = (bf16[2,2,16,128]{3,2,1,0:T(8,128)(2,1)}, bf16[2,2,16,128]{3,2,1,0:T(8,128)(2,1)S(1)}, u32[]{:S(2)}) copy-start(bf16[2,2,16,128]{3,2,1,0:T(8,128)(2,1)S(1)} %collective-permute-done.10.refs_8_) | copy-start | bytes 49156
  32.8 13.6 %collective-permute-start.2 = (bf16[144,1024]{1,0:T(8,128)(2,1)S(1)}, bf16[144,1024]{1,0:T(8,128)(2,1)S(1)}, u32[]{:S(2)}, u32[]{:S(2)}) collective-permute-start(bf16[144,1024]{1,0:T(8,128)(2,1)S(1)} %constant_dynamic-update-slice_fusion.refs_0_), channel_id=1, source_target_pairs={{0,8},{8,16},{16,24},{24,0},{1,9},{9,17},{17,25},{25,1},{2,10},{10... | collective-permute-start | bytes 884744 | tf_op jit(solution)/shard_map/ppermute | solution.py:341
  34.9 12.4 %copy-start.4 = (bf16[144,1024]{1,0:T(8,128)(2,1)}, bf16[144,1024]{1,0:T(8,128)(2,1)S(1)}, u32[]{:S(2)}) copy-start(bf16[144,1024]{1,0:T(8,128)(2,1)S(1)} %collective-permute-done.4.refs_3_) | copy-start | bytes 884740
  46.4 0.9 copy-start.5
  46.4 0.9 copy-start.6
  46.4 1.0 copy-start
  46.4 1.2 %copy-start.1 = (bf16[2,8,16,1024]{3,2,1,0:T(8,128)(2,1)}, bf16[2,8,16,1024]{3,2,1,0:T(8,128)(2,1)S(1)}, u32[]{:S(2)}) copy-start(bf16[2,8,16,1024]{3,2,1,0:T(8,128)(2,1)S(1)} %collective-permute-done.12.refs_10_) | copy-start | bytes 1572868
where the time goes:
time: 109 us; the launch traced here: 108 us
  Pallas kernels  67.1 us (62%)
  waiting for transfers between devices  21.5 us (20%)
  starting transfers between devices  17 us (16%)
  local copies, waits for them, and re-layouts  2.72 us (2%)
    pallas_call x1, Pallas kernels, relax(): pl.pallas_call(functools.partial(relax_kernel, slots=slots, pairs=pairs,...  60.8 us
    ppermute x13, waiting for transfers between devices, moved(): lax.ppermute(value, axis, [(i, (i + steps) % count) for i in range(count)])  21.5 us
    ppermute x13, starting transfers between devices, moved(): lax.ppermute(value, axis, [(i, (i + steps) % count) for i in range(count)])  17 us
    pallas_call x1, Pallas kernels, pack_edges(): pl.pallas_call(functools.partial(edges_kernel, pairs=pairs, tiles=tiles,...  6.23 us
  transfers between devices with their start and end apart: 13, of which 5 were waited for; matrix products, arithmetic and copies ran while one was open for 1% of the time, Pallas kernels for 6%

commit v1 on v0

--- a/solution.py
+++ b/solution.py
@@ -10,6 +10,8 @@
 LANES = 128
 EDGE = 8
 LAG = 4
+UNROLL = 6
+SPANS = 3
 VMEM_BYTES = 60 * 1024 * 1024
 
 
@@ -148,12 +150,11 @@
 
 
 def relax_kernel(*refs, slots, pairs, rows, tiles):
-    rotor = refs[:slots]
-    (skew, from_left, from_right, corner_prev, corner_next, from_prev, from_next,
+    rotor, rotor_edge = refs[:slots], refs[slots : 2 * slots]
+    (skew, skew_edge, from_left, from_right, corner_prev, corner_next, from_prev, from_next,
      u_ref, s_ref, j_ref, out_ref,
-     red_a, red_b, black_a, black_b, sig_r, sig_b, cur_r, cur_b, side) = refs[slots:]
+     red_a, red_b, black_a, black_b, sig_r, sig_b, cur_r, cur_b, side) = refs[2 * slots :]
     g = pl.program_id(0)
-    ext = rows + 2 * EDGE
     blocks = rows // 16
     even8 = checker(8)
     even16 = checker(16)
@@ -171,27 +172,31 @@
         for bit in range(bits):
             needs.append(needs[-1] | {(q - (1 << bit)) % panels for q in needs[-1]})
 
-        def rotor_rows(b, _):
-            at = pl.ds(pl.multiple_of(16 * b, 16), 16)
-            turn = skew[at, :]
+        def place(sources, at, turn, spots):
             cur = {}
             for q in sorted(needs[bits]):
-                source = rotor[slots - 1 - q // tiles]
                 c = q % tiles
-                cur[q] = f32(source[at, c * LANES : (c + 1) * LANES])
+                cur[q] = f32(sources[slots - 1 - q // tiles][at, c * LANES : (c + 1) * LANES])
             for bit in reversed(range(bits)):
                 on = ((turn >> bit) & 1) == 1
                 cur = {q: jnp.where(on, cur[(q - (1 << bit)) % panels], cur[q]) for q in sorted(needs[bit])}
             placed = [cur[want[p + 1]] for p in range(tiles)]
             placed.append(jnp.where(lane16 < LANES // 2, cur[want[tiles + 1]], cur[want[0]]))
-            zero = jnp.zeros((16, LANES), jnp.float32)
+            zero = jnp.zeros((8, LANES), jnp.float32)
             for buf in (red_a, red_b, black_a, black_b):
                 for c in range(tiles + 1):
-                    buf[0, c, at, :] = placed[c]
-                    buf[pairs + 1, c, at, :] = zero
+                    for half, to in enumerate(spots):
+                        buf[0, c, to, :] = placed[c][8 * half : 8 * half + 8]
+                        buf[pairs + 1, c, to, :] = zero
+
+        def rotor_rows(b, _):
+            at = pl.ds(pl.multiple_of(16 * b, 16), 16)
+            spots = [pl.ds(pl.multiple_of(16 * b + EDGE + 8 * half, 8), 8) for half in (0, 1)]
+            place(rotor, at, skew[at, :], spots)
             return 0
 
-        lax.fori_loop(0, ext // 16, rotor_rows, 0)
+        lax.fori_loop(0, blocks, rotor_rows, 0)
+        place(rotor_edge, slice(0, 16), skew_edge[...].astype(jnp.int32), [pl.ds(0, 8), pl.ds(EDGE + rows, 8)])
 
         left_slot = (lane & 7) < 4
 
@@ -258,13 +263,11 @@
                     else:
                         dst[plane, tiles, pl.ds(EDGE + rows, 8), :] = pltpu.roll(side[colour, item, blocks + 1], turn, 1)
 
-    def half_step(m, colour, own, other, sig, cur, start, count, write):
-        def body(r, _):
-            at = start + 8 * r
+    def half_step(m, colour, own, other, sig, cur, start, stride, outputs, write):
+        def row_tile(at):
             centre = [other[m + 1, c, pl.ds(at, 8), :] for c in range(tiles + 1)]
             ahead = [pltpu.roll(x, 1, 1) for x in centre]
             back = [pltpu.roll(x, LANES - 1, 1) for x in centre]
-            outputs = tiles if write is not None and count * 8 == rows else tiles + 1
             for c in range(outputs):
                 left = jnp.where(lane_first, ahead[c - 1], ahead[c])
                 right = jnp.where(lane_last, back[(c + 1) % (tiles + 1)], back[c])
@@ -275,39 +278,45 @@
                 far = own[m + 1, c, pl.ds(at + 2, 8), :] - own[m + 1, c, pl.ds(at - 2, 8), :]
                 total = (left + right) + (centre[c] + outer)
                 new = cur[m, c, pl.ds(at, 8), :] + 0.25 * total - sig[m, c, pl.ds(at, 8), :] * (8.0 * near - far)
-                write(m, c, at, r, new)
+                write(m, c, at, new)
+
+        def body(r, _):
+            for k in range(UNROLL):
+                row_tile(start + stride * r + 8 * k)
             return 0
 
-        lax.fori_loop(0, count, body, 0)
+        lax.fori_loop(0, SPANS, body, 0)
 
     def keep(buf):
-        def write(m, c, at, r, new):
+        def write(m, c, at, new):
             buf[m + 1, c, pl.ds(at, 8), :] = new
 
         return write
 
-    def emit(m, c, at, r, new):
+    def emit(m, c, at, new):
         red = red_a[m + 1, c, pl.ds(at, 8), :]
         cols = slice(c * LANES, (c + 1) * LANES)
-        to = pl.ds(pl.multiple_of(8 * r, 8), 8)
+        to = pl.ds(pl.multiple_of(at - EDGE, 8), 8)
         out_ref[0, to, cols] = jnp.where(even8, red, new)
         out_ref[1, to, cols] = jnp.where(even8, new, red)
 
-    wide = (EDGE - 4, rows // 8 + 1)
+    window = 8 * UNROLL
+    wide = (EDGE - 4, (rows + 8 - window) // (SPANS - 1), tiles + 1)
+    last = (EDGE, (rows - window) // (SPANS - 1), tiles)
     plan = (
         (1, 0, red_a, black_a, sig_r, cur_r, wide, keep(red_b)),
         (2, 1, black_a, red_b, sig_b, cur_b, wide, keep(black_b)),
         (3, 0, red_b, black_b, sig_r, cur_r, wide, keep(red_a)),
-        (4, 1, black_b, red_a, sig_b, cur_b, (EDGE, rows // 8), emit),
+        (4, 1, black_b, red_a, sig_b, cur_b, last, emit),
     )
-    for lag, colour, own, other, sig, cur, (start, count), write in plan:
+    for lag, colour, own, other, sig, cur, where, write in plan:
 
         @pl.when((g >= lag) & (g < pairs + lag))
-        def phase(lag=lag, colour=colour, own=own, other=other, sig=sig, cur=cur, start=start, count=count, write=write):
-            half_step(g - lag, colour, own, other, sig, cur, start, count, write)
-
-
-def relax(rotor, skew, from_left, from_right, corner_prev, corner_next, from_prev, from_next, field, sigma, current):
+        def phase(lag=lag, colour=colour, own=own, other=other, sig=sig, cur=cur, where=where, write=write):
+            half_step(g - lag, colour, own, other, sig, cur, *where, write)
+
+
+def relax(rotor, rotor_edge, skew, skew_edge, from_left, from_right, corner_prev, corner_next, from_prev, from_next, field, sigma, current):
     layers, rows, cols = field.shape
     pairs, tiles, slots = layers // 2, cols // LANES, len(rotor)
     ext = rows + 2 * EDGE
@@ -321,7 +330,7 @@
 
     halo = pl.BlockSpec((2, 1, 16, cols), lambda g: (0, coming(g), 0, 0))
     block = pl.BlockSpec((2, rows, cols), lambda g: (coming(g), 0, 0))
-    fixed = list(rotor) + [skew, from_left, from_right, corner_prev, corner_next]
+    fixed = list(rotor) + list(rotor_edge) + [skew, skew_edge, from_left, from_right, corner_prev, corner_next]
     state = pltpu.VMEM((pairs + 2, tiles + 1, ext, LANES), jnp.float32)
     coef = pltpu.VMEM((pairs, tiles + 1, ext, LANES), jnp.float32)
     return pl.pallas_call(
@@ -342,14 +351,17 @@
 
 
 def local(field, sigma, current, rotor_cycle, skew_list):
-    rows = field.shape[1]
-    rotor = jnp.concatenate(
-        [moved(rotor_cycle[rows - EDGE :], "ta", 1), rotor_cycle, moved(rotor_cycle[:EDGE], "ta", -1)], 0
-    )
-    skew = jnp.concatenate(
-        [moved(skew_list[rows - EDGE :], "ta", 1), skew_list, moved(skew_list[:EDGE], "ta", -1)], 0
-    )
-    skew = jnp.broadcast_to(skew[:, None], (rows + 2 * EDGE, LANES))
+    rows, cols = field.shape[1:]
+    shifts = range(1, lax.axis_size("az"))
+    skew = jnp.broadcast_to(skew_list[:, None], (rows, LANES))
+    slab = [
+        jnp.concatenate([rotor_cycle[part], skew[part].astype(jnp.bfloat16)], 1)
+        for part in (slice(rows - EDGE, rows), slice(0, EDGE))
+    ]
+    slab = jnp.concatenate([moved(slab[0], "ta", 1), moved(slab[1], "ta", -1)], 0)
+    rotor = [rotor_cycle] + [moved(rotor_cycle, "az", s) for s in shifts]
+    rotor_edge, skew_edge = slab[:, :cols], slab[:, cols:]
+    rotor_edge = [rotor_edge] + [moved(rotor_edge, "az", s) for s in shifts]
     to_prev, to_next, to_left, to_right = pack_edges(field, sigma, current)
     from_left = moved(to_right, "az", 1)
     from_right = moved(to_left, "az", -1)
@@ -357,9 +369,8 @@
     from_next = moved(to_prev, "ta", -1)
     corner_prev = moved(jnp.stack([from_left[-1], from_right[-1]]), "ta", 1)
     corner_next = moved(jnp.stack([from_left[0], from_right[0]]), "ta", -1)
-    slots = [rotor] + [moved(rotor, "az", s) for s in range(1, lax.axis_size("az"))]
     return relax(
-        slots, skew, from_left, from_right, corner_prev, corner_next, from_prev, from_next, field, sigma, current
+        rotor, rotor_edge, skew, skew_edge, from_left, from_right, corner_prev, corner_next, from_prev, from_next, field, sigma, current
     )
 
 

time: 109 us -> 74.7 us (0.69)
  Pallas kernels: 67.1 us -> 36.7 us
  waiting for transfers between devices: 21.5 us -> 11.6 us
  starting transfers between devices: 17 us -> 22.6 us
    pallas_call x1, Pallas kernels: 60.8 us -> 30.4 us  [relax(): pl.pallas_call(functools.partial(relax_kernel, slots=slots, pairs=pairs,...]
    ppermute x13 -> x14, waiting for transfers between devices: 21.5 us -> 11.6 us  [moved(): lax.ppermute(value, axis, [(i, (i + steps) % count) for i in range(count)])]
    ppermute x13 -> x14, starting transfers between devices: 17 us -> 22.6 us  [moved(): lax.ppermute(value, axis, [(i, (i + steps) % count) for i in range(count)])]
  transfers between devices with their start and end apart: 13 -> 14, of which waited for: 5 -> 4; matrix products, arithmetic and copies ran while one was open for 1% -> 1% of each run, Pallas kernels for 6% -> 8%
where the time goes in v1:
time: 74.7 us; the launch traced here: 74.4 us
  Pallas kernels  36.7 us (49%)
  starting transfers between devices  22.6 us (30%)
  waiting for transfers between devices  11.6 us (16%)
  local copies, waits for them, and re-layouts  2.66 us (4%)
    pallas_call x1, Pallas kernels, relax(): pl.pallas_call(functools.partial(relax_kernel, slots=slots, pairs=pairs,...  30.4 us
    ppermute x14, starting transfers between devices, moved(): lax.ppermute(value, axis, [(i, (i + steps) % count) for i in range(count)])  22.6 us
    ppermute x14, waiting for transfers between devices, moved(): lax.ppermute(value, axis, [(i, (i + steps) % count) for i in range(count)])  11.6 us
    pallas_call x1, Pallas kernels, pack_edges(): pl.pallas_call(functools.partial(edges_kernel, pairs=pairs, tiles=tiles,...  6.23 us
  transfers between devices with their start and end apart: 14, of which 4 were waited for; matrix products, arithmetic and copies ran while one was open for 1% of the time, Pallas kernels for 8%

profile of v1, /device:TPU:0, one launch (start us, length us, event | category | flops | bytes accessed | tf_op | source)
XLA Modules:
  0.0 74.4 jit_solution(4807142877788770032)
XLA Ops:
  0.0 0.7 convert.4
  0.7 0.1 fusion.3
  0.7 0.7 fusion
  1.5 0.1 broadcast_in_dim.10
  1.6 0.5 collective-permute-start.3
  2.0 0.1 broadcast_in_dim.11
  2.1 4.1 %collective-permute-start.4 = (bf16[8,1152]{1,0:T(8,128)(2,1)S(1)}, bf16[8,1152]{1,0:T(8,128)(2,1)S(1)}, u32[]{:S(2)}, u32[]{:S(2)}) collective-permute-start(bf16[8,1152]{1,0:T(8,128)(2,1)S(1)} %pad_maximum_fusion.1), channel_id=1, source_target_pairs={{0,7},{1,0},{2,1},{3,2},{4,3},{5,4},{6,5},{7,6},{8,15},{9,8},{10,9... | collective-permute-start | bytes 55304 | tf_op jit(solution)/shard_map/ppermute | solution.py:350
  6.2 6.2 %edges.1 = (bf16[2,8,16,1024]{3,2,1,0:T(8,128)(2,1)}, bf16[2,8,16,1024]{3,2,1,0:T(8,128)(2,1)}, bf16[8,2,16,128]{3,2,1,0:T(8,128)(2,1)}, bf16[8,2,16,128]{3,2,1,0:T(8,128)(2,1)}) custom-call(f32[16,128,1024]{2,1,0:T(8,128)} %refs_16_.1, f32[16,128,1024]{2,1,0:T(8,128)} %refs_16_.1, bf16[16,128,1024]{2,1,0:T(8,128)(2,1)} %refs_17_.1, ...), custom_call_target="tpu_custom_call" | custom-call | tf_op jit(solution)/shard_map/edges/pallas_call | solution.py:137
  12.4 2.0 %collective-permute-start.8 = (bf16[8,2,16,128]{3,2,1,0:T(8,128)(2,1)}, bf16[8,2,16,128]{3,2,1,0:T(8,128)(2,1)S(1)}, u32[]{:S(2)}, u32[]{:S(2)}) collective-permute-start(bf16[8,2,16,128]{3,2,1,0:T(8,128)(2,1)} %get-tuple-element.9), channel_id=1, source_target_pairs={{0,8},{8,16},{16,24},{24,0},{1,9},{9,17},{17,25},{25,1},{2,10},{10... | collective-permute-start | bytes 196616 | tf_op jit(solution)/shard_map/ppermute | solution.py:350
  14.4 1.0 %collective-permute-start.9 = (bf16[8,2,16,128]{3,2,1,0:T(8,128)(2,1)}, bf16[8,2,16,128]{3,2,1,0:T(8,128)(2,1)S(1)}, u32[]{:S(2)}, u32[]{:S(2)}) collective-permute-start(bf16[8,2,16,128]{3,2,1,0:T(8,128)(2,1)} %get-tuple-element.10), channel_id=1, source_target_pairs={{0,24},{8,0},{16,8},{24,16},{1,25},{9,1},{17,9},{25,17},{2,26},{10... | collective-permute-start | bytes 196616 | tf_op jit(solution)/shard_map/ppermute | solution.py:350
  15.4 0.0 collective-permute-start.12
  15.4 0.0 collective-permute-done.3
  15.4 3.5 %collective-permute-start.13 = (bf16[2,8,16,1024]{3,2,1,0:T(8,128)(2,1)}, bf16[2,8,16,1024]{3,2,1,0:T(8,128)(2,1)S(1)}, u32[]{:S(2)}, u32[]{:S(2)}) collective-permute-start(bf16[2,8,16,1024]{3,2,1,0:T(8,128)(2,1)} %get-tuple-element.12), channel_id=1, source_target_pairs={{0,7},{1,0},{2,1},{3,2},{4,3},{5,4},{6,5},{7,6},{8,15},{9,8},{10,9... | collective-permute-start | bytes 1572872 | tf_op jit(solution)/shard_map/ppermute | solution.py:350
  18.9 0.0 collective-permute-done.4
  19.0 0.0 copy-start.6
  19.0 2.0 %collective-permute-start.7 = (bf16[16,1024]{1,0:T(8,128)(2,1)S(1)}, bf16[16,1024]{1,0:T(8,128)(2,1)S(1)}, u32[]{:S(2)}, u32[]{:S(2)}) collective-permute-start(bf16[16,1024]{1,0:T(8,128)(2,1)S(1)} %slice.45.refs_4_), channel_id=1, source_target_pairs={{0,24},{8,0},{16,8},{24,16},{1,25},{9,1},{17,9},{25,17},{2,26},{10... | collective-permute-start | bytes 98312 | tf_op jit(solution)/shard_map/ppermute | solution.py:350
  21.0 0.0 collective-permute-done.8.refs_10_
  21.0 0.5 collective-permute-start.6
  21.5 0.0 collective-permute-done.9.refs_11_
  21.5 1.5 %collective-permute-start.5 = (bf16[16,1024]{1,0:T(8,128)(2,1)S(1)}, bf16[16,1024]{1,0:T(8,128)(2,1)S(1)}, u32[]{:S(2)}, u32[]{:S(2)}) collective-permute-start(bf16[16,1024]{1,0:T(8,128)(2,1)S(1)} %slice.45.refs_4_), channel_id=1, source_target_pairs={{0,8},{8,16},{16,24},{24,0},{1,9},{9,17},{17,25},{25,1},{2,10},{10... | collective-permute-start | bytes 98312 | tf_op jit(solution)/shard_map/ppermute | solution.py:350
  23.1 0.0 collective-permute-done.7.refs_7_
  23.1 0.1 collective-permute-start.10
  23.2 1.8 %collective-permute-done.6.refs_6_ = bf16[16,1024]{1,0:T(8,128)(2,1)S(1)} collective-permute-done((bf16[16,1024]{1,0:T(8,128)(2,1)S(1)}, bf16[16,1024]{1,0:T(8,128)(2,1)S(1)}, u32[]{:S(2)}, u32[]{:S(2)}) %collective-permute-start.6) | collective-permute-done | bytes 32800 | tf_op jit(solution)/shard_map/ppermute | solution.py:350
  24.9 1.8 %collective-permute-start.11 = (bf16[2,2,16,128]{3,2,1,0:T(8,128)(2,1)S(1)}, bf16[2,2,16,128]{3,2,1,0:T(8,128)(2,1)S(1)}, u32[]{:S(2)}, u32[]{:S(2)}) collective-permute-start(bf16[2,2,16,128]{3,2,1,0:T(8,128)(2,1)S(1)} %pad_maximum_fusion.3), channel_id=1, source_target_pairs={{0,7},{1,0},{2,1},{3,2},{4,3},{5,4},{6,5},{7,6},{8,15},{9,8},{10,9... | collective-permute-start | bytes 49160 | tf_op jit(solution)/shard_map/ppermute | solution.py:350
  26.7 0.0 collective-permute-done.5.refs_5_
  26.7 2.7 %collective-permute-start.2 = (bf16[128,1024]{1,0:T(8,128)(2,1)S(1)}, bf16[128,1024]{1,0:T(8,128)(2,1)S(1)}, u32[]{:S(2)}, u32[]{:S(2)}) collective-permute-start(bf16[128,1024]{1,0:T(8,128)(2,1)S(1)} %copy-done.2), channel_id=1, source_target_pairs={{0,24},{8,0},{16,8},{24,16},{1,25},{9,1},{17,9},{25,17},{2,26},{10... | collective-permute-start | bytes 786440 | tf_op jit(solution)/shard_map/ppermute | solution.py:350
  29.4 1.9 %collective-permute-done.10.refs_12_ = bf16[2,2,16,128]{3,2,1,0:T(8,128)(2,1)S(1)} collective-permute-done((bf16[2,2,16,128]{3,2,1,0:T(8,128)(2,1)S(1)}, bf16[2,2,16,128]{3,2,1,0:T(8,128)(2,1)S(1)}, u32[]{:S(2)}, u32[]{:S(2)}) %collective-permute-start.10) | collective-permute-done | bytes 16416 | tf_op jit(solution)/shard_map/ppermute | solution.py:350
  31.3 2.3 %collective-permute-start.1 = (bf16[128,1024]{1,0:T(8,128)(2,1)S(1)}, bf16[128,1024]{1,0:T(8,128)(2,1)S(1)}, u32[]{:S(2)}, u32[]{:S(2)}) collective-permute-start(bf16[128,1024]{1,0:T(8,128)(2,1)S(1)} %copy-done.2), channel_id=1, source_target_pairs={{0,16},{8,24},{16,0},{24,8},{1,17},{9,25},{17,1},{25,9},{2,18},{10... | collective-permute-start | bytes 786440 | tf_op jit(solution)/shard_map/ppermute | solution.py:350
  33.6 0.0 collective-permute-done.11.refs_13_
  33.6 0.6 collective-permute-start
  34.2 0.6 slice.46.refs_9_
  34.8 1.2 %collective-permute-done.2.refs_3_ = bf16[128,1024]{1,0:T(8,128)(2,1)S(1)} collective-permute-done((bf16[128,1024]{1,0:T(8,128)(2,1)S(1)}, bf16[128,1024]{1,0:T(8,128)(2,1)S(1)}, u32[]{:S(2)}, u32[]{:S(2)}) %collective-permute-start.2) | collective-permute-done | bytes 262176 | tf_op jit(solution)/shard_map/ppermute | solution.py:350
  36.0 6.7 %collective-permute-done.1.refs_2_ = bf16[128,1024]{1,0:T(8,128)(2,1)S(1)} collective-permute-done((bf16[128,1024]{1,0:T(8,128)(2,1)S(1)}, bf16[128,1024]{1,0:T(8,128)(2,1)S(1)}, u32[]{:S(2)}, u32[]{:S(2)}) %collective-permute-start.1) | collective-permute-done | bytes 262176 | tf_op jit(solution)/shard_map/ppermute | solution.py:350
  42.7 0.0 collective-permute-done.refs_1_
  42.7 0.0 collective-permute-done.12.refs_14_
  42.8 0.0 collective-permute-done.13.refs_15_
  42.8 0.9 %broadcast_in_dim.12.refs_8_ = s32[128,128]{1,0:T(8,128)} broadcast(s32[128]{0:T(128)S(1)} %copy-done.14), dimensions={0} | broadcast | bytes 66048 | tf_op jit(solution)/shard_map/broadcast_in_dim | solution.py:356
  43.6 0.0 copy-done.6
  43.7 0.0 copy-done.10
  43.7 0.0 copy-done.11
  43.7 0.0 copy-done.12
  43.7 0.0 copy-done.13
  43.7 0.0 copy-done.3
  43.7 0.0 copy-done.4
  43.7 0.0 copy-done.5
  43.7 0.0 copy-done
  43.7 0.2 copy-done.1
  43.9 30.4 %relax.1 = f32[16,128,1024]{2,1,0:T(8,128)} custom-call(bf16[128,1024]{1,0:T(8,128)(2,1)} %refs_0_.1, bf16[128,1024]{1,0:T(8,128)(2,1)} %copy-done.5, bf16[128,1024]{1,0:T(8,128)(2,1)} %copy-done.4, bf16[128,1024]{1,0:T(8,128)(2,1)} %copy-done.3, bf16[16,1024]{1,0:T(8,128)(2,1)} %copy-done.6, bf16[16,1024]{1,0:T(8,128)(2,1)} %copy-done.11, ...), custom_call_target="tpu_custom_call" | custom-call | tf_op jit(solution)/shard_map/relax/pallas_call | solution.py:336
  (28 shorter events, 0.1 us)
Async XLA Ops:
  1.6 13.8 %collective-permute-start.3 = (bf16[8,1152]{1,0:T(8,128)(2,1)S(1)}, bf16[8,1152]{1,0:T(8,128)(2,1)S(1)}, u32[]{:S(2)}, u32[]{:S(2)}) collective-permute-start(bf16[8,1152]{1,0:T(8,128)(2,1)S(1)} %pad_maximum_fusion), channel_id=1, source_target_pairs={{0,1},{1,2},{2,3},{3,4},{4,5},{5,6},{6,7},{7,0},{8,9},{9,10},{10,1... | collective-permute-start | bytes 55304 | tf_op jit(solution)/shard_map/ppermute | solution.py:350
  2.1 24.6 %copy-start.2 = (bf16[128,1024]{1,0:T(8,128)(2,1)S(1)}, bf16[128,1024]{1,0:T(8,128)(2,1)}, u32[]{:S(2)}) copy-start(bf16[128,1024]{1,0:T(8,128)(2,1)} %refs_0_.1) | copy-start | bytes 786436
  2.1 40.7 %copy-start.14 = (s32[128]{0:T(128)S(1)}, s32[128]{0:T(128)}, u32[]{:S(2)}) copy-start(s32[128]{0:T(128)} %param.9) | copy-start | bytes 1540
  2.1 16.9 %collective-permute-start.4 = (bf16[8,1152]{1,0:T(8,128)(2,1)S(1)}, bf16[8,1152]{1,0:T(8,128)(2,1)S(1)}, u32[]{:S(2)}, u32[]{:S(2)}) collective-permute-start(bf16[8,1152]{1,0:T(8,128)(2,1)S(1)} %pad_maximum_fusion.1), channel_id=1, source_target_pairs={{0,7},{1,0},{2,1},{3,2},{4,3},{5,4},{6,5},{7,6},{8,15},{9,8},{10,9... | collective-permute-start | bytes 55304 | tf_op jit(solution)/shard_map/ppermute | solution.py:350
  12.4 8.6 %collective-permute-start.8 = (bf16[8,2,16,128]{3,2,1,0:T(8,128)(2,1)}, bf16[8,2,16,128]{3,2,1,0:T(8,128)(2,1)S(1)}, u32[]{:S(2)}, u32[]{:S(2)}) collective-permute-start(bf16[8,2,16,128]{3,2,1,0:T(8,128)(2,1)} %get-tuple-element.9), channel_id=1, source_target_pairs={{0,8},{8,16},{16,24},{24,0},{1,9},{9,17},{17,25},{25,1},{2,10},{10... | collective-permute-start | bytes 196616 | tf_op jit(solution)/shard_map/ppermute | solution.py:350
  14.4 7.1 %collective-permute-start.9 = (bf16[8,2,16,128]{3,2,1,0:T(8,128)(2,1)}, bf16[8,2,16,128]{3,2,1,0:T(8,128)(2,1)S(1)}, u32[]{:S(2)}, u32[]{:S(2)}) collective-permute-start(bf16[8,2,16,128]{3,2,1,0:T(8,128)(2,1)} %get-tuple-element.10), channel_id=1, source_target_pairs={{0,24},{8,0},{16,8},{24,16},{1,25},{9,1},{17,9},{25,17},{2,26},{10... | collective-permute-start | bytes 196616 | tf_op jit(solution)/shard_map/ppermute | solution.py:350
  15.4 27.4 %collective-permute-start.12 = (bf16[2,8,16,1024]{3,2,1,0:T(8,128)(2,1)}, bf16[2,8,16,1024]{3,2,1,0:T(8,128)(2,1)S(1)}, u32[]{:S(2)}, u32[]{:S(2)}) collective-permute-start(bf16[2,8,16,1024]{3,2,1,0:T(8,128)(2,1)} %get-tuple-element.11), channel_id=1, source_target_pairs={{0,1},{1,2},{2,3},{3,4},{4,5},{5,6},{6,7},{7,0},{8,9},{9,10},{10,1... | collective-permute-start | bytes 1572872 | tf_op jit(solution)/shard_map/ppermute | solution.py:350
  15.4 27.4 %collective-permute-start.13 = (bf16[2,8,16,1024]{3,2,1,0:T(8,128)(2,1)}, bf16[2,8,16,1024]{3,2,1,0:T(8,128)(2,1)S(1)}, u32[]{:S(2)}, u32[]{:S(2)}) collective-permute-start(bf16[2,8,16,1024]{3,2,1,0:T(8,128)(2,1)} %get-tuple-element.12), channel_id=1, source_target_pairs={{0,7},{1,0},{2,1},{3,2},{4,3},{5,4},{6,5},{7,6},{8,15},{9,8},{10,9... | collective-permute-start | bytes 1572872 | tf_op jit(solution)/shard_map/ppermute | solution.py:350
  19.0 24.7 %copy-start.6 = (bf16[16,1024]{1,0:T(8,128)(2,1)}, bf16[16,1024]{1,0:T(8,128)(2,1)S(1)}, u32[]{:S(2)}) copy-start(bf16[16,1024]{1,0:T(8,128)(2,1)S(1)} %slice.45.refs_4_) | copy-start | bytes 98308
  19.0 4.1 %collective-permute-start.7 = (bf16[16,1024]{1,0:T(8,128)(2,1)S(1)}, bf16[16,1024]{1,0:T(8,128)(2,1)S(1)}, u32[]{:S(2)}, u32[]{:S(2)}) collective-permute-start(bf16[16,1024]{1,0:T(8,128)(2,1)S(1)} %slice.45.refs_4_), channel_id=1, source_target_pairs={{0,24},{8,0},{16,8},{24,16},{1,25},{9,1},{17,9},{25,17},{2,26},{10... | collective-permute-start | bytes 98312 | tf_op jit(solution)/shard_map/ppermute | solution.py:350
  21.0 22.6 %copy-start.7 = (bf16[8,2,16,128]{3,2,1,0:T(8,128)(2,1)}, bf16[8,2,16,128]{3,2,1,0:T(8,128)(2,1)S(1)}, u32[]{:S(2)}) copy-start(bf16[8,2,16,128]{3,2,1,0:T(8,128)(2,1)S(1)} %collective-permute-done.8.refs_10_) | copy-start | bytes 196612
  21.0 3.9 %collective-permute-start.6 = (bf16[16,1024]{1,0:T(8,128)(2,1)S(1)}, bf16[16,1024]{1,0:T(8,128)(2,1)S(1)}, u32[]{:S(2)}, u32[]{:S(2)}) collective-permute-start(bf16[16,1024]{1,0:T(8,128)(2,1)S(1)} %slice.45.refs_4_), channel_id=1, source_target_pairs={{0,16},{8,24},{16,0},{24,8},{1,17},{9,25},{17,1},{25,9},{2,18},{10... | collective-permute-start | bytes 98312 | tf_op jit(solution)/shard_map/ppermute | solution.py:350
  21.5 22.1 %copy-start.8 = (bf16[8,2,16,128]{3,2,1,0:T(8,128)(2,1)}, bf16[8,2,16,128]{3,2,1,0:T(8,128)(2,1)S(1)}, u32[]{:S(2)}) copy-start(bf16[8,2,16,128]{3,2,1,0:T(8,128)(2,1)S(1)} %collective-permute-done.9.refs_11_) | copy-start | bytes 196612
  21.5 5.2 %collective-permute-start.5 = (bf16[16,1024]{1,0:T(8,128)(2,1)S(1)}, bf16[16,1024]{1,0:T(8,128)(2,1)S(1)}, u32[]{:S(2)}, u32[]{:S(2)}) collective-permute-start(bf16[16,1024]{1,0:T(8,128)(2,1)S(1)} %slice.45.refs_4_), channel_id=1, source_target_pairs={{0,8},{8,16},{16,24},{24,0},{1,9},{9,17},{17,25},{25,1},{2,10},{10... | collective-permute-start | bytes 98312 | tf_op jit(solution)/shard_map/ppermute | solution.py:350
  23.1 20.6 %copy-start.9 = (bf16[16,1024]{1,0:T(8,128)(2,1)}, bf16[16,1024]{1,0:T(8,128)(2,1)S(1)}, u32[]{:S(2)}) copy-start(bf16[16,1024]{1,0:T(8,128)(2,1)S(1)} %collective-permute-done.7.refs_7_) | copy-start | bytes 98308
  23.1 8.2 %collective-permute-start.10 = (bf16[2,2,16,128]{3,2,1,0:T(8,128)(2,1)S(1)}, bf16[2,2,16,128]{3,2,1,0:T(8,128)(2,1)S(1)}, u32[]{:S(2)}, u32[]{:S(2)}) collective-permute-start(bf16[2,2,16,128]{3,2,1,0:T(8,128)(2,1)S(1)} %pad_maximum_fusion.2), channel_id=1, source_target_pairs={{0,1},{1,2},{2,3},{3,4},{4,5},{5,6},{6,7},{7,0},{8,9},{9,10},{10,1... | collective-permute-start | bytes 49160 | tf_op jit(solution)/shard_map/ppermute | solution.py:350
  24.9 18.7 %copy-start.10 = (bf16[16,1024]{1,0:T(8,128)(2,1)}, bf16[16,1024]{1,0:T(8,128)(2,1)S(1)}, u32[]{:S(2)}) copy-start(bf16[16,1024]{1,0:T(8,128)(2,1)S(1)} %collective-permute-done.6.refs_6_) | copy-start | bytes 98308
  24.9 8.7 %collective-permute-start.11 = (bf16[2,2,16,128]{3,2,1,0:T(8,128)(2,1)S(1)}, bf16[2,2,16,128]{3,2,1,0:T(8,128)(2,1)S(1)}, u32[]{:S(2)}, u32[]{:S(2)}) collective-permute-start(bf16[2,2,16,128]{3,2,1,0:T(8,128)(2,1)S(1)} %pad_maximum_fusion.3), channel_id=1, source_target_pairs={{0,7},{1,0},{2,1},{3,2},{4,3},{5,4},{6,5},{7,6},{8,15},{9,8},{10,9... | collective-permute-start | bytes 49160 | tf_op jit(solution)/shard_map/ppermute | solution.py:350
  26.7 17.0 %copy-start.11 = (bf16[16,1024]{1,0:T(8,128)(2,1)}, bf16[16,1024]{1,0:T(8,128)(2,1)S(1)}, u32[]{:S(2)}) copy-start(bf16[16,1024]{1,0:T(8,128)(2,1)S(1)} %collective-permute-done.5.refs_5_) | copy-start | bytes 98308
  26.7 9.3 %collective-permute-start.2 = (bf16[128,1024]{1,0:T(8,128)(2,1)S(1)}, bf16[128,1024]{1,0:T(8,128)(2,1)S(1)}, u32[]{:S(2)}, u32[]{:S(2)}) collective-permute-start(bf16[128,1024]{1,0:T(8,128)(2,1)S(1)} %copy-done.2), channel_id=1, source_target_pairs={{0,24},{8,0},{16,8},{24,16},{1,25},{9,1},{17,9},{25,17},{2,26},{10... | collective-permute-start | bytes 786440 | tf_op jit(solution)/shard_map/ppermute | solution.py:350
  31.3 12.4 %copy-start.12 = (bf16[2,2,16,128]{3,2,1,0:T(8,128)(2,1)}, bf16[2,2,16,128]{3,2,1,0:T(8,128)(2,1)S(1)}, u32[]{:S(2)}) copy-start(bf16[2,2,16,128]{3,2,1,0:T(8,128)(2,1)S(1)} %collective-permute-done.10.refs_12_) | copy-start | bytes 49156
  31.3 11.4 %collective-permute-start.1 = (bf16[128,1024]{1,0:T(8,128)(2,1)S(1)}, bf16[128,1024]{1,0:T(8,128)(2,1)S(1)}, u32[]{:S(2)}, u32[]{:S(2)}) collective-permute-start(bf16[128,1024]{1,0:T(8,128)(2,1)S(1)} %copy-done.2), channel_id=1, source_target_pairs={{0,16},{8,24},{16,0},{24,8},{1,17},{9,25},{17,1},{25,9},{2,18},{10... | collective-permute-start | bytes 786440 | tf_op jit(solution)/shard_map/ppermute | solution.py:350
  33.6 10.1 %copy-start.13 = (bf16[2,2,16,128]{3,2,1,0:T(8,128)(2,1)}, bf16[2,2,16,128]{3,2,1,0:T(8,128)(2,1)S(1)}, u32[]{:S(2)}) copy-start(bf16[2,2,16,128]{3,2,1,0:T(8,128)(2,1)S(1)} %collective-permute-done.11.refs_13_) | copy-start | bytes 49156
  33.6 9.1 %collective-permute-start = (bf16[128,1024]{1,0:T(8,128)(2,1)S(1)}, bf16[128,1024]{1,0:T(8,128)(2,1)S(1)}, u32[]{:S(2)}, u32[]{:S(2)}) collective-permute-start(bf16[128,1024]{1,0:T(8,128)(2,1)S(1)} %copy-done.2), channel_id=1, source_target_pairs={{0,8},{8,16},{16,24},{24,0},{1,9},{9,17},{17,25},{25,1},{2,10},{10... | collective-permute-start | bytes 786440 | tf_op jit(solution)/shard_map/ppermute | solution.py:350
  36.0 7.7 %copy-start.3 = (bf16[128,1024]{1,0:T(8,128)(2,1)}, bf16[128,1024]{1,0:T(8,128)(2,1)S(1)}, u32[]{:S(2)}) copy-start(bf16[128,1024]{1,0:T(8,128)(2,1)S(1)} %collective-permute-done.2.refs_3_) | copy-start | bytes 786436
  42.7 1.0 %copy-start.4 = (bf16[128,1024]{1,0:T(8,128)(2,1)}, bf16[128,1024]{1,0:T(8,128)(2,1)S(1)}, u32[]{:S(2)}) copy-start(bf16[128,1024]{1,0:T(8,128)(2,1)S(1)} %collective-permute-done.1.refs_2_) | copy-start | bytes 786436
  42.7 1.0 %copy-start.5 = (bf16[128,1024]{1,0:T(8,128)(2,1)}, bf16[128,1024]{1,0:T(8,128)(2,1)S(1)}, u32[]{:S(2)}) copy-start(bf16[128,1024]{1,0:T(8,128)(2,1)S(1)} %collective-permute-done.refs_1_) | copy-start | bytes 786436
  42.7 1.0 %copy-start = (bf16[2,8,16,1024]{3,2,1,0:T(8,128)(2,1)}, bf16[2,8,16,1024]{3,2,1,0:T(8,128)(2,1)S(1)}, u32[]{:S(2)}) copy-start(bf16[2,8,16,1024]{3,2,1,0:T(8,128)(2,1)S(1)} %collective-permute-done.12.refs_14_) | copy-start | bytes 1572868
  42.8 1.1 %copy-start.1 = (bf16[2,8,16,1024]{3,2,1,0:T(8,128)(2,1)}, bf16[2,8,16,1024]{3,2,1,0:T(8,128)(2,1)S(1)}, u32[]{:S(2)}) copy-start(bf16[2,8,16,1024]{3,2,1,0:T(8,128)(2,1)S(1)} %collective-permute-done.13.refs_15_) | copy-start | bytes 1572868

commit v2 on v1

--- a/solution.py
+++ b/solution.py
@@ -150,10 +150,9 @@
 
 
 def relax_kernel(*refs, slots, pairs, rows, tiles):
-    rotor, rotor_edge = refs[:slots], refs[slots : 2 * slots]
-    (skew, skew_edge, from_left, from_right, corner_prev, corner_next, from_prev, from_next,
+    (rotor, rotor_edge, skew, skew_edge, from_left, from_right, corner_prev, corner_next, from_prev, from_next,
      u_ref, s_ref, j_ref, out_ref,
-     red_a, red_b, black_a, black_b, sig_r, sig_b, cur_r, cur_b, side) = refs[2 * slots :]
+     red_a, red_b, black_a, black_b, sig_r, sig_b, cur_r, cur_b, side) = refs
     g = pl.program_id(0)
     blocks = rows // 16
     even8 = checker(8)
@@ -167,6 +166,8 @@
     def prologue():
         panels = slots * tiles
         bits = (panels - 1).bit_length()
+        here = lax.axis_index("az")
+        device = [lax.rem(here + slots - r, slots) for r in range(slots)]
         want = [(panels - tiles - 1 + p) % panels for p in range(tiles + 2)]
         needs = [set(want)]
         for bit in range(bits):
@@ -176,7 +177,7 @@
             cur = {}
             for q in sorted(needs[bits]):
                 c = q % tiles
-                cur[q] = f32(sources[slots - 1 - q // tiles][at, c * LANES : (c + 1) * LANES])
+                cur[q] = f32(sources[device[slots - 1 - q // tiles], at, c * LANES : (c + 1) * LANES])
             for bit in reversed(range(bits)):
                 on = ((turn >> bit) & 1) == 1
                 cur = {q: jnp.where(on, cur[(q - (1 << bit)) % panels], cur[q]) for q in sorted(needs[bit])}
@@ -318,7 +319,7 @@
 
 def relax(rotor, rotor_edge, skew, skew_edge, from_left, from_right, corner_prev, corner_next, from_prev, from_next, field, sigma, current):
     layers, rows, cols = field.shape
-    pairs, tiles, slots = layers // 2, cols // LANES, len(rotor)
+    pairs, tiles, slots = layers // 2, cols // LANES, rotor.shape[0]
     ext = rows + 2 * EDGE
 
     def whole(array):
@@ -330,7 +331,7 @@
 
     halo = pl.BlockSpec((2, 1, 16, cols), lambda g: (0, coming(g), 0, 0))
     block = pl.BlockSpec((2, rows, cols), lambda g: (coming(g), 0, 0))
-    fixed = list(rotor) + list(rotor_edge) + [skew, skew_edge, from_left, from_right, corner_prev, corner_next]
+    fixed = [rotor, rotor_edge, skew, skew_edge, from_left, from_right, corner_prev, corner_next]
     state = pltpu.VMEM((pairs + 2, tiles + 1, ext, LANES), jnp.float32)
     coef = pltpu.VMEM((pairs, tiles + 1, ext, LANES), jnp.float32)
     return pl.pallas_call(
@@ -352,16 +353,15 @@
 
 def local(field, sigma, current, rotor_cycle, skew_list):
     rows, cols = field.shape[1:]
-    shifts = range(1, lax.axis_size("az"))
     skew = jnp.broadcast_to(skew_list[:, None], (rows, LANES))
     slab = [
         jnp.concatenate([rotor_cycle[part], skew[part].astype(jnp.bfloat16)], 1)
         for part in (slice(rows - EDGE, rows), slice(0, EDGE))
     ]
     slab = jnp.concatenate([moved(slab[0], "ta", 1), moved(slab[1], "ta", -1)], 0)
-    rotor = [rotor_cycle] + [moved(rotor_cycle, "az", s) for s in shifts]
-    rotor_edge, skew_edge = slab[:, :cols], slab[:, cols:]
-    rotor_edge = [rotor_edge] + [moved(rotor_edge, "az", s) for s in shifts]
+    rotor = lax.all_gather(rotor_cycle, "az")
+    rotor_edge = lax.all_gather(slab[:, :cols], "az")
+    skew_edge = slab[:, cols:]
     to_prev, to_next, to_left, to_right = pack_edges(field, sigma, current)
     from_left = moved(to_right, "az", 1)
     from_right = moved(to_left, "az", -1)

time: 74.7 us -> 79.5 us (1.064)
  between operations: 0.16 us -> 13.5 us
  waiting for transfers between devices: 11.6 us -> 1.56 us
  blocking collectives: 0 us -> 9.67 us
  starting transfers between devices: 22.6 us -> 14.6 us
    ppermute x14 -> x8, waiting for transfers between devices: 11.6 us -> 0.83 us  [moved(): lax.ppermute(value, axis, [(i, (i + steps) % count) for i in range(count)])]
    all_gather x0 -> x1, blocking collectives: none -> 9.67 us  [local(): rotor_edge = lax.all_gather(slab[:, :cols], 'az')]
    ppermute x14 -> x8, starting transfers between devices: 22.6 us -> 14.6 us  [moved(): lax.ppermute(value, axis, [(i, (i + steps) % count) for i in range(count)])]
  transfers between devices with their start and end apart: 14 -> 9, of which waited for: 4 -> 1; matrix products, arithmetic and copies ran while one was open for 1% -> 3% of each run, Pallas kernels for 8% -> 8%
where the time goes in v2:
time: 79.5 us; the launch traced here: 79.1 us
  Pallas kernels  36.6 us (46%)
  starting transfers between devices  14.6 us (18%)
  between operations  13.5 us (17%)
  blocking collectives  9.67 us (12%)
  local copies, waits for them, and re-layouts  2.49 us (3%)
  waiting for transfers between devices  1.56 us (2%)
    pallas_call x1, Pallas kernels, relax(): pl.pallas_call(functools.partial(relax_kernel, slots=slots, pairs=pairs,...  30.4 us
    ppermute x8, starting transfers between devices, moved(): lax.ppermute(value, axis, [(i, (i + steps) % count) for i in range(count)])  14.6 us
    all_gather x1, blocking collectives, local(): rotor_edge = lax.all_gather(slab[:, :cols], 'az')  9.67 us
    pallas_call x1, Pallas kernels, pack_edges(): pl.pallas_call(functools.partial(edges_kernel, pairs=pairs, tiles=tiles,...  6.25 us
  transfers between devices with their start and end apart: 9, of which 1 were waited for; matrix products, arithmetic and copies ran while one was open for 3% of the time, Pallas kernels for 8%

profile of v2, /device:TPU:0, one launch (start us, length us, event | category | flops | bytes accessed | tf_op | source)
XLA Modules:
  0.0 79.1 jit_solution(10130736642334824618)
XLA Ops:
  6.5 0.0 all-gather.4.cloned.1.call-start
  6.5 0.7 all-gather.4.cloned.1.call-update
  7.3 0.7 fusion
  8.0 0.7 convert.4
  8.7 0.1 fusion.3
  8.7 0.1 broadcast_in_dim.10
  8.8 0.5 collective-permute-start
  9.3 0.1 broadcast_in_dim.11
  9.3 0.0 copy-start.6
  9.3 4.0 %collective-permute-start.1 = (bf16[8,1152]{1,0:T(8,128)(2,1)S(1)}, bf16[8,1152]{1,0:T(8,128)(2,1)S(1)}, u32[]{:S(2)}, u32[]{:S(2)}) collective-permute-start(bf16[8,1152]{1,0:T(8,128)(2,1)S(1)} %pad_maximum_fusion.1), channel_id=1, source_target_pairs={{0,7},{1,0},{2,1},{3,2},{4,3},{5,4},{6,5},{7,6},{8,15},{9,8},{10,9... | collective-permute-start | bytes 55304 | tf_op jit(solution)/shard_map/ppermute | solution.py:351
  13.4 6.2 %edges.1 = (bf16[2,8,16,1024]{3,2,1,0:T(8,128)(2,1)}, bf16[2,8,16,1024]{3,2,1,0:T(8,128)(2,1)}, bf16[8,2,16,128]{3,2,1,0:T(8,128)(2,1)}, bf16[8,2,16,128]{3,2,1,0:T(8,128)(2,1)}) custom-call(f32[16,128,1024]{2,1,0:T(8,128)} %refs_10_.1, f32[16,128,1024]{2,1,0:T(8,128)} %refs_10_.1, bf16[16,128,1024]{2,1,0:T(8,128)(2,1)} %refs_11_.1, ...), custom_call_target="tpu_custom_call" | custom-call | tf_op jit(solution)/shard_map/edges/pallas_call | solution.py:137
  19.6 2.0 %collective-permute-start.2 = (bf16[8,2,16,128]{3,2,1,0:T(8,128)(2,1)}, bf16[8,2,16,128]{3,2,1,0:T(8,128)(2,1)S(1)}, u32[]{:S(2)}, u32[]{:S(2)}) collective-permute-start(bf16[8,2,16,128]{3,2,1,0:T(8,128)(2,1)} %get-tuple-element.9), channel_id=1, source_target_pairs={{0,8},{8,16},{16,24},{24,0},{1,9},{9,17},{17,25},{25,1},{2,10},{10... | collective-permute-start | bytes 196616 | tf_op jit(solution)/shard_map/ppermute | solution.py:351
  21.6 1.0 %collective-permute-start.3 = (bf16[8,2,16,128]{3,2,1,0:T(8,128)(2,1)}, bf16[8,2,16,128]{3,2,1,0:T(8,128)(2,1)S(1)}, u32[]{:S(2)}, u32[]{:S(2)}) collective-permute-start(bf16[8,2,16,128]{3,2,1,0:T(8,128)(2,1)} %get-tuple-element.10), channel_id=1, source_target_pairs={{0,24},{8,0},{16,8},{24,16},{1,25},{9,1},{17,9},{25,17},{2,26},{10... | collective-permute-start | bytes 196616 | tf_op jit(solution)/shard_map/ppermute | solution.py:351
  22.6 0.0 collective-permute-start.6
  22.6 0.0 collective-permute-done
  22.6 3.5 %collective-permute-start.7 = (bf16[2,8,16,1024]{3,2,1,0:T(8,128)(2,1)}, bf16[2,8,16,1024]{3,2,1,0:T(8,128)(2,1)S(1)}, u32[]{:S(2)}, u32[]{:S(2)}) collective-permute-start(bf16[2,8,16,1024]{3,2,1,0:T(8,128)(2,1)} %get-tuple-element.12), channel_id=1, source_target_pairs={{0,7},{1,0},{2,1},{3,2},{4,3},{5,4},{6,5},{7,6},{8,15},{9,8},{10,9... | collective-permute-start | bytes 1572872 | tf_op jit(solution)/shard_map/ppermute | solution.py:351
  26.2 0.0 collective-permute-done.1
  26.2 0.6 slice.46.refs_3_
  26.8 0.0 collective-permute-done.2.refs_4_
  26.8 0.0 copy-start.2
  26.8 0.8 %collective-permute-done.3.refs_5_ = bf16[8,2,16,128]{3,2,1,0:T(8,128)(2,1)S(1)} collective-permute-done((bf16[8,2,16,128]{3,2,1,0:T(8,128)(2,1)}, bf16[8,2,16,128]{3,2,1,0:T(8,128)(2,1)S(1)}, u32[]{:S(2)}, u32[]{:S(2)}) %collective-permute-start.3) | collective-permute-done | bytes 65568 | tf_op jit(solution)/shard_map/ppermute | solution.py:351
  27.6 0.0 copy-start.3
  27.6 0.1 collective-permute-start.4
  27.7 3.5 %collective-permute-start.5 = (bf16[2,2,16,128]{3,2,1,0:T(8,128)(2,1)S(1)}, bf16[2,2,16,128]{3,2,1,0:T(8,128)(2,1)S(1)}, u32[]{:S(2)}, u32[]{:S(2)}) collective-permute-start(bf16[2,2,16,128]{3,2,1,0:T(8,128)(2,1)S(1)} %pad_maximum_fusion.3), channel_id=1, source_target_pairs={{0,7},{1,0},{2,1},{3,2},{4,3},{5,4},{6,5},{7,6},{8,15},{9,8},{10,9... | collective-permute-start | bytes 49160 | tf_op jit(solution)/shard_map/ppermute | solution.py:351
  31.2 9.7 %all-gather.1 = bf16[64,1024]{1,0:T(8,128)(2,1)} all-gather(bf16[16,1024]{1,0:T(8,128)(2,1)S(1)} %slice.45), channel_id=3, replica_groups=mesh['az'=4,'ta'=8] {'az'}, dimensions={0}, use_global_device_ids=true | all-gather | bytes 163840 | tf_op jit(solution)/shard_map/all_gather | solution.py:363
  40.9 0.0 collective-permute-done.4.refs_6_
  40.9 0.0 copy-start.4
  40.9 0.0 collective-permute-done.5.refs_7_
  40.9 0.0 copy-start.5
  40.9 0.0 collective-permute-done.6.refs_8_
  40.9 0.0 copy-start
  40.9 0.0 collective-permute-done.7.refs_9_
  41.0 0.0 copy-start.1
  41.0 0.0 all-gather.4.cloned.1.call-done
  41.0 0.0 copy-done.6
  41.0 0.9 %broadcast_in_dim.12.refs_2_ = s32[128,128]{1,0:T(8,128)} broadcast(s32[128]{0:T(128)S(1)} %copy-done.6), dimensions={0} | broadcast | bytes 66048 | tf_op jit(solution)/shard_map/broadcast_in_dim | solution.py:356
  41.9 0.0 copy-done.2
  41.9 0.0 copy-done.3
  41.9 0.0 copy-done.4
  41.9 0.0 copy-done.5
  41.9 0.0 copy-done
  41.9 0.0 copy-done.1
  41.9 30.4 %relax.1 = f32[16,128,1024]{2,1,0:T(8,128)} custom-call(bf16[4,128,1024]{2,1,0:T(8,128)(2,1)} %bitcast.2, bf16[4,16,1024]{2,1,0:T(8,128)(2,1)} %bitcast.3, s32[128,128]{1,0:T(8,128)} %broadcast_in_dim.12.refs_2_, bf16[16,128]{1,0:T(8,128)(2,1)} %slice.46.refs_3_, bf16[8,2,16,128]{3,2,1,0:T(8,128)(2,1)} %copy-done.2, bf16[8,2,16,128]{3,2,1,0:T(8,128)(2,1)} %copy-done.3, ...), custom_call_target="tpu_custom_call" | custom-call | tf_op jit(solution)/shard_map/relax/pallas_call | solution.py:337
  (9 shorter events, 0.0 us)
Async XLA Ops:
  6.5 34.5 %all-gather.4.cloned.1.call-start = ((), (), s32[]{:S(2)}) async-start(), calls=%async_computation | async-start | bytes 1310720 | tf_op jit(solution)/shard_map/all_gather | solution.py:362
  8.8 13.8 %collective-permute-start = (bf16[8,1152]{1,0:T(8,128)(2,1)S(1)}, bf16[8,1152]{1,0:T(8,128)(2,1)S(1)}, u32[]{:S(2)}, u32[]{:S(2)}) collective-permute-start(bf16[8,1152]{1,0:T(8,128)(2,1)S(1)} %pad_maximum_fusion), channel_id=1, source_target_pairs={{0,1},{1,2},{2,3},{3,4},{4,5},{5,6},{6,7},{7,0},{8,9},{9,10},{10,1... | collective-permute-start | bytes 55304 | tf_op jit(solution)/shard_map/ppermute | solution.py:351
  9.3 31.6 %copy-start.6 = (s32[128]{0:T(128)S(1)}, s32[128]{0:T(128)}, u32[]{:S(2)}) copy-start(s32[128]{0:T(128)} %param.9) | copy-start | bytes 1540
  9.3 16.8 %collective-permute-start.1 = (bf16[8,1152]{1,0:T(8,128)(2,1)S(1)}, bf16[8,1152]{1,0:T(8,128)(2,1)S(1)}, u32[]{:S(2)}, u32[]{:S(2)}) collective-permute-start(bf16[8,1152]{1,0:T(8,128)(2,1)S(1)} %pad_maximum_fusion.1), channel_id=1, source_target_pairs={{0,7},{1,0},{2,1},{3,2},{4,3},{5,4},{6,5},{7,6},{8,15},{9,8},{10,9... | collective-permute-start | bytes 55304 | tf_op jit(solution)/shard_map/ppermute | solution.py:351
  19.6 7.2 %collective-permute-start.2 = (bf16[8,2,16,128]{3,2,1,0:T(8,128)(2,1)}, bf16[8,2,16,128]{3,2,1,0:T(8,128)(2,1)S(1)}, u32[]{:S(2)}, u32[]{:S(2)}) collective-permute-start(bf16[8,2,16,128]{3,2,1,0:T(8,128)(2,1)} %get-tuple-element.9), channel_id=1, source_target_pairs={{0,8},{8,16},{16,24},{24,0},{1,9},{9,17},{17,25},{25,1},{2,10},{10... | collective-permute-start | bytes 196616 | tf_op jit(solution)/shard_map/ppermute | solution.py:351
  21.6 6.0 %collective-permute-start.3 = (bf16[8,2,16,128]{3,2,1,0:T(8,128)(2,1)}, bf16[8,2,16,128]{3,2,1,0:T(8,128)(2,1)S(1)}, u32[]{:S(2)}, u32[]{:S(2)}) collective-permute-start(bf16[8,2,16,128]{3,2,1,0:T(8,128)(2,1)} %get-tuple-element.10), channel_id=1, source_target_pairs={{0,24},{8,0},{16,8},{24,16},{1,25},{9,1},{17,9},{25,17},{2,26},{10... | collective-permute-start | bytes 196616 | tf_op jit(solution)/shard_map/ppermute | solution.py:351
  22.6 18.3 %collective-permute-start.6 = (bf16[2,8,16,1024]{3,2,1,0:T(8,128)(2,1)}, bf16[2,8,16,1024]{3,2,1,0:T(8,128)(2,1)S(1)}, u32[]{:S(2)}, u32[]{:S(2)}) collective-permute-start(bf16[2,8,16,1024]{3,2,1,0:T(8,128)(2,1)} %get-tuple-element.11), channel_id=1, source_target_pairs={{0,1},{1,2},{2,3},{3,4},{4,5},{5,6},{6,7},{7,0},{8,9},{9,10},{10,1... | collective-permute-start | bytes 1572872 | tf_op jit(solution)/shard_map/ppermute | solution.py:351
  22.6 18.3 %collective-permute-start.7 = (bf16[2,8,16,1024]{3,2,1,0:T(8,128)(2,1)}, bf16[2,8,16,1024]{3,2,1,0:T(8,128)(2,1)S(1)}, u32[]{:S(2)}, u32[]{:S(2)}) collective-permute-start(bf16[2,8,16,1024]{3,2,1,0:T(8,128)(2,1)} %get-tuple-element.12), channel_id=1, source_target_pairs={{0,7},{1,0},{2,1},{3,2},{4,3},{5,4},{6,5},{7,6},{8,15},{9,8},{10,9... | collective-permute-start | bytes 1572872 | tf_op jit(solution)/shard_map/ppermute | solution.py:351
  26.8 15.1 %copy-start.2 = (bf16[8,2,16,128]{3,2,1,0:T(8,128)(2,1)}, bf16[8,2,16,128]{3,2,1,0:T(8,128)(2,1)S(1)}, u32[]{:S(2)}) copy-start(bf16[8,2,16,128]{3,2,1,0:T(8,128)(2,1)S(1)} %collective-permute-done.2.refs_4_) | copy-start | bytes 196612
  27.6 14.3 %copy-start.3 = (bf16[8,2,16,128]{3,2,1,0:T(8,128)(2,1)}, bf16[8,2,16,128]{3,2,1,0:T(8,128)(2,1)S(1)}, u32[]{:S(2)}) copy-start(bf16[8,2,16,128]{3,2,1,0:T(8,128)(2,1)S(1)} %collective-permute-done.3.refs_5_) | copy-start | bytes 196612
  27.6 13.3 %collective-permute-start.4 = (bf16[2,2,16,128]{3,2,1,0:T(8,128)(2,1)S(1)}, bf16[2,2,16,128]{3,2,1,0:T(8,128)(2,1)S(1)}, u32[]{:S(2)}, u32[]{:S(2)}) collective-permute-start(bf16[2,2,16,128]{3,2,1,0:T(8,128)(2,1)S(1)} %pad_maximum_fusion.2), channel_id=1, source_target_pairs={{0,1},{1,2},{2,3},{3,4},{4,5},{5,6},{6,7},{7,0},{8,9},{9,10},{10,1... | collective-permute-start | bytes 49160 | tf_op jit(solution)/shard_map/ppermute | solution.py:351
  27.7 13.2 %collective-permute-start.5 = (bf16[2,2,16,128]{3,2,1,0:T(8,128)(2,1)S(1)}, bf16[2,2,16,128]{3,2,1,0:T(8,128)(2,1)S(1)}, u32[]{:S(2)}, u32[]{:S(2)}) collective-permute-start(bf16[2,2,16,128]{3,2,1,0:T(8,128)(2,1)S(1)} %pad_maximum_fusion.3), channel_id=1, source_target_pairs={{0,7},{1,0},{2,1},{3,2},{4,3},{5,4},{6,5},{7,6},{8,15},{9,8},{10,9... | collective-permute-start | bytes 49160 | tf_op jit(solution)/shard_map/ppermute | solution.py:351
  40.9 1.0 %copy-start.4 = (bf16[2,2,16,128]{3,2,1,0:T(8,128)(2,1)}, bf16[2,2,16,128]{3,2,1,0:T(8,128)(2,1)S(1)}, u32[]{:S(2)}) copy-start(bf16[2,2,16,128]{3,2,1,0:T(8,128)(2,1)S(1)} %collective-permute-done.4.refs_6_) | copy-start | bytes 49156
  40.9 1.0 %copy-start.5 = (bf16[2,2,16,128]{3,2,1,0:T(8,128)(2,1)}, bf16[2,2,16,128]{3,2,1,0:T(8,128)(2,1)S(1)}, u32[]{:S(2)}) copy-start(bf16[2,2,16,128]{3,2,1,0:T(8,128)(2,1)S(1)} %collective-permute-done.5.refs_7_) | copy-start | bytes 49156
  40.9 1.0 %copy-start = (bf16[2,8,16,1024]{3,2,1,0:T(8,128)(2,1)}, bf16[2,8,16,1024]{3,2,1,0:T(8,128)(2,1)S(1)}, u32[]{:S(2)}) copy-start(bf16[2,8,16,1024]{3,2,1,0:T(8,128)(2,1)S(1)} %collective-permute-done.6.refs_8_) | copy-start | bytes 1572868
  41.0 1.0 %copy-start.1 = (bf16[2,8,16,1024]{3,2,1,0:T(8,128)(2,1)}, bf16[2,8,16,1024]{3,2,1,0:T(8,128)(2,1)S(1)}, u32[]{:S(2)}) copy-start(bf16[2,8,16,1024]{3,2,1,0:T(8,128)(2,1)S(1)} %collective-permute-done.7.refs_9_) | copy-start | bytes 1572868
Sparse Core Ops, SparseCore 0:
  9.2 31.7 all-gather.3

commit v3 on v2

--- a/solution.py
+++ b/solution.py
@@ -30,15 +30,9 @@
     return high, value - high
 
 
-def edges_kernel(
-    u_top, u_bot, s_top, s_bot, j_top, j_bot,
-    u_left, u_right, s_left, s_right, j_left, j_right,
-    to_prev, to_next, to_left, to_right, *, pairs, tiles, blocks,
-):
+def rows_kernel(u_top, u_bot, s_top, s_bot, j_top, j_bot, to_prev, to_next, *, pairs, tiles):
     even8 = checker(8)
-    even16 = checker(16)
     sub = lax.broadcasted_iota(jnp.int32, (8, LANES), 0)
-    lane = lax.broadcasted_iota(jnp.int32, (16, LANES), 1)
     field_rows = sub < 5
 
     def pair_rows(m, _):
@@ -77,8 +71,13 @@
 
     lax.fori_loop(0, pairs, pair_rows, 0)
 
-    group_of = lane // 8
-    first_half = (lane & 7) < 4
+
+def cols_kernel(
+    u_left, u_right, s_left, s_right, j_left, j_right, r_top, r_bot, k_top, k_bot,
+    to_left, to_right, small_prev, small_next, *, pairs, tiles, blocks,
+):
+    even16 = checker(16)
+    lane = lax.broadcasted_iota(jnp.int32, (16, LANES), 1)
 
     def block_cols(q, _):
         rows = pl.ds(pl.multiple_of(16 * q, 16), 16)
@@ -108,49 +107,72 @@
                         total = jnp.where((l8 >= far_slot) & (l8 < far_slot + 4), far, total)
                 packed.append(total)
             high, low = split_high_low(packed[0])
-            out_ref[q, 0] = jnp.concatenate([high, low], 0).astype(jnp.bfloat16)
-            out_ref[q, 1] = jnp.concatenate([packed[1], packed[2]], 0).astype(jnp.bfloat16)
+            out_ref[2 * q] = jnp.concatenate([high, low], 0).astype(jnp.bfloat16)
+            out_ref[2 * q + 1] = jnp.concatenate([packed[1], packed[2]], 0).astype(jnp.bfloat16)
         return 0
 
     lax.fori_loop(0, blocks, block_cols, 0)
-
-
-def pack_edges(field, sigma, current):
+    for out_ref, near, r_ref, k_ref in (
+        (small_prev, 0, r_top, k_top),
+        (small_next, 2 * blocks - 2, r_bot, k_bot),
+    ):
+        for i in (0, 1):
+            out_ref[i] = to_left[near + i]
+            out_ref[2 + i] = to_right[near + i]
+        for c in range(tiles):
+            out_ref[4 + c] = r_ref[:, c * LANES : (c + 1) * LANES]
+        out_ref[4 + tiles] = f32(k_ref[...]).astype(jnp.bfloat16)
+
+
+def whole_at(shape, index):
+    return pl.BlockSpec(shape, lambda i: index)
+
+
+def pack_rows(field, sigma, current):
+    layers, rows, cols = field.shape
+    pairs, tiles = layers // 2, cols // LANES
+
+    def row_specs(height):
+        shape = (layers, height, cols)
+        return [whole_at(shape, (0, 0, 0)), whole_at(shape, (0, rows // height - 1, 0))]
+
+    shape = (2, pairs, 16, cols)
+    return pl.pallas_call(
+        functools.partial(rows_kernel, pairs=pairs, tiles=tiles),
+        grid=(1,),
+        in_specs=row_specs(8) + row_specs(16) * 2,
+        out_specs=[whole_at(shape, (0,) * 4)] * 2,
+        out_shape=[jax.ShapeDtypeStruct(shape, jnp.bfloat16)] * 2,
+        compiler_params=pltpu.CompilerParams(vmem_limit_bytes=VMEM_BYTES),
+        cost_estimate=pl.CostEstimate(flops=0, bytes_accessed=12 << 20, transcendentals=0),
+        name="pack_rows",
+    )(field, field, sigma, sigma, current, current)
+
+
+def pack_cols(field, sigma, current, rotor_cycle, skew):
     layers, rows, cols = field.shape
     pairs, tiles, blocks = layers // 2, cols // LANES, rows // 16
-
-    def whole(shape, index):
-        return pl.BlockSpec(shape, lambda i: index)
-
-    def row_specs(height):
-        return [
-            whole((layers, height, cols), (0, 0, 0)),
-            whole((layers, height, cols), (0, rows // height - 1, 0)),
-        ]
-
-    col_specs = [
-        whole((layers, rows, LANES), (0, 0, 0)),
-        whole((layers, rows, LANES), (0, 0, tiles - 1)),
-    ]
-    ta_shape = (2, pairs, 16, cols)
-    az_shape = (blocks, 2, 16, LANES)
+    shape = (layers, rows, LANES)
+    cols_specs = [whole_at(shape, (0, 0, 0)), whole_at(shape, (0, 0, tiles - 1))]
+    rotor_specs = [whole_at((16, cols), (i, 0)) for i in (0, blocks - 1)]
+    skew_specs = [whole_at((16, LANES), (i, 0)) for i in (0, blocks - 1)]
+    out = [(2 * blocks, 16, LANES)] * 2 + [(tiles + 5, 16, LANES)] * 2
     return pl.pallas_call(
-        functools.partial(edges_kernel, pairs=pairs, tiles=tiles, blocks=blocks),
+        functools.partial(cols_kernel, pairs=pairs, tiles=tiles, blocks=blocks),
         grid=(1,),
-        in_specs=row_specs(8) + row_specs(16) * 2 + col_specs * 3,
-        out_specs=[whole(ta_shape, (0,) * 4)] * 2 + [whole(az_shape, (0,) * 4)] * 2,
-        out_shape=[jax.ShapeDtypeStruct(ta_shape, jnp.bfloat16)] * 2
-        + [jax.ShapeDtypeStruct(az_shape, jnp.bfloat16)] * 2,
+        in_specs=cols_specs * 3 + rotor_specs + skew_specs,
+        out_specs=[whole_at(x, (0,) * 3) for x in out],
+        out_shape=[jax.ShapeDtypeStruct(x, jnp.bfloat16) for x in out],
         compiler_params=pltpu.CompilerParams(vmem_limit_bytes=VMEM_BYTES),
-        name="edges",
-    )(
-        field, field, sigma, sigma, current, current,
-        field, field, sigma, sigma, current, current,
-    )
+        cost_estimate=pl.CostEstimate(flops=0, bytes_accessed=16 << 20, transcendentals=0),
+        name="pack_cols",
+    )(field, field, sigma, sigma, current, current, rotor_cycle, rotor_cycle, skew, skew)
 
 
 def relax_kernel(*refs, slots, pairs, rows, tiles):
-    (rotor, rotor_edge, skew, skew_edge, from_left, from_right, corner_prev, corner_next, from_prev, from_next,
+    rotor, refs = refs[:slots], refs[slots:]
+    others, refs = refs[: slots - 3], refs[slots - 3 :]
+    (skew, small_prev, small_next, from_left, from_right, from_prev, from_next,
      u_ref, s_ref, j_ref, out_ref,
      red_a, red_b, black_a, black_b, sig_r, sig_b, cur_r, cur_b, side) = refs
     g = pl.program_id(0)
@@ -166,18 +188,13 @@
     def prologue():
         panels = slots * tiles
         bits = (panels - 1).bit_length()
-        here = lax.axis_index("az")
-        device = [lax.rem(here + slots - r, slots) for r in range(slots)]
         want = [(panels - tiles - 1 + p) % panels for p in range(tiles + 2)]
         needs = [set(want)]
         for bit in range(bits):
             needs.append(needs[-1] | {(q - (1 << bit)) % panels for q in needs[-1]})
 
-        def place(sources, at, turn, spots):
-            cur = {}
-            for q in sorted(needs[bits]):
-                c = q % tiles
-                cur[q] = f32(sources[device[slots - 1 - q // tiles], at, c * LANES : (c + 1) * LANES])
+        def place(panel, turn, spots):
+            cur = {q: f32(panel(slots - 1 - q // tiles, q % tiles)) for q in sorted(needs[bits])}
             for bit in reversed(range(bits)):
                 on = ((turn >> bit) & 1) == 1
                 cur = {q: jnp.where(on, cur[(q - (1 << bit)) % panels], cur[q]) for q in sorted(needs[bit])}
@@ -186,18 +203,33 @@
             zero = jnp.zeros((8, LANES), jnp.float32)
             for buf in (red_a, red_b, black_a, black_b):
                 for c in range(tiles + 1):
-                    for half, to in enumerate(spots):
+                    for half, to in spots:
                         buf[0, c, to, :] = placed[c][8 * half : 8 * half + 8]
                         buf[pairs + 1, c, to, :] = zero
 
         def rotor_rows(b, _):
             at = pl.ds(pl.multiple_of(16 * b, 16), 16)
-            spots = [pl.ds(pl.multiple_of(16 * b + EDGE + 8 * half, 8), 8) for half in (0, 1)]
-            place(rotor, at, skew[at, :], spots)
+            spots = [(half, pl.ds(pl.multiple_of(16 * b + EDGE + 8 * half, 8), 8)) for half in (0, 1)]
+            place(lambda r, c: rotor[r][at, c * LANES : (c + 1) * LANES], skew[at, :], spots)
             return 0
 
         lax.fori_loop(0, blocks, rotor_rows, 0)
-        place(rotor_edge, slice(0, 16), skew_edge[...].astype(jnp.int32), [pl.ds(0, 8), pl.ds(EDGE + rows, 8)])
+        base = 2 * blocks + 4
+        for small, first, spot in (
+            (small_prev, 0, (1, pl.ds(0, 8))),
+            (small_next, tiles, (0, pl.ds(EDGE + rows, 8))),
+        ):
+
+            def edge_panel(r, c, small=small, first=first):
+                if r == 0:
+                    return small[4 + c]
+                if r == 1:
+                    return from_left[base + first + c]
+                if r == slots - 1:
+                    return from_right[base + first + c]
+                return others[r - 2][first + c]
+
+            place(edge_panel, f32(small[4 + tiles]).astype(jnp.int32), [spot])
 
         left_slot = (lane & 7) < 4
 
@@ -212,10 +244,9 @@
                 side[0, item, q] = jnp.where(left_slot, a, b) * scale
                 side[1, item, q] = jnp.where(left_slot, b, a) * scale
 
-        for q in range(blocks):
-            decode(q, from_left[q], from_right[q])
-        decode(blocks, corner_prev[0], corner_prev[1])
-        decode(blocks + 1, corner_next[0], corner_next[1])
+        for q in range(blocks + 2):
+            pick = slice(2 * q, 2 * q + 2)
+            decode(q, from_left[pick], from_right[pick])
 
     @pl.when(g < pairs)
     def load():
@@ -317,9 +348,9 @@
             half_step(g - lag, colour, own, other, sig, cur, *where, write)
 
 
-def relax(rotor, rotor_edge, skew, skew_edge, from_left, from_right, corner_prev, corner_next, from_prev, from_next, field, sigma, current):
+def relax(rotor, others, skew, small_prev, small_next, from_left, from_right, from_prev, from_next, field, sigma, current):
     layers, rows, cols = field.shape
-    pairs, tiles, slots = layers // 2, cols // LANES, rotor.shape[0]
+    pairs, tiles, slots = layers // 2, cols // LANES, len(rotor)
     ext = rows + 2 * EDGE
 
     def whole(array):
@@ -331,7 +362,7 @@
 
     halo = pl.BlockSpec((2, 1, 16, cols), lambda g: (0, coming(g), 0, 0))
     block = pl.BlockSpec((2, rows, cols), lambda g: (coming(g), 0, 0))
-    fixed = [rotor, rotor_edge, skew, skew_edge, from_left, from_right, corner_prev, corner_next]
+    fixed = list(rotor) + list(others) + [skew, small_prev, small_next, from_left, from_right]
     state = pltpu.VMEM((pairs + 2, tiles + 1, ext, LANES), jnp.float32)
     coef = pltpu.VMEM((pairs, tiles + 1, ext, LANES), jnp.float32)
     return pl.pallas_call(
@@ -353,24 +384,24 @@
 
 def local(field, sigma, current, rotor_cycle, skew_list):
     rows, cols = field.shape[1:]
+    tiles = cols // LANES
+    count = lax.axis_size("az")
     skew = jnp.broadcast_to(skew_list[:, None], (rows, LANES))
-    slab = [
-        jnp.concatenate([rotor_cycle[part], skew[part].astype(jnp.bfloat16)], 1)
-        for part in (slice(rows - EDGE, rows), slice(0, EDGE))
-    ]
-    slab = jnp.concatenate([moved(slab[0], "ta", 1), moved(slab[1], "ta", -1)], 0)
-    rotor = lax.all_gather(rotor_cycle, "az")
-    rotor_edge = lax.all_gather(slab[:, :cols], "az")
-    skew_edge = slab[:, cols:]
-    to_prev, to_next, to_left, to_right = pack_edges(field, sigma, current)
-    from_left = moved(to_right, "az", 1)
-    from_right = moved(to_left, "az", -1)
+    rotor = [rotor_cycle] + [moved(rotor_cycle, "az", s) for s in range(1, count)]
+    to_prev, to_next = pack_rows(field, sigma, current)
     from_prev = moved(to_next, "ta", 1)
     from_next = moved(to_prev, "ta", -1)
-    corner_prev = moved(jnp.stack([from_left[-1], from_right[-1]]), "ta", 1)
-    corner_next = moved(jnp.stack([from_left[0], from_right[0]]), "ta", -1)
+    to_left, to_right, small_to_prev, small_to_next = pack_cols(field, sigma, current, rotor_cycle, skew)
+    small_prev = moved(small_to_next, "ta", 1)
+    small_next = moved(small_to_prev, "ta", -1)
+    rotor_edge = [small_prev[4 : 4 + tiles], small_next[4 : 4 + tiles]]
+    from_right = moved(jnp.concatenate([to_left, small_prev[:2], small_next[:2]] + rotor_edge), "az", -1)
+    from_left = moved(jnp.concatenate([to_right, small_prev[2:4], small_next[2:4]] + rotor_edge), "az", 1)
+    rotor_edge = jnp.concatenate(rotor_edge)
+    others = [moved(rotor_edge, "az", s) for s in range(2, count - 1)]
     return relax(
-        rotor, rotor_edge, skew, skew_edge, from_left, from_right, corner_prev, corner_next, from_prev, from_next, field, sigma, current
+        rotor, others, skew, small_prev, small_next, from_left, from_right, from_prev, from_next,
+        field, sigma, current,
     )
 
 

time: 79.5 us -> 72.7 us (0.914)
  between operations: 13.5 us -> 0.14 us
  waiting for transfers between devices: 1.56 us -> 11.7 us
  blocking collectives: 9.67 us -> 0 us
  starting transfers between devices: 14.6 us -> 19.2 us
  Pallas kernels: 36.6 us -> 38.3 us
    ppermute x8 -> x10, waiting for transfers between devices: 0.83 us -> 11.7 us  [moved(): lax.ppermute(value, axis, [(i, (i + steps) % count) for i in range(count)])]
    all_gather x1 -> x0, blocking collectives: 9.67 us -> none  [local(): rotor_edge = lax.all_gather(slab[:, :cols], 'az')]
    ppermute x8 -> x10, starting transfers between devices: 14.6 us -> 19.2 us  [moved(): lax.ppermute(value, axis, [(i, (i + steps) % count) for i in range(count)])]
    unnamed x15 -> x30, local copies, waits for them, and re-layouts: 0.06 us -> 1.79 us
    pallas_call x1 -> x2, Pallas kernels: 6.25 us -> 7.92 us  [the longest x1 4.59 us: pack_cols(): pl.pallas_call(functools.partial(cols_kernel, pairs=pairs, tiles=tiles, b...]
    slice x6 -> x0, local copies, waits for them, and re-layouts: 1.41 us -> none  [the longest x1 0.74 us: local(): rotor_cycle[part]]
  transfers between devices with their start and end apart: 9 -> 10, of which waited for: 1 -> 3; matrix products, arithmetic and copies ran while one was open for 3% -> 0% of each run, Pallas kernels for 8% -> 5%
where the time goes in v3:
time: 72.7 us; the launch traced here: 72.5 us
  Pallas kernels  38.3 us (53%)
  starting transfers between devices  19.2 us (26%)
  waiting for transfers between devices  11.7 us (16%)
  local copies, waits for them, and re-layouts  3.16 us (4%)
    pallas_call x1, Pallas kernels, relax(): pl.pallas_call(functools.partial(relax_kernel, slots=slots, pairs=pairs,...  30.4 us
    ppermute x10, starting transfers between devices, moved(): lax.ppermute(value, axis, [(i, (i + steps) % count) for i in range(count)])  19.2 us
    ppermute x10, waiting for transfers between devices, moved(): lax.ppermute(value, axis, [(i, (i + steps) % count) for i in range(count)])  11.7 us
    pallas_call x1, Pallas kernels, pack_cols(): pl.pallas_call(functools.partial(cols_kernel, pairs=pairs, tiles=tiles, b...  4.59 us
    pallas_call x1, Pallas kernels, pack_rows(): pl.pallas_call(functools.partial(rows_kernel, pairs=pairs, tiles=tiles),...  3.33 us
    unnamed x30, local copies, waits for them, and re-layouts  1.79 us
  transfers between devices with their start and end apart: 10, of which 3 were waited for; matrix products, arithmetic and copies ran while one was open for 0% of the time, Pallas kernels for 5%

profile of v3, /device:TPU:0, one launch (start us, length us, event | category | flops | bytes accessed | tf_op | source)
XLA Modules:
  0.0 72.5 jit_solution(2371939285310957154)
XLA Ops:
  0.0 1.3 %broadcast_in_dim.2.k_top.k_bot.refs_5_ = s32[128,128]{1,0:T(8,128)} broadcast(s32[128]{0:T(128)} %param.9), dimensions={0} | broadcast | bytes 66048 | tf_op jit(solution)/shard_map/broadcast_in_dim | solution.py:389
  1.3 4.6 %pack_cols.1 = (bf16[16,16,128]{2,1,0:T(8,128)(2,1)}, bf16[16,16,128]{2,1,0:T(8,128)(2,1)}, bf16[13,16,128]{2,1,0:T(8,128)(2,1)}, bf16[13,16,128]{2,1,0:T(8,128)(2,1)}) custom-call(f32[16,128,1024]{2,1,0:T(8,128)} %refs_12_.1, f32[16,128,1024]{2,1,0:T(8,128)} %refs_12_.1, bf16[16,128,1024]{2,1,0:T(8,128)(2,1)} %refs_13_.1, bf16[16,128,1024]{2,1,0:T(8,128)(2,1)} %refs_13_.1, ...), custom_call_target="tpu_custom_call" | custom-call | bytes 16777216 | tf_op jit(solution)/shard_map/pack_cols/pallas_call | solution.py:160
  5.9 0.5 collective-permute-start.3
  6.4 0.0 copy-start.11
  6.4 0.0 copy-start.12
  6.4 0.0 copy-start
  6.4 4.1 %collective-permute-start.4 = (bf16[13,16,128]{2,1,0:T(8,128)(2,1)}, bf16[13,16,128]{2,1,0:T(8,128)(2,1)S(1)}, u32[]{:S(2)}, u32[]{:S(2)}) collective-permute-start(bf16[13,16,128]{2,1,0:T(8,128)(2,1)} %get-tuple-element.12), channel_id=1, source_target_pairs={{0,7},{1,0},{2,1},{3,2},{4,3},{5,4},{6,5},{7,6},{8,15},{9,8},{10,9... | collective-permute-start | bytes 159752 | tf_op jit(solution)/shard_map/ppermute | solution.py:382
  10.5 3.3 %pack_rows.1 = (bf16[2,8,16,1024]{3,2,1,0:T(8,128)(2,1)}, bf16[2,8,16,1024]{3,2,1,0:T(8,128)(2,1)}) custom-call(f32[16,128,1024]{2,1,0:T(8,128)} %refs_12_.1, f32[16,128,1024]{2,1,0:T(8,128)} %refs_12_.1, bf16[16,128,1024]{2,1,0:T(8,128)(2,1)} %refs_13_.1, bf16[16,128,1024]{2,1,0:T(8,128)(2,1)} %refs_13_.1, bf16[16,128,1024]{2,1,0:T(8,128)(2,1)} %refs_14_.1, ...), custom_call_target="tpu_custom_call" | custom-call | bytes 12582912 | tf_op jit(solution)/shard_map/pack_rows/pallas_call | solution.py:140
  13.8 0.0 collective-permute-start.8
  13.8 3.5 %collective-permute-start.9 = (bf16[2,8,16,1024]{3,2,1,0:T(8,128)(2,1)}, bf16[2,8,16,1024]{3,2,1,0:T(8,128)(2,1)S(1)}, u32[]{:S(2)}, u32[]{:S(2)}) collective-permute-start(bf16[2,8,16,1024]{3,2,1,0:T(8,128)(2,1)} %get-tuple-element.16), channel_id=1, source_target_pairs={{0,7},{1,0},{2,1},{3,2},{4,3},{5,4},{6,5},{7,6},{8,15},{9,8},{10,9... | collective-permute-start | bytes 1572872 | tf_op jit(solution)/shard_map/ppermute | solution.py:382
  17.4 0.0 copy-done.11
  17.4 0.0 copy-done.12
  17.4 0.0 collective-permute-done.3.refs_6_
  17.4 0.0 copy-start.6
  17.4 0.0 collective-permute-done.4.refs_7_
  17.5 0.0 copy-start.7
  17.5 2.9 %collective-permute-start.7 = (bf16[36,16,128]{2,1,0:T(8,128)(2,1)S(1)}, bf16[36,16,128]{2,1,0:T(8,128)(2,1)S(1)}, u32[]{:S(2)}, u32[]{:S(2)}) collective-permute-start(bf16[36,16,128]{2,1,0:T(8,128)(2,1)S(1)} %get-tuple-element.17), channel_id=1, source_target_pairs={{0,24},{8,0},{16,8},{24,16},{1,25},{9,1},{17,9},{25,17},{2,26},{10... | collective-permute-start | bytes 442376 | tf_op jit(solution)/shard_map/ppermute | solution.py:382
  20.5 0.0 collective-permute-start.6
  20.5 1.2 %collective-permute-start.5 = (bf16[16,16,128]{2,1,0:T(8,128)(2,1)S(1)}, bf16[16,16,128]{2,1,0:T(8,128)(2,1)S(1)}, u32[]{:S(2)}, u32[]{:S(2)}) collective-permute-start(bf16[16,16,128]{2,1,0:T(8,128)(2,1)S(1)} %pad_maximum_fusion), channel_id=1, source_target_pairs={{0,16},{8,24},{16,0},{24,8},{1,17},{9,25},{17,1},{25,9},{2,18},{10... | collective-permute-start | bytes 196616 | tf_op jit(solution)/shard_map/ppermute | solution.py:382
  21.6 3.2 %collective-permute-done.5.refs_4_ = bf16[16,16,128]{2,1,0:T(8,128)(2,1)S(1)} collective-permute-done((bf16[16,16,128]{2,1,0:T(8,128)(2,1)S(1)}, bf16[16,16,128]{2,1,0:T(8,128)(2,1)S(1)}, u32[]{:S(2)}, u32[]{:S(2)}) %collective-permute-start.5) | collective-permute-done | bytes 65568 | tf_op jit(solution)/shard_map/ppermute | solution.py:382
  24.8 0.0 copy-done
  24.8 0.0 copy-start.10
  24.8 6.4 %collective-permute-start.2 = (bf16[128,1024]{1,0:T(8,128)(2,1)S(1)}, bf16[128,1024]{1,0:T(8,128)(2,1)S(1)}, u32[]{:S(2)}, u32[]{:S(2)}) collective-permute-start(bf16[128,1024]{1,0:T(8,128)(2,1)S(1)} %copy-done), channel_id=1, source_target_pairs={{0,24},{8,0},{16,8},{24,16},{1,25},{9,1},{17,9},{25,17},{2,26},{10... | collective-permute-start | bytes 786440 | tf_op jit(solution)/shard_map/ppermute | solution.py:382
  31.2 0.0 collective-permute-done.7.refs_9_
  31.2 0.4 collective-permute-start.1
  31.6 0.0 collective-permute-done.6.refs_8_
  31.6 0.0 copy-start.9
  31.6 0.2 collective-permute-start
  31.8 3.3 %collective-permute-done.2.refs_3_ = bf16[128,1024]{1,0:T(8,128)(2,1)S(1)} collective-permute-done((bf16[128,1024]{1,0:T(8,128)(2,1)S(1)}, bf16[128,1024]{1,0:T(8,128)(2,1)S(1)}, u32[]{:S(2)}, u32[]{:S(2)}) %collective-permute-start.2) | collective-permute-done | bytes 262176 | tf_op jit(solution)/shard_map/ppermute | solution.py:382
  35.1 0.0 copy-start.3
  35.1 5.2 %collective-permute-done.1.refs_2_ = bf16[128,1024]{1,0:T(8,128)(2,1)S(1)} collective-permute-done((bf16[128,1024]{1,0:T(8,128)(2,1)S(1)}, bf16[128,1024]{1,0:T(8,128)(2,1)S(1)}, u32[]{:S(2)}, u32[]{:S(2)}) %collective-permute-start.1) | collective-permute-done | bytes 262176 | tf_op jit(solution)/shard_map/ppermute | solution.py:382
  40.4 0.0 copy-start.4
  40.4 0.0 collective-permute-done.refs_1_
  40.4 0.0 copy-start.5
  40.4 0.0 collective-permute-done.8.refs_10_
  40.4 0.0 copy-start.1
  40.4 0.0 collective-permute-done.9.refs_11_
  40.4 0.0 copy-done.6
  40.4 0.0 copy-done.7
  40.4 0.0 copy-done.10
  40.4 0.0 copy-done.8
  40.4 0.0 copy-done.9
  40.4 0.0 copy-done.3
  40.4 0.6 copy-done.4
  41.1 0.1 copy-done.5
  41.2 0.2 copy-done.1
  41.3 0.8 %copy-done.2 = bf16[2,8,16,1024]{3,2,1,0:T(8,128)(2,1)} copy-done((bf16[2,8,16,1024]{3,2,1,0:T(8,128)(2,1)}, bf16[2,8,16,1024]{3,2,1,0:T(8,128)(2,1)S(1)}, u32[]{:S(2)}) %copy-start.2) | copy-done | bytes 524312
  42.1 30.4 %relax.1 = f32[16,128,1024]{2,1,0:T(8,128)} custom-call(bf16[128,1024]{1,0:T(8,128)(2,1)} %refs_0_.1, bf16[128,1024]{1,0:T(8,128)(2,1)} %copy-done.5, bf16[128,1024]{1,0:T(8,128)(2,1)} %copy-done.4, bf16[128,1024]{1,0:T(8,128)(2,1)} %copy-done.3, bf16[16,16,128]{2,1,0:T(8,128)(2,1)} %copy-done.10, s32[128,128]{1,0:T(8,128)} %broadcast_in_dim.2.k_top.k_bot.refs_5_, ...), custom_call_target="tpu_custom_call" | custom-call | tf_op jit(solution)/shard_map/relax/pallas_call | solution.py:368
  (8 shorter events, 0.1 us)
Async XLA Ops:
  5.9 11.5 %collective-permute-start.3 = (bf16[13,16,128]{2,1,0:T(8,128)(2,1)}, bf16[13,16,128]{2,1,0:T(8,128)(2,1)S(1)}, u32[]{:S(2)}, u32[]{:S(2)}) collective-permute-start(bf16[13,16,128]{2,1,0:T(8,128)(2,1)} %get-tuple-element.11), channel_id=1, source_target_pairs={{0,1},{1,2},{2,3},{3,4},{4,5},{5,6},{6,7},{7,0},{8,9},{9,10},{10,1... | collective-permute-start | bytes 159752 | tf_op jit(solution)/shard_map/ppermute | solution.py:382
  6.4 11.0 %copy-start.11 = (bf16[16,16,128]{2,1,0:T(8,128)(2,1)S(1)}, bf16[16,16,128]{2,1,0:T(8,128)(2,1)}, u32[]{:S(2)}) copy-start(bf16[16,16,128]{2,1,0:T(8,128)(2,1)} %get-tuple-element.14) | copy-start | bytes 196612
  6.4 11.0 %copy-start.12 = (bf16[16,16,128]{2,1,0:T(8,128)(2,1)S(1)}, bf16[16,16,128]{2,1,0:T(8,128)(2,1)}, u32[]{:S(2)}) copy-start(bf16[16,16,128]{2,1,0:T(8,128)(2,1)} %get-tuple-element.13) | copy-start | bytes 196612
  6.4 18.4 %copy-start = (bf16[128,1024]{1,0:T(8,128)(2,1)S(1)}, bf16[128,1024]{1,0:T(8,128)(2,1)}, u32[]{:S(2)}) copy-start(bf16[128,1024]{1,0:T(8,128)(2,1)} %refs_0_.1) | copy-start | bytes 786436
  6.4 11.0 %collective-permute-start.4 = (bf16[13,16,128]{2,1,0:T(8,128)(2,1)}, bf16[13,16,128]{2,1,0:T(8,128)(2,1)S(1)}, u32[]{:S(2)}, u32[]{:S(2)}) collective-permute-start(bf16[13,16,128]{2,1,0:T(8,128)(2,1)} %get-tuple-element.12), channel_id=1, source_target_pairs={{0,7},{1,0},{2,1},{3,2},{4,3},{5,4},{6,5},{7,6},{8,15},{9,8},{10,9... | collective-permute-start | bytes 159752 | tf_op jit(solution)/shard_map/ppermute | solution.py:382
  13.8 26.5 %collective-permute-start.8 = (bf16[2,8,16,1024]{3,2,1,0:T(8,128)(2,1)}, bf16[2,8,16,1024]{3,2,1,0:T(8,128)(2,1)S(1)}, u32[]{:S(2)}, u32[]{:S(2)}) collective-permute-start(bf16[2,8,16,1024]{3,2,1,0:T(8,128)(2,1)} %get-tuple-element.15), channel_id=1, source_target_pairs={{0,1},{1,2},{2,3},{3,4},{4,5},{5,6},{6,7},{7,0},{8,9},{9,10},{10,1... | collective-permute-start | bytes 1572872 | tf_op jit(solution)/shard_map/ppermute | solution.py:382
  13.8 26.5 %collective-permute-start.9 = (bf16[2,8,16,1024]{3,2,1,0:T(8,128)(2,1)}, bf16[2,8,16,1024]{3,2,1,0:T(8,128)(2,1)S(1)}, u32[]{:S(2)}, u32[]{:S(2)}) collective-permute-start(bf16[2,8,16,1024]{3,2,1,0:T(8,128)(2,1)} %get-tuple-element.16), channel_id=1, source_target_pairs={{0,7},{1,0},{2,1},{3,2},{4,3},{5,4},{6,5},{7,6},{8,15},{9,8},{10,9... | collective-permute-start | bytes 1572872 | tf_op jit(solution)/shard_map/ppermute | solution.py:382
  17.4 23.0 %copy-start.6 = (bf16[13,16,128]{2,1,0:T(8,128)(2,1)}, bf16[13,16,128]{2,1,0:T(8,128)(2,1)S(1)}, u32[]{:S(2)}) copy-start(bf16[13,16,128]{2,1,0:T(8,128)(2,1)S(1)} %collective-permute-done.3.refs_6_) | copy-start | bytes 159748
  17.5 22.9 %copy-start.7 = (bf16[13,16,128]{2,1,0:T(8,128)(2,1)}, bf16[13,16,128]{2,1,0:T(8,128)(2,1)S(1)}, u32[]{:S(2)}) copy-start(bf16[13,16,128]{2,1,0:T(8,128)(2,1)S(1)} %collective-permute-done.4.refs_7_) | copy-start | bytes 159748
  17.5 13.6 %collective-permute-start.7 = (bf16[36,16,128]{2,1,0:T(8,128)(2,1)S(1)}, bf16[36,16,128]{2,1,0:T(8,128)(2,1)S(1)}, u32[]{:S(2)}, u32[]{:S(2)}) collective-permute-start(bf16[36,16,128]{2,1,0:T(8,128)(2,1)S(1)} %get-tuple-element.17), channel_id=1, source_target_pairs={{0,24},{8,0},{16,8},{24,16},{1,25},{9,1},{17,9},{25,17},{2,26},{10... | collective-permute-start | bytes 442376 | tf_op jit(solution)/shard_map/ppermute | solution.py:382
  20.5 11.1 %collective-permute-start.6 = (bf16[36,16,128]{2,1,0:T(8,128)(2,1)S(1)}, bf16[36,16,128]{2,1,0:T(8,128)(2,1)S(1)}, u32[]{:S(2)}, u32[]{:S(2)}) collective-permute-start(bf16[36,16,128]{2,1,0:T(8,128)(2,1)S(1)} %get-tuple-element.18), channel_id=1, source_target_pairs={{0,8},{8,16},{16,24},{24,0},{1,9},{9,17},{17,25},{25,1},{2,10},{10... | collective-permute-start | bytes 442376 | tf_op jit(solution)/shard_map/ppermute | solution.py:382
  20.5 4.3 %collective-permute-start.5 = (bf16[16,16,128]{2,1,0:T(8,128)(2,1)S(1)}, bf16[16,16,128]{2,1,0:T(8,128)(2,1)S(1)}, u32[]{:S(2)}, u32[]{:S(2)}) collective-permute-start(bf16[16,16,128]{2,1,0:T(8,128)(2,1)S(1)} %pad_maximum_fusion), channel_id=1, source_target_pairs={{0,16},{8,24},{16,0},{24,8},{1,17},{9,25},{17,1},{25,9},{2,18},{10... | collective-permute-start | bytes 196616 | tf_op jit(solution)/shard_map/ppermute | solution.py:382
  24.8 15.6 %copy-start.10 = (bf16[16,16,128]{2,1,0:T(8,128)(2,1)}, bf16[16,16,128]{2,1,0:T(8,128)(2,1)S(1)}, u32[]{:S(2)}) copy-start(bf16[16,16,128]{2,1,0:T(8,128)(2,1)S(1)} %collective-permute-done.5.refs_4_) | copy-start | bytes 196612
  24.8 10.3 %collective-permute-start.2 = (bf16[128,1024]{1,0:T(8,128)(2,1)S(1)}, bf16[128,1024]{1,0:T(8,128)(2,1)S(1)}, u32[]{:S(2)}, u32[]{:S(2)}) collective-permute-start(bf16[128,1024]{1,0:T(8,128)(2,1)S(1)} %copy-done), channel_id=1, source_target_pairs={{0,24},{8,0},{16,8},{24,16},{1,25},{9,1},{17,9},{25,17},{2,26},{10... | collective-permute-start | bytes 786440 | tf_op jit(solution)/shard_map/ppermute | solution.py:382
  31.2 9.3 %copy-start.8 = (bf16[36,16,128]{2,1,0:T(8,128)(2,1)}, bf16[36,16,128]{2,1,0:T(8,128)(2,1)S(1)}, u32[]{:S(2)}) copy-start(bf16[36,16,128]{2,1,0:T(8,128)(2,1)S(1)} %collective-permute-done.7.refs_9_) | copy-start | bytes 442372
  31.2 9.2 %collective-permute-start.1 = (bf16[128,1024]{1,0:T(8,128)(2,1)S(1)}, bf16[128,1024]{1,0:T(8,128)(2,1)S(1)}, u32[]{:S(2)}, u32[]{:S(2)}) collective-permute-start(bf16[128,1024]{1,0:T(8,128)(2,1)S(1)} %copy-done), channel_id=1, source_target_pairs={{0,16},{8,24},{16,0},{24,8},{1,17},{9,25},{17,1},{25,9},{2,18},{10... | collective-permute-start | bytes 786440 | tf_op jit(solution)/shard_map/ppermute | solution.py:382
  31.6 8.8 %copy-start.9 = (bf16[36,16,128]{2,1,0:T(8,128)(2,1)}, bf16[36,16,128]{2,1,0:T(8,128)(2,1)S(1)}, u32[]{:S(2)}) copy-start(bf16[36,16,128]{2,1,0:T(8,128)(2,1)S(1)} %collective-permute-done.6.refs_8_) | copy-start | bytes 442372
  31.6 8.8 %collective-permute-start = (bf16[128,1024]{1,0:T(8,128)(2,1)S(1)}, bf16[128,1024]{1,0:T(8,128)(2,1)S(1)}, u32[]{:S(2)}, u32[]{:S(2)}) collective-permute-start(bf16[128,1024]{1,0:T(8,128)(2,1)S(1)} %copy-done), channel_id=1, source_target_pairs={{0,8},{8,16},{16,24},{24,0},{1,9},{9,17},{17,25},{25,1},{2,10},{10... | collective-permute-start | bytes 786440 | tf_op jit(solution)/shard_map/ppermute | solution.py:382
  35.1 5.3 %copy-start.3 = (bf16[128,1024]{1,0:T(8,128)(2,1)}, bf16[128,1024]{1,0:T(8,128)(2,1)S(1)}, u32[]{:S(2)}) copy-start(bf16[128,1024]{1,0:T(8,128)(2,1)S(1)} %collective-permute-done.2.refs_3_) | copy-start | bytes 786436
  40.4 0.7 copy-start.4
  40.4 0.8 %copy-start.5 = (bf16[128,1024]{1,0:T(8,128)(2,1)}, bf16[128,1024]{1,0:T(8,128)(2,1)S(1)}, u32[]{:S(2)}) copy-start(bf16[128,1024]{1,0:T(8,128)(2,1)S(1)} %collective-permute-done.refs_1_) | copy-start | bytes 786436
  40.4 1.0 %copy-start.1 = (bf16[2,8,16,1024]{3,2,1,0:T(8,128)(2,1)}, bf16[2,8,16,1024]{3,2,1,0:T(8,128)(2,1)S(1)}, u32[]{:S(2)}) copy-start(bf16[2,8,16,1024]{3,2,1,0:T(8,128)(2,1)S(1)} %collective-permute-done.8.refs_10_) | copy-start | bytes 1572868
  41.3 0.8 %copy-start.2 = (bf16[2,8,16,1024]{3,2,1,0:T(8,128)(2,1)}, bf16[2,8,16,1024]{3,2,1,0:T(8,128)(2,1)S(1)}, u32[]{:S(2)}) copy-start(bf16[2,8,16,1024]{3,2,1,0:T(8,128)(2,1)S(1)} %collective-permute-done.9.refs_11_) | copy-start | bytes 1572868

commit v4 on v3

--- a/solution.py
+++ b/solution.py
@@ -73,14 +73,17 @@
 
 
 def cols_kernel(
-    u_left, u_right, s_left, s_right, j_left, j_right, r_top, r_bot, k_top, k_bot,
-    to_left, to_right, small_prev, small_next, *, pairs, tiles, blocks,
+    u_left, u_right, s_left, s_right, j_left, j_right, rotor, to_left, to_right, *, pairs, tiles, blocks
 ):
     even16 = checker(16)
     lane = lax.broadcasted_iota(jnp.int32, (16, LANES), 1)
 
     def block_cols(q, _):
         rows = pl.ds(pl.multiple_of(16 * q, 16), 16)
+        for c in range(tiles):
+            panel = rotor[rows, c * LANES : (c + 1) * LANES]
+            to_left[2 * blocks + q * tiles + c] = panel
+            to_right[2 * blocks + q * tiles + c] = panel
         for refs, out_ref, red_first in (
             ((u_left, s_left, j_left), to_left, False),
             ((u_right, s_right, j_right), to_right, True),
@@ -112,16 +115,6 @@
         return 0
 
     lax.fori_loop(0, blocks, block_cols, 0)
-    for out_ref, near, r_ref, k_ref in (
-        (small_prev, 0, r_top, k_top),
-        (small_next, 2 * blocks - 2, r_bot, k_bot),
-    ):
-        for i in (0, 1):
-            out_ref[i] = to_left[near + i]
-            out_ref[2 + i] = to_right[near + i]
-        for c in range(tiles):
-            out_ref[4 + c] = r_ref[:, c * LANES : (c + 1) * LANES]
-        out_ref[4 + tiles] = f32(k_ref[...]).astype(jnp.bfloat16)
 
 
 def whole_at(shape, index):
@@ -149,87 +142,117 @@
     )(field, field, sigma, sigma, current, current)
 
 
-def pack_cols(field, sigma, current, rotor_cycle, skew):
+def pack_cols(field, sigma, current, rotor_cycle):
     layers, rows, cols = field.shape
     pairs, tiles, blocks = layers // 2, cols // LANES, rows // 16
     shape = (layers, rows, LANES)
-    cols_specs = [whole_at(shape, (0, 0, 0)), whole_at(shape, (0, 0, tiles - 1))]
-    rotor_specs = [whole_at((16, cols), (i, 0)) for i in (0, blocks - 1)]
-    skew_specs = [whole_at((16, LANES), (i, 0)) for i in (0, blocks - 1)]
-    out = [(2 * blocks, 16, LANES)] * 2 + [(tiles + 5, 16, LANES)] * 2
+    col_specs = [whole_at(shape, (0, 0, 0)), whole_at(shape, (0, 0, tiles - 1))]
+    out = (blocks * (tiles + 2), 16, LANES)
     return pl.pallas_call(
         functools.partial(cols_kernel, pairs=pairs, tiles=tiles, blocks=blocks),
         grid=(1,),
-        in_specs=cols_specs * 3 + rotor_specs + skew_specs,
+        in_specs=col_specs * 3 + [whole_at((rows, cols), (0, 0))],
+        out_specs=[whole_at(out, (0,) * 3)] * 2,
+        out_shape=[jax.ShapeDtypeStruct(out, jnp.bfloat16)] * 2,
+        compiler_params=pltpu.CompilerParams(vmem_limit_bytes=VMEM_BYTES),
+        cost_estimate=pl.CostEstimate(flops=0, bytes_accessed=16 << 20, transcendentals=0),
+        name="pack_cols",
+    )(field, field, sigma, sigma, current, current, rotor_cycle)
+
+
+def place_kernel(*refs, slots, rows, tiles):
+    rotor = refs[: slots - 2]
+    skew, from_left, from_right, placed_ref, small_prev, small_next = refs[slots - 2 :]
+    blocks = rows // 16
+    lane16 = lax.broadcasted_iota(jnp.int32, (16, LANES), 1)
+    panels = slots * tiles
+    bits = (panels - 1).bit_length()
+    want = [(panels - tiles - 1 + p) % panels for p in range(tiles + 2)]
+    needs = [set(want)]
+    for bit in range(bits):
+        needs.append(needs[-1] | {(q - (1 << bit)) % panels for q in needs[-1]})
+
+    def rotor_rows(b, _):
+        at = pl.ds(pl.multiple_of(16 * b, 16), 16)
+        turn = skew[at, :]
+
+        def panel(steps, c):
+            if steps in (1, slots - 1):
+                source = from_left if steps == 1 else from_right
+                return source[2 * blocks + b * tiles + c]
+            source = rotor[0] if steps == 0 else rotor[steps - 1]
+            return source[at, c * LANES : (c + 1) * LANES]
+
+        cur = {q: f32(panel(slots - 1 - q // tiles, q % tiles)) for q in sorted(needs[bits])}
+        for bit in reversed(range(bits)):
+            on = ((turn >> bit) & 1) == 1
+            cur = {q: jnp.where(on, cur[(q - (1 << bit)) % panels], cur[q]) for q in sorted(needs[bit])}
+        for p in range(tiles):
+            placed_ref[p, at, :] = cur[want[p + 1]].astype(jnp.bfloat16)
+        side = jnp.where(lane16 < LANES // 2, cur[want[tiles + 1]], cur[want[0]])
+        placed_ref[tiles, at, :] = side.astype(jnp.bfloat16)
+        return 0
+
+    lax.fori_loop(0, rows // 16, rotor_rows, 0)
+    for out_ref, corner, first in (
+        (small_prev, 0, 0),
+        (small_next, 2 * blocks - 2, rows - 16),
+    ):
+        for i in (0, 1):
+            out_ref[i] = from_left[corner + i]
+            out_ref[2 + i] = from_right[corner + i]
+        for c in range(tiles + 1):
+            out_ref[4 + c] = placed_ref[c, first : first + 16, :]
+
+
+def place_cycle(rotor, skew, from_left, from_right):
+    rows, cols = rotor[0].shape
+    tiles = cols // LANES
+    sides = whole_at(from_left.shape, (0, 0, 0))
+    out = [(tiles + 1, rows, LANES)] + [(tiles + 5, 16, LANES)] * 2
+    return pl.pallas_call(
+        functools.partial(place_kernel, slots=len(rotor) + 2, rows=rows, tiles=tiles),
+        grid=(1,),
+        in_specs=[whole_at((rows, cols), (0, 0))] * len(rotor) + [whole_at((rows, LANES), (0, 0)), sides, sides],
         out_specs=[whole_at(x, (0,) * 3) for x in out],
         out_shape=[jax.ShapeDtypeStruct(x, jnp.bfloat16) for x in out],
         compiler_params=pltpu.CompilerParams(vmem_limit_bytes=VMEM_BYTES),
-        cost_estimate=pl.CostEstimate(flops=0, bytes_accessed=16 << 20, transcendentals=0),
-        name="pack_cols",
-    )(field, field, sigma, sigma, current, current, rotor_cycle, rotor_cycle, skew, skew)
-
-
-def relax_kernel(*refs, slots, pairs, rows, tiles):
-    rotor, refs = refs[:slots], refs[slots:]
-    others, refs = refs[: slots - 3], refs[slots - 3 :]
-    (skew, small_prev, small_next, from_left, from_right, from_prev, from_next,
+        cost_estimate=pl.CostEstimate(flops=0, bytes_accessed=4 << 20, transcendentals=0),
+        name="place_cycle",
+    )(*rotor, skew, from_left, from_right)
+
+
+def relax_kernel(placed, small_prev, small_next, from_left, from_right, from_prev, from_next,
      u_ref, s_ref, j_ref, out_ref,
-     red_a, red_b, black_a, black_b, sig_r, sig_b, cur_r, cur_b, side) = refs
+     red_a, red_b, black_a, black_b, sig_r, sig_b, cur_r, cur_b, side, *, pairs, rows, tiles):
     g = pl.program_id(0)
     blocks = rows // 16
     even8 = checker(8)
     even16 = checker(16)
     lane = lax.broadcasted_iota(jnp.int32, (8, LANES), 1)
-    lane16 = lax.broadcasted_iota(jnp.int32, (16, LANES), 1)
     lane_first = lane == 0
     lane_last = lane == LANES - 1
 
     @pl.when(g == 0)
     def prologue():
-        panels = slots * tiles
-        bits = (panels - 1).bit_length()
-        want = [(panels - tiles - 1 + p) % panels for p in range(tiles + 2)]
-        needs = [set(want)]
-        for bit in range(bits):
-            needs.append(needs[-1] | {(q - (1 << bit)) % panels for q in needs[-1]})
-
-        def place(panel, turn, spots):
-            cur = {q: f32(panel(slots - 1 - q // tiles, q % tiles)) for q in sorted(needs[bits])}
-            for bit in reversed(range(bits)):
-                on = ((turn >> bit) & 1) == 1
-                cur = {q: jnp.where(on, cur[(q - (1 << bit)) % panels], cur[q]) for q in sorted(needs[bit])}
-            placed = [cur[want[p + 1]] for p in range(tiles)]
-            placed.append(jnp.where(lane16 < LANES // 2, cur[want[tiles + 1]], cur[want[0]]))
+        def fill(value, c, spots):
             zero = jnp.zeros((8, LANES), jnp.float32)
             for buf in (red_a, red_b, black_a, black_b):
-                for c in range(tiles + 1):
-                    for half, to in spots:
-                        buf[0, c, to, :] = placed[c][8 * half : 8 * half + 8]
-                        buf[pairs + 1, c, to, :] = zero
-
-        def rotor_rows(b, _):
+                for half, to in spots:
+                    buf[0, c, to, :] = value[8 * half : 8 * half + 8]
+                    buf[pairs + 1, c, to, :] = zero
+
+        def placed_rows(b, _):
             at = pl.ds(pl.multiple_of(16 * b, 16), 16)
             spots = [(half, pl.ds(pl.multiple_of(16 * b + EDGE + 8 * half, 8), 8)) for half in (0, 1)]
-            place(lambda r, c: rotor[r][at, c * LANES : (c + 1) * LANES], skew[at, :], spots)
+            for c in range(tiles + 1):
+                fill(f32(placed[c, at, :]), c, spots)
             return 0
 
-        lax.fori_loop(0, blocks, rotor_rows, 0)
-        base = 2 * blocks + 4
-        for small, first, spot in (
-            (small_prev, 0, (1, pl.ds(0, 8))),
-            (small_next, tiles, (0, pl.ds(EDGE + rows, 8))),
-        ):
-
-            def edge_panel(r, c, small=small, first=first):
-                if r == 0:
-                    return small[4 + c]
-                if r == 1:
-                    return from_left[base + first + c]
-                if r == slots - 1:
-                    return from_right[base + first + c]
-                return others[r - 2][first + c]
-
-            place(edge_panel, f32(small[4 + tiles]).astype(jnp.int32), [spot])
+        lax.fori_loop(0, blocks, placed_rows, 0)
+        for c in range(tiles + 1):
+            fill(f32(small_prev[4 + c]), c, [(1, pl.ds(0, 8))])
+            fill(f32(small_next[4 + c]), c, [(0, pl.ds(EDGE + rows, 8))])
 
         left_slot = (lane & 7) < 4
 
@@ -244,9 +267,11 @@
                 side[0, item, q] = jnp.where(left_slot, a, b) * scale
                 side[1, item, q] = jnp.where(left_slot, b, a) * scale
 
-        for q in range(blocks + 2):
+        for q in range(blocks):
             pick = slice(2 * q, 2 * q + 2)
             decode(q, from_left[pick], from_right[pick])
+        decode(blocks, small_prev[0:2], small_prev[2:4])
+        decode(blocks + 1, small_next[0:2], small_next[2:4])
 
     @pl.when(g < pairs)
     def load():
@@ -348,9 +373,9 @@
             half_step(g - lag, colour, own, other, sig, cur, *where, write)
 
 
-def relax(rotor, others, skew, small_prev, small_next, from_left, from_right, from_prev, from_next, field, sigma, current):
+def relax(placed, small_prev, small_next, from_left, from_right, from_prev, from_next, field, sigma, current):
     layers, rows, cols = field.shape
-    pairs, tiles, slots = layers // 2, cols // LANES, len(rotor)
+    pairs, tiles = layers // 2, cols // LANES
     ext = rows + 2 * EDGE
 
     def whole(array):
@@ -362,19 +387,20 @@
 
     halo = pl.BlockSpec((2, 1, 16, cols), lambda g: (0, coming(g), 0, 0))
     block = pl.BlockSpec((2, rows, cols), lambda g: (coming(g), 0, 0))
-    fixed = list(rotor) + list(others) + [skew, small_prev, small_next, from_left, from_right]
+    fixed = [placed, small_prev, small_next]
+    side = pl.BlockSpec((rows // 8, 16, LANES), lambda g: (0, 0, 0))
     state = pltpu.VMEM((pairs + 2, tiles + 1, ext, LANES), jnp.float32)
     coef = pltpu.VMEM((pairs, tiles + 1, ext, LANES), jnp.float32)
     return pl.pallas_call(
-        functools.partial(relax_kernel, slots=slots, pairs=pairs, rows=rows, tiles=tiles),
+        functools.partial(relax_kernel, pairs=pairs, rows=rows, tiles=tiles),
         grid=(pairs + LAG,),
-        in_specs=[whole(a) for a in fixed] + [halo, halo, block, block, block],
+        in_specs=[whole(a) for a in fixed] + [side, side, halo, halo, block, block, block],
         out_specs=pl.BlockSpec((2, rows, cols), lambda g: (jnp.maximum(g - LAG, 0), 0, 0)),
         out_shape=jax.ShapeDtypeStruct(field.shape, jnp.float32),
         scratch_shapes=[state] * 4 + [coef] * 4 + [pltpu.VMEM((2, 3, rows // 16 + 2, 8, LANES), jnp.float32)],
         compiler_params=pltpu.CompilerParams(vmem_limit_bytes=VMEM_BYTES),
         name="relax",
-    )(*fixed, from_prev, from_next, field, sigma, current)
+    )(*fixed, from_left, from_right, from_prev, from_next, field, sigma, current)
 
 
 def moved(value, axis, steps):
@@ -383,25 +409,17 @@
 
 
 def local(field, sigma, current, rotor_cycle, skew_list):
-    rows, cols = field.shape[1:]
-    tiles = cols // LANES
-    count = lax.axis_size("az")
+    rows = field.shape[1]
     skew = jnp.broadcast_to(skew_list[:, None], (rows, LANES))
-    rotor = [rotor_cycle] + [moved(rotor_cycle, "az", s) for s in range(1, count)]
+    rotor = [rotor_cycle] + [moved(rotor_cycle, "az", s) for s in range(2, lax.axis_size("az") - 1)]
+    to_left, to_right = pack_cols(field, sigma, current, rotor_cycle)
+    from_left, from_right = moved(to_right, "az", 1), moved(to_left, "az", -1)
     to_prev, to_next = pack_rows(field, sigma, current)
-    from_prev = moved(to_next, "ta", 1)
-    from_next = moved(to_prev, "ta", -1)
-    to_left, to_right, small_to_prev, small_to_next = pack_cols(field, sigma, current, rotor_cycle, skew)
-    small_prev = moved(small_to_next, "ta", 1)
-    small_next = moved(small_to_prev, "ta", -1)
-    rotor_edge = [small_prev[4 : 4 + tiles], small_next[4 : 4 + tiles]]
-    from_right = moved(jnp.concatenate([to_left, small_prev[:2], small_next[:2]] + rotor_edge), "az", -1)
-    from_left = moved(jnp.concatenate([to_right, small_prev[2:4], small_next[2:4]] + rotor_edge), "az", 1)
-    rotor_edge = jnp.concatenate(rotor_edge)
-    others = [moved(rotor_edge, "az", s) for s in range(2, count - 1)]
+    from_prev, from_next = moved(to_next, "ta", 1), moved(to_prev, "ta", -1)
+    placed, small_to_prev, small_to_next = place_cycle(rotor, skew, from_left, from_right)
+    small_prev, small_next = moved(small_to_next, "ta", 1), moved(small_to_prev, "ta", -1)
     return relax(
-        rotor, others, skew, small_prev, small_next, from_left, from_right, from_prev, from_next,
-        field, sigma, current,
+        placed, small_prev, small_next, from_left, from_right, from_prev, from_next, field, sigma, current
     )
 
 

time: 72.7 us -> 69 us (0.949)
  starting transfers between devices: 19.2 us -> 13 us
  Pallas kernels: 38.3 us -> 40.3 us
  waiting for transfers between devices: 11.7 us -> 13.7 us
  local copies, waits for them, and re-layouts: 3.16 us -> 1.76 us
    ppermute x10 -> x7, starting transfers between devices: 19.2 us -> 13 us  [moved(): lax.ppermute(value, axis, [(i, (i + steps) % count) for i in range(count)])]
    ppermute x10 -> x7, waiting for transfers between devices: 11.7 us -> 13.7 us  [moved(): lax.ppermute(value, axis, [(i, (i + steps) % count) for i in range(count)])]
    pallas_call x1 -> x2, Pallas kernels: 30.4 us -> 32.2 us  [the longest x1 29.8 us: relax(): pl.pallas_call(functools.partial(relax_kernel, pairs=pairs, rows=rows, ti...]
    unnamed x30 -> x18, local copies, waits for them, and re-layouts: 1.79 us -> 1 us
  transfers between devices with their start and end apart: 10 -> 7, of which waited for: 3 -> 3; matrix products, arithmetic and copies ran while one was open for 0% -> 1% of each run, Pallas kernels for 5% -> 10%
where the time goes in v4:
time: 69 us; the launch traced here: 68.8 us
  Pallas kernels  40.3 us (58%)
  waiting for transfers between devices  13.7 us (20%)
  starting transfers between devices  13 us (19%)
  local copies, waits for them, and re-layouts  1.76 us (3%)
    pallas_call x1, Pallas kernels, relax(): pl.pallas_call(functools.partial(relax_kernel, pairs=pairs, rows=rows, ti...  29.8 us
    ppermute x7, waiting for transfers between devices, moved(): lax.ppermute(value, axis, [(i, (i + steps) % count) for i in range(count)])  13.7 us
    ppermute x7, starting transfers between devices, moved(): lax.ppermute(value, axis, [(i, (i + steps) % count) for i in range(count)])  13 us
    pallas_call x1, Pallas kernels, pack_cols(): pl.pallas_call(functools.partial(cols_kernel, pairs=pairs, tiles=tiles, b...  4.79 us
    pallas_call x1, Pallas kernels, pack_rows(): pl.pallas_call(functools.partial(rows_kernel, pairs=pairs, tiles=tiles),...  3.33 us
    pallas_call x1, Pallas kernels, place_cycle(): pl.pallas_call(functools.partial(place_kernel, slots=len(rotor) + 2, rows...  2.4 us
  transfers between devices with their start and end apart: 7, of which 3 were waited for; matrix products, arithmetic and copies ran while one was open for 1% of the time, Pallas kernels for 10%

profile of v4, /device:TPU:0, one launch (start us, length us, event | category | flops | bytes accessed | tf_op | source)
XLA Modules:
  0.0 68.8 jit_solution(4605283114784371422)
XLA Ops:
  0.0 3.3 %pack_rows.1 = (bf16[2,8,16,1024]{3,2,1,0:T(8,128)(2,1)}, bf16[2,8,16,1024]{3,2,1,0:T(8,128)(2,1)}) custom-call(f32[16,128,1024]{2,1,0:T(8,128)} %u_ref.1, f32[16,128,1024]{2,1,0:T(8,128)} %u_ref.1, bf16[16,128,1024]{2,1,0:T(8,128)(2,1)} %s_ref.1, bf16[16,128,1024]{2,1,0:T(8,128)(2,1)} %s_ref.1, bf16[16,128,1024]{2,1,0:T(8,128)(2,1)} %j_ref.1, ...), custom_call_target="tpu_custom_call" | custom-call | bytes 12582912 | tf_op jit(solution)/shard_map/pack_rows/pallas_call | solution.py:133
  3.3 0.5 collective-permute-start.5
  3.8 0.0 copy-start.2
  3.8 0.0 copy-start.8
  3.8 4.1 %collective-permute-start.6 = (bf16[2,8,16,1024]{3,2,1,0:T(8,128)(2,1)}, bf16[2,8,16,1024]{3,2,1,0:T(8,128)(2,1)S(1)}, u32[]{:S(2)}, u32[]{:S(2)}) collective-permute-start(bf16[2,8,16,1024]{3,2,1,0:T(8,128)(2,1)} %get-tuple-element.18), channel_id=1, source_target_pairs={{0,7},{1,0},{2,1},{3,2},{4,3},{5,4},{6,5},{7,6},{8,15},{9,8},{10,9... | collective-permute-start | bytes 1572872 | tf_op jit(solution)/shard_map/ppermute | solution.py:408
  7.9 4.8 %pack_cols.1 = (bf16[80,16,128]{2,1,0:T(8,128)(2,1)}, bf16[80,16,128]{2,1,0:T(8,128)(2,1)}) custom-call(f32[16,128,1024]{2,1,0:T(8,128)} %u_ref.1, f32[16,128,1024]{2,1,0:T(8,128)} %u_ref.1, bf16[16,128,1024]{2,1,0:T(8,128)(2,1)} %s_ref.1, bf16[16,128,1024]{2,1,0:T(8,128)(2,1)} %s_ref.1, bf16[16,128,1024]{2,1,0:T(8,128)(2,1)} %j_ref.1, ...), custom_call_target="tpu_custom_call" | custom-call | bytes 16777216 | tf_op jit(solution)/shard_map/pack_cols/pallas_call | solution.py:151
  12.7 1.9 %collective-permute-start.1 = (bf16[80,16,128]{2,1,0:T(8,128)(2,1)}, bf16[80,16,128]{2,1,0:T(8,128)(2,1)S(1)}, u32[]{:S(2)}, u32[]{:S(2)}) collective-permute-start(bf16[80,16,128]{2,1,0:T(8,128)(2,1)} %get-tuple-element.12), channel_id=1, source_target_pairs={{0,8},{8,16},{16,24},{24,0},{1,9},{9,17},{17,25},{25,1},{2,10},{10... | collective-permute-start | bytes 983048 | tf_op jit(solution)/shard_map/ppermute | solution.py:408
  14.6 1.0 %collective-permute-start.2 = (bf16[80,16,128]{2,1,0:T(8,128)(2,1)}, bf16[80,16,128]{2,1,0:T(8,128)(2,1)S(1)}, u32[]{:S(2)}, u32[]{:S(2)}) collective-permute-start(bf16[80,16,128]{2,1,0:T(8,128)(2,1)} %get-tuple-element.13), channel_id=1, source_target_pairs={{0,24},{8,0},{16,8},{24,16},{1,25},{9,1},{17,9},{25,17},{2,26},{10... | collective-permute-start | bytes 983048 | tf_op jit(solution)/shard_map/ppermute | solution.py:408
  15.6 0.0 copy-done.2
  15.6 2.0 %collective-permute-start = (bf16[128,1024]{1,0:T(8,128)(2,1)S(1)}, bf16[128,1024]{1,0:T(8,128)(2,1)S(1)}, u32[]{:S(2)}, u32[]{:S(2)}) collective-permute-start(bf16[128,1024]{1,0:T(8,128)(2,1)S(1)} %copy-done.2), channel_id=1, source_target_pairs={{0,16},{8,24},{16,0},{24,8},{1,17},{9,25},{17,1},{25,9},{2,18},{10... | collective-permute-start | bytes 786440 | tf_op jit(solution)/shard_map/ppermute | solution.py:408
  17.6 10.1 %collective-permute-done.refs_1_ = bf16[128,1024]{1,0:T(8,128)(2,1)S(1)} collective-permute-done((bf16[128,1024]{1,0:T(8,128)(2,1)S(1)}, bf16[128,1024]{1,0:T(8,128)(2,1)S(1)}, u32[]{:S(2)}, u32[]{:S(2)}) %collective-permute-start) | collective-permute-done | bytes 262176 | tf_op jit(solution)/shard_map/ppermute | solution.py:408
  27.7 0.0 copy-start.5
  27.7 0.0 collective-permute-done.1.refs_3_.from_left
  27.7 0.0 copy-start
  27.7 1.5 %collective-permute-done.2.refs_4_.from_right = bf16[80,16,128]{2,1,0:T(8,128)(2,1)S(1)} collective-permute-done((bf16[80,16,128]{2,1,0:T(8,128)(2,1)}, bf16[80,16,128]{2,1,0:T(8,128)(2,1)S(1)}, u32[]{:S(2)}, u32[]{:S(2)}) %collective-permute-start.2) | collective-permute-done | bytes 327712 | tf_op jit(solution)/shard_map/ppermute | solution.py:408
  29.2 0.0 copy-done.8
  29.2 0.0 copy-start.1
  29.2 0.8 %broadcast_in_dim.2.refs_2_ = s32[128,128]{1,0:T(8,128)} broadcast(s32[128]{0:T(128)S(1)} %copy-done.8), dimensions={0} | broadcast | bytes 66048 | tf_op jit(solution)/shard_map/broadcast_in_dim | solution.py:413
  29.9 0.0 copy-done.5
  29.9 0.0 copy-done
  29.9 0.0 copy-done.1
  29.9 2.4 %place_cycle.1 = (bf16[9,128,128]{2,1,0:T(8,128)(2,1)}, bf16[13,16,128]{2,1,0:T(8,128)(2,1)}, bf16[13,16,128]{2,1,0:T(8,128)(2,1)}) custom-call(bf16[128,1024]{1,0:T(8,128)(2,1)} %refs_0_.1, bf16[128,1024]{1,0:T(8,128)(2,1)} %copy-done.5, s32[128,128]{1,0:T(8,128)} %broadcast_in_dim.2.refs_2_, bf16[80,16,128]{2,1,0:T(8,128)(2,1)} %copy-done, ...), custom_call_target="tpu_custom_call" | custom-call | bytes 4194304 | tf_op jit(solution)/shard_map/place_cycle/pallas_call | solution.py:213
  32.3 0.0 collective-permute-start.3
  32.3 3.5 %collective-permute-start.4 = (bf16[13,16,128]{2,1,0:T(8,128)(2,1)}, bf16[13,16,128]{2,1,0:T(8,128)(2,1)S(1)}, u32[]{:S(2)}, u32[]{:S(2)}) collective-permute-start(bf16[13,16,128]{2,1,0:T(8,128)(2,1)} %get-tuple-element.16), channel_id=1, source_target_pairs={{0,7},{1,0},{2,1},{3,2},{4,3},{5,4},{6,5},{7,6},{8,15},{9,8},{10,9... | collective-permute-start | bytes 159752 | tf_op jit(solution)/shard_map/ppermute | solution.py:408
  35.9 2.1 %collective-permute-done.3.small_prev = bf16[13,16,128]{2,1,0:T(8,128)(2,1)S(1)} collective-permute-done((bf16[13,16,128]{2,1,0:T(8,128)(2,1)}, bf16[13,16,128]{2,1,0:T(8,128)(2,1)S(1)}, u32[]{:S(2)}, u32[]{:S(2)}) %collective-permute-start.3) | collective-permute-done | bytes 53280 | tf_op jit(solution)/shard_map/ppermute | solution.py:408
  38.0 0.0 copy-start.6
  38.0 0.0 collective-permute-done.4.small_next
  38.0 0.0 copy-start.7
  38.0 0.0 collective-permute-done.5.from_prev
  38.0 0.0 copy-start.3
  38.0 0.0 collective-permute-done.6.from_next
  38.0 0.0 copy-start.4
  38.0 0.6 copy-done.6
  38.6 0.0 copy-done.7
  38.6 0.2 copy-done.3
  38.8 0.2 copy-done.4
  39.0 29.8 %relax.1 = f32[16,128,1024]{2,1,0:T(8,128)} custom-call(bf16[9,128,128]{2,1,0:T(8,128)(2,1)} %get-tuple-element.14.placed, bf16[13,16,128]{2,1,0:T(8,128)(2,1)} %copy-done.6, bf16[13,16,128]{2,1,0:T(8,128)(2,1)} %copy-done.7, bf16[80,16,128]{2,1,0:T(8,128)(2,1)} %copy-done, bf16[80,16,128]{2,1,0:T(8,128)(2,1)} %copy-done.1, ...), custom_call_target="tpu_custom_call" | custom-call | tf_op jit(solution)/shard_map/relax/pallas_call | solution.py:394
Async XLA Ops:
  3.3 34.7 %collective-permute-start.5 = (bf16[2,8,16,1024]{3,2,1,0:T(8,128)(2,1)}, bf16[2,8,16,1024]{3,2,1,0:T(8,128)(2,1)S(1)}, u32[]{:S(2)}, u32[]{:S(2)}) collective-permute-start(bf16[2,8,16,1024]{3,2,1,0:T(8,128)(2,1)} %get-tuple-element.17), channel_id=1, source_target_pairs={{0,1},{1,2},{2,3},{3,4},{4,5},{5,6},{6,7},{7,0},{8,9},{9,10},{10,1... | collective-permute-start | bytes 1572872 | tf_op jit(solution)/shard_map/ppermute | solution.py:408
  3.8 11.8 %copy-start.2 = (bf16[128,1024]{1,0:T(8,128)(2,1)S(1)}, bf16[128,1024]{1,0:T(8,128)(2,1)}, u32[]{:S(2)}) copy-start(bf16[128,1024]{1,0:T(8,128)(2,1)} %refs_0_.1) | copy-start | bytes 786436
  3.8 25.4 %copy-start.8 = (s32[128]{0:T(128)S(1)}, s32[128]{0:T(128)}, u32[]{:S(2)}) copy-start(s32[128]{0:T(128)} %param.9) | copy-start | bytes 1540
  3.8 34.2 %collective-permute-start.6 = (bf16[2,8,16,1024]{3,2,1,0:T(8,128)(2,1)}, bf16[2,8,16,1024]{3,2,1,0:T(8,128)(2,1)S(1)}, u32[]{:S(2)}, u32[]{:S(2)}) collective-permute-start(bf16[2,8,16,1024]{3,2,1,0:T(8,128)(2,1)} %get-tuple-element.18), channel_id=1, source_target_pairs={{0,7},{1,0},{2,1},{3,2},{4,3},{5,4},{6,5},{7,6},{8,15},{9,8},{10,9... | collective-permute-start | bytes 1572872 | tf_op jit(solution)/shard_map/ppermute | solution.py:408
  12.7 15.0 %collective-permute-start.1 = (bf16[80,16,128]{2,1,0:T(8,128)(2,1)}, bf16[80,16,128]{2,1,0:T(8,128)(2,1)S(1)}, u32[]{:S(2)}, u32[]{:S(2)}) collective-permute-start(bf16[80,16,128]{2,1,0:T(8,128)(2,1)} %get-tuple-element.12), channel_id=1, source_target_pairs={{0,8},{8,16},{16,24},{24,0},{1,9},{9,17},{17,25},{25,1},{2,10},{10... | collective-permute-start | bytes 983048 | tf_op jit(solution)/shard_map/ppermute | solution.py:408
  14.6 14.5 %collective-permute-start.2 = (bf16[80,16,128]{2,1,0:T(8,128)(2,1)}, bf16[80,16,128]{2,1,0:T(8,128)(2,1)S(1)}, u32[]{:S(2)}, u32[]{:S(2)}) collective-permute-start(bf16[80,16,128]{2,1,0:T(8,128)(2,1)} %get-tuple-element.13), channel_id=1, source_target_pairs={{0,24},{8,0},{16,8},{24,16},{1,25},{9,1},{17,9},{25,17},{2,26},{10... | collective-permute-start | bytes 983048 | tf_op jit(solution)/shard_map/ppermute | solution.py:408
  15.6 12.0 %collective-permute-start = (bf16[128,1024]{1,0:T(8,128)(2,1)S(1)}, bf16[128,1024]{1,0:T(8,128)(2,1)S(1)}, u32[]{:S(2)}, u32[]{:S(2)}) collective-permute-start(bf16[128,1024]{1,0:T(8,128)(2,1)S(1)} %copy-done.2), channel_id=1, source_target_pairs={{0,16},{8,24},{16,0},{24,8},{1,17},{9,25},{17,1},{25,9},{2,18},{10... | collective-permute-start | bytes 786440 | tf_op jit(solution)/shard_map/ppermute | solution.py:408
  27.7 2.3 %copy-start.5 = (bf16[128,1024]{1,0:T(8,128)(2,1)}, bf16[128,1024]{1,0:T(8,128)(2,1)S(1)}, u32[]{:S(2)}) copy-start(bf16[128,1024]{1,0:T(8,128)(2,1)S(1)} %collective-permute-done.refs_1_) | copy-start | bytes 786436
  27.7 2.3 %copy-start = (bf16[80,16,128]{2,1,0:T(8,128)(2,1)}, bf16[80,16,128]{2,1,0:T(8,128)(2,1)S(1)}, u32[]{:S(2)}) copy-start(bf16[80,16,128]{2,1,0:T(8,128)(2,1)S(1)} %collective-permute-done.1.refs_3_.from_left) | copy-start | bytes 983044
  29.2 0.8 %copy-start.1 = (bf16[80,16,128]{2,1,0:T(8,128)(2,1)}, bf16[80,16,128]{2,1,0:T(8,128)(2,1)S(1)}, u32[]{:S(2)}) copy-start(bf16[80,16,128]{2,1,0:T(8,128)(2,1)S(1)} %collective-permute-done.2.refs_4_.from_right) | copy-start | bytes 983044
  32.3 5.6 %collective-permute-start.3 = (bf16[13,16,128]{2,1,0:T(8,128)(2,1)}, bf16[13,16,128]{2,1,0:T(8,128)(2,1)S(1)}, u32[]{:S(2)}, u32[]{:S(2)}) collective-permute-start(bf16[13,16,128]{2,1,0:T(8,128)(2,1)} %get-tuple-element.15), channel_id=1, source_target_pairs={{0,1},{1,2},{2,3},{3,4},{4,5},{5,6},{6,7},{7,0},{8,9},{9,10},{10,1... | collective-permute-start | bytes 159752 | tf_op jit(solution)/shard_map/ppermute | solution.py:408
  32.3 5.6 %collective-permute-start.4 = (bf16[13,16,128]{2,1,0:T(8,128)(2,1)}, bf16[13,16,128]{2,1,0:T(8,128)(2,1)S(1)}, u32[]{:S(2)}, u32[]{:S(2)}) collective-permute-start(bf16[13,16,128]{2,1,0:T(8,128)(2,1)} %get-tuple-element.16), channel_id=1, source_target_pairs={{0,7},{1,0},{2,1},{3,2},{4,3},{5,4},{6,5},{7,6},{8,15},{9,8},{10,9... | collective-permute-start | bytes 159752 | tf_op jit(solution)/shard_map/ppermute | solution.py:408
  38.0 0.6 copy-start.6
  38.0 0.6 copy-start.7
  38.0 0.8 %copy-start.3 = (bf16[2,8,16,1024]{3,2,1,0:T(8,128)(2,1)}, bf16[2,8,16,1024]{3,2,1,0:T(8,128)(2,1)S(1)}, u32[]{:S(2)}) copy-start(bf16[2,8,16,1024]{3,2,1,0:T(8,128)(2,1)S(1)} %collective-permute-done.5.from_prev) | copy-start | bytes 1572868
  38.0 1.0 %copy-start.4 = (bf16[2,8,16,1024]{3,2,1,0:T(8,128)(2,1)}, bf16[2,8,16,1024]{3,2,1,0:T(8,128)(2,1)S(1)}, u32[]{:S(2)}) copy-start(bf16[2,8,16,1024]{3,2,1,0:T(8,128)(2,1)S(1)} %collective-permute-done.6.from_next) | copy-start | bytes 1572868

commit v5 on v4

--- a/solution.py
+++ b/solution.py
@@ -10,8 +10,6 @@
 LANES = 128
 EDGE = 8
 LAG = 4
-UNROLL = 6
-SPANS = 3
 VMEM_BYTES = 60 * 1024 * 1024
 
 
@@ -30,7 +28,7 @@
     return high, value - high
 
 
-def rows_kernel(u_top, u_bot, s_top, s_bot, j_top, j_bot, to_prev, to_next, *, pairs, tiles):
+def rows_kernel(u_top, u_bot, s_top, s_bot, j_top, j_bot, after, to_prev, to_next, *, pairs, tiles):
     even8 = checker(8)
     sub = lax.broadcasted_iota(jnp.int32, (8, LANES), 0)
     field_rows = sub < 5
@@ -76,22 +74,21 @@
     u_left, u_right, s_left, s_right, j_left, j_right, rotor, to_left, to_right, *, pairs, tiles, blocks
 ):
     even16 = checker(16)
-    lane = lax.broadcasted_iota(jnp.int32, (16, LANES), 1)
-
-    def block_cols(q, _):
-        rows = pl.ds(pl.multiple_of(16 * q, 16), 16)
+    slot = lax.broadcasted_iota(jnp.int32, (8, LANES), 1) // 4
+    slots = LANES // 4
+    for q in range(blocks):
+        rows = slice(16 * q, 16 * q + 16)
         for c in range(tiles):
             panel = rotor[rows, c * LANES : (c + 1) * LANES]
-            to_left[2 * blocks + q * tiles + c] = panel
-            to_right[2 * blocks + q * tiles + c] = panel
-        for refs, out_ref, red_first in (
-            ((u_left, s_left, j_left), to_left, False),
-            ((u_right, s_right, j_right), to_right, True),
+            to_left[q, 2 + c] = panel
+            to_right[q, 2 + c] = panel
+        for refs, out_ref, near_at, far_at in (
+            ((u_left, s_left, j_left), to_left, 1, 2),
+            ((u_right, s_right, j_right), to_right, 0, 1),
         ):
             packed = []
             for ref in refs:
-                acc = [jnp.zeros((8, LANES), jnp.float32)]
-                total = acc[0]
+                total = jnp.zeros((8, LANES), jnp.float32)
                 for m in range(pairs):
                     first = f32(ref[2 * m, rows, :])
                     second = f32(ref[2 * m + 1, rows, :])
@@ -101,27 +98,19 @@
                         g = m + pairs * w
                         near = pltpu.roll(red[8 * w : 8 * w + 8], (8 * g + 4) % LANES, 1)
                         far = pltpu.roll(black[8 * w : 8 * w + 8], (8 * g + 8) % LANES, 1)
-                        if red_first:
-                            near_slot, far_slot = 8 * g, 8 * g + 4
-                        else:
-                            near_slot, far_slot = 8 * g + 4, (8 * g + 8) % LANES
-                        l8 = lane[:8]
-                        total = jnp.where((l8 >= near_slot) & (l8 < near_slot + 4), near, total)
-                        total = jnp.where((l8 >= far_slot) & (l8 < far_slot + 4), far, total)
+                        total = jnp.where(slot == (2 * g + near_at) % slots, near, total)
+                        total = jnp.where(slot == (2 * g + far_at) % slots, far, total)
                 packed.append(total)
             high, low = split_high_low(packed[0])
-            out_ref[2 * q] = jnp.concatenate([high, low], 0).astype(jnp.bfloat16)
-            out_ref[2 * q + 1] = jnp.concatenate([packed[1], packed[2]], 0).astype(jnp.bfloat16)
-        return 0
-
-    lax.fori_loop(0, blocks, block_cols, 0)
+            out_ref[q, 0] = jnp.concatenate([high, low], 0).astype(jnp.bfloat16)
+            out_ref[q, 1] = jnp.concatenate([packed[1], packed[2]], 0).astype(jnp.bfloat16)
 
 
 def whole_at(shape, index):
     return pl.BlockSpec(shape, lambda i: index)
 
 
-def pack_rows(field, sigma, current):
+def pack_rows(field, sigma, current, after):
     layers, rows, cols = field.shape
     pairs, tiles = layers // 2, cols // LANES
 
@@ -133,93 +122,125 @@
     return pl.pallas_call(
         functools.partial(rows_kernel, pairs=pairs, tiles=tiles),
         grid=(1,),
-        in_specs=row_specs(8) + row_specs(16) * 2,
+        in_specs=row_specs(8) + row_specs(16) * 2 + [pl.BlockSpec(memory_space=pl.ANY)],
         out_specs=[whole_at(shape, (0,) * 4)] * 2,
         out_shape=[jax.ShapeDtypeStruct(shape, jnp.bfloat16)] * 2,
         compiler_params=pltpu.CompilerParams(vmem_limit_bytes=VMEM_BYTES),
         cost_estimate=pl.CostEstimate(flops=0, bytes_accessed=12 << 20, transcendentals=0),
         name="pack_rows",
-    )(field, field, sigma, sigma, current, current)
+    )(field, field, sigma, sigma, current, current, after)
 
 
 def pack_cols(field, sigma, current, rotor_cycle):
     layers, rows, cols = field.shape
     pairs, tiles, blocks = layers // 2, cols // LANES, rows // 16
-    shape = (layers, rows, LANES)
-    col_specs = [whole_at(shape, (0, 0, 0)), whole_at(shape, (0, 0, tiles - 1))]
-    out = (blocks * (tiles + 2), 16, LANES)
+    part = 2
+    shape = (layers, 16 * part, LANES)
+    col_specs = [pl.BlockSpec(shape, lambda i: (0, i, 0)), pl.BlockSpec(shape, lambda i: (0, i, tiles - 1))]
+    out_spec = pl.BlockSpec((part, tiles + 2, 16, LANES), lambda i: (i, 0, 0, 0))
     return pl.pallas_call(
-        functools.partial(cols_kernel, pairs=pairs, tiles=tiles, blocks=blocks),
-        grid=(1,),
-        in_specs=col_specs * 3 + [whole_at((rows, cols), (0, 0))],
-        out_specs=[whole_at(out, (0,) * 3)] * 2,
-        out_shape=[jax.ShapeDtypeStruct(out, jnp.bfloat16)] * 2,
+        functools.partial(cols_kernel, pairs=pairs, tiles=tiles, blocks=part),
+        grid=(blocks // part,),
+        in_specs=col_specs * 3 + [pl.BlockSpec((16 * part, cols), lambda i: (i, 0))],
+        out_specs=[out_spec] * 2,
+        out_shape=[jax.ShapeDtypeStruct((blocks, tiles + 2, 16, LANES), jnp.bfloat16)] * 2,
         compiler_params=pltpu.CompilerParams(vmem_limit_bytes=VMEM_BYTES),
         cost_estimate=pl.CostEstimate(flops=0, bytes_accessed=16 << 20, transcendentals=0),
         name="pack_cols",
     )(field, field, sigma, sigma, current, current, rotor_cycle)
 
 
-def place_kernel(*refs, slots, rows, tiles):
-    rotor = refs[: slots - 2]
-    skew, from_left, from_right, placed_ref, small_prev, small_next = refs[slots - 2 :]
-    blocks = rows // 16
+def place_block(row, skew, rotor, from_left, from_right, at, slots, tiles):
     lane16 = lax.broadcasted_iota(jnp.int32, (16, LANES), 1)
+    sub16 = lax.broadcasted_iota(jnp.int32, (16, LANES), 0)
     panels = slots * tiles
     bits = (panels - 1).bit_length()
     want = [(panels - tiles - 1 + p) % panels for p in range(tiles + 2)]
     needs = [set(want)]
     for bit in range(bits):
         needs.append(needs[-1] | {(q - (1 << bit)) % panels for q in needs[-1]})
+    turn = jnp.zeros((16, LANES), jnp.int32)
+    for i in range(16):
+        turn = jnp.where(sub16 == i, skew[row + i], turn)
+
+    def panel(steps, c):
+        if steps in (1, slots - 1):
+            return (from_left if steps == 1 else from_right)[at, 2 + c]
+        source = rotor[0] if steps == 0 else rotor[steps - 1]
+        return source[pl.ds(pl.multiple_of(16 * at, 16), 16), c * LANES : (c + 1) * LANES]
+
+    cur = {q: f32(panel(slots - 1 - q // tiles, q % tiles)) for q in sorted(needs[bits])}
+    for bit in reversed(range(bits)):
+        on = ((turn >> bit) & 1) == 1
+        cur = {q: jnp.where(on, cur[(q - (1 << bit)) % panels], cur[q]) for q in sorted(needs[bit])}
+    placed = [cur[want[p + 1]] for p in range(tiles)]
+    placed.append(jnp.where(lane16 < LANES // 2, cur[want[tiles + 1]], cur[want[0]]))
+    return [x.astype(jnp.bfloat16) for x in placed]
+
+
+def place_edges_kernel(skew, *refs, slots, rows, tiles):
+    near, far, outs = refs[:slots], refs[slots : 2 * slots], refs[2 * slots :]
+    for out_ref, ins, row in ((outs[0], near, 0), (outs[1], far, rows - 16)):
+        from_left, from_right = ins[slots - 2 :]
+        for i in (0, 1):
+            out_ref[i] = from_left[0, i]
+            out_ref[2 + i] = from_right[0, i]
+        for c, value in enumerate(place_block(row, skew, ins[: slots - 2], from_left, from_right, 0, slots, tiles)):
+            out_ref[4 + c] = value
+
+
+def place_edges(rotor, skew_list, from_left, from_right):
+    rows, cols = rotor[0].shape
+    tiles, slots, blocks = cols // LANES, len(rotor) + 2, rows // 16
+
+    def specs(i):
+        side = whole_at((1, tiles + 2, 16, LANES), (i, 0, 0, 0))
+        return [whole_at((16, cols), (i, 0))] * len(rotor) + [side, side]
+
+    out = (tiles + 5, 16, LANES)
+    ins = [*rotor, from_left, from_right]
+    return pl.pallas_call(
+        functools.partial(place_edges_kernel, slots=slots, rows=rows, tiles=tiles),
+        grid=(1,),
+        in_specs=[pl.BlockSpec(memory_space=pltpu.SMEM)] + specs(0) + specs(blocks - 1),
+        out_specs=[whole_at(out, (0,) * 3)] * 2,
+        out_shape=[jax.ShapeDtypeStruct(out, jnp.bfloat16)] * 2,
+        compiler_params=pltpu.CompilerParams(vmem_limit_bytes=VMEM_BYTES),
+        cost_estimate=pl.CostEstimate(flops=0, bytes_accessed=1 << 20, transcendentals=0),
+        name="place_edges",
+    )(skew_list, *ins, *ins)
+
+
+def place_kernel(skew, *refs, slots, rows, tiles):
+    rotor = refs[: slots - 2]
+    from_left, from_right, after, placed_ref = refs[slots - 2 :]
 
     def rotor_rows(b, _):
         at = pl.ds(pl.multiple_of(16 * b, 16), 16)
-        turn = skew[at, :]
-
-        def panel(steps, c):
-            if steps in (1, slots - 1):
-                source = from_left if steps == 1 else from_right
-                return source[2 * blocks + b * tiles + c]
-            source = rotor[0] if steps == 0 else rotor[steps - 1]
-            return source[at, c * LANES : (c + 1) * LANES]
-
-        cur = {q: f32(panel(slots - 1 - q // tiles, q % tiles)) for q in sorted(needs[bits])}
-        for bit in reversed(range(bits)):
-            on = ((turn >> bit) & 1) == 1
-            cur = {q: jnp.where(on, cur[(q - (1 << bit)) % panels], cur[q]) for q in sorted(needs[bit])}
-        for p in range(tiles):
-            placed_ref[p, at, :] = cur[want[p + 1]].astype(jnp.bfloat16)
-        side = jnp.where(lane16 < LANES // 2, cur[want[tiles + 1]], cur[want[0]])
-        placed_ref[tiles, at, :] = side.astype(jnp.bfloat16)
+        for p, value in enumerate(place_block(16 * b, skew, rotor, from_left, from_right, b, slots, tiles)):
+            placed_ref[p, at, :] = value
         return 0
 
     lax.fori_loop(0, rows // 16, rotor_rows, 0)
-    for out_ref, corner, first in (
-        (small_prev, 0, 0),
-        (small_next, 2 * blocks - 2, rows - 16),
-    ):
-        for i in (0, 1):
-            out_ref[i] = from_left[corner + i]
-            out_ref[2 + i] = from_right[corner + i]
-        for c in range(tiles + 1):
-            out_ref[4 + c] = placed_ref[c, first : first + 16, :]
-
-
-def place_cycle(rotor, skew, from_left, from_right):
+
+
+def place_cycle(rotor, skew_list, from_left, from_right, after):
     rows, cols = rotor[0].shape
     tiles = cols // LANES
-    sides = whole_at(from_left.shape, (0, 0, 0))
-    out = [(tiles + 1, rows, LANES)] + [(tiles + 5, 16, LANES)] * 2
+    sides = whole_at(from_left.shape, (0, 0, 0, 0))
+    out = (tiles + 1, rows, LANES)
     return pl.pallas_call(
         functools.partial(place_kernel, slots=len(rotor) + 2, rows=rows, tiles=tiles),
         grid=(1,),
-        in_specs=[whole_at((rows, cols), (0, 0))] * len(rotor) + [whole_at((rows, LANES), (0, 0)), sides, sides],
-        out_specs=[whole_at(x, (0,) * 3) for x in out],
-        out_shape=[jax.ShapeDtypeStruct(x, jnp.bfloat16) for x in out],
+        in_specs=[pl.BlockSpec(memory_space=pltpu.SMEM)]
+        + [whole_at((rows, cols), (0, 0))] * len(rotor)
+        + [sides, sides, pl.BlockSpec(memory_space=pl.ANY)],
+        out_specs=whole_at(out, (0,) * 3),
+        out_shape=jax.ShapeDtypeStruct(out, jnp.bfloat16),
         compiler_params=pltpu.CompilerParams(vmem_limit_bytes=VMEM_BYTES),
         cost_estimate=pl.CostEstimate(flops=0, bytes_accessed=4 << 20, transcendentals=0),
         name="place_cycle",
-    )(*rotor, skew, from_left, from_right)
+    )(skew_list, *rotor, from_left, from_right, after)
 
 
 def relax_kernel(placed, small_prev, small_next, from_left, from_right, from_prev, from_next,
@@ -268,8 +289,7 @@
                 side[1, item, q] = jnp.where(left_slot, b, a) * scale
 
         for q in range(blocks):
-            pick = slice(2 * q, 2 * q + 2)
-            decode(q, from_left[pick], from_right[pick])
+            decode(q, from_left[q], from_right[q])
         decode(blocks, small_prev[0:2], small_prev[2:4])
         decode(blocks + 1, small_next[0:2], small_next[2:4])
 
@@ -320,7 +340,7 @@
                     else:
                         dst[plane, tiles, pl.ds(EDGE + rows, 8), :] = pltpu.roll(side[colour, item, blocks + 1], turn, 1)
 
-    def half_step(m, colour, own, other, sig, cur, start, stride, outputs, write):
+    def half_step(m, colour, own, other, sig, cur, start, count, outputs, write):
         def row_tile(at):
             centre = [other[m + 1, c, pl.ds(at, 8), :] for c in range(tiles + 1)]
             ahead = [pltpu.roll(x, 1, 1) for x in centre]
@@ -337,12 +357,8 @@
                 new = cur[m, c, pl.ds(at, 8), :] + 0.25 * total - sig[m, c, pl.ds(at, 8), :] * (8.0 * near - far)
                 write(m, c, at, new)
 
-        def body(r, _):
-            for k in range(UNROLL):
-                row_tile(start + stride * r + 8 * k)
-            return 0
-
-        lax.fori_loop(0, SPANS, body, 0)
+        for r in range(count):
+            row_tile(start + 8 * r)
 
     def keep(buf):
         def write(m, c, at, new):
@@ -357,9 +373,8 @@
         out_ref[0, to, cols] = jnp.where(even8, red, new)
         out_ref[1, to, cols] = jnp.where(even8, new, red)
 
-    window = 8 * UNROLL
-    wide = (EDGE - 4, (rows + 8 - window) // (SPANS - 1), tiles + 1)
-    last = (EDGE, (rows - window) // (SPANS - 1), tiles)
+    wide = (EDGE - 4, rows // 8 + 1, tiles + 1)
+    last = (EDGE, rows // 8, tiles)
     plan = (
         (1, 0, red_a, black_a, sig_r, cur_r, wide, keep(red_b)),
         (2, 1, black_a, red_b, sig_b, cur_b, wide, keep(black_b)),
@@ -388,7 +403,7 @@
     halo = pl.BlockSpec((2, 1, 16, cols), lambda g: (0, coming(g), 0, 0))
     block = pl.BlockSpec((2, rows, cols), lambda g: (coming(g), 0, 0))
     fixed = [placed, small_prev, small_next]
-    side = pl.BlockSpec((rows // 8, 16, LANES), lambda g: (0, 0, 0))
+    side = pl.BlockSpec((rows // 16, 2, 16, LANES), lambda g: (0, 0, 0, 0))
     state = pltpu.VMEM((pairs + 2, tiles + 1, ext, LANES), jnp.float32)
     coef = pltpu.VMEM((pairs, tiles + 1, ext, LANES), jnp.float32)
     return pl.pallas_call(
@@ -409,15 +424,14 @@
 
 
 def local(field, sigma, current, rotor_cycle, skew_list):
-    rows = field.shape[1]
-    skew = jnp.broadcast_to(skew_list[:, None], (rows, LANES))
     rotor = [rotor_cycle] + [moved(rotor_cycle, "az", s) for s in range(2, lax.axis_size("az") - 1)]
     to_left, to_right = pack_cols(field, sigma, current, rotor_cycle)
     from_left, from_right = moved(to_right, "az", 1), moved(to_left, "az", -1)
-    to_prev, to_next = pack_rows(field, sigma, current)
+    to_prev, to_next = pack_rows(field, sigma, current, to_left)
     from_prev, from_next = moved(to_next, "ta", 1), moved(to_prev, "ta", -1)
-    placed, small_to_prev, small_to_next = place_cycle(rotor, skew, from_left, from_right)
+    small_to_prev, small_to_next = place_edges(rotor, skew_list, from_left, from_right)
     small_prev, small_next = moved(small_to_next, "ta", 1), moved(small_to_prev, "ta", -1)
+    placed = place_cycle(rotor, skew_list, from_left, from_right, small_to_prev)
     return relax(
         placed, small_prev, small_next, from_left, from_right, from_prev, from_next, field, sigma, current
     )

time: 69 us -> 63.8 us (0.925)
  Pallas kernels: 40.3 us -> 36.8 us
  waiting for transfers between devices: 13.7 us -> 11.3 us
    pallas_call x1, Pallas kernels: 29.8 us -> 24.9 us  [relax(): pl.pallas_call(functools.partial(relax_kernel, pairs=pairs, rows=rows, ti...]
    ppermute x7, waiting for transfers between devices: 13.7 us -> 11.3 us  [moved(): lax.ppermute(value, axis, [(i, (i + steps) % count) for i in range(count)])]
    pallas_call x0 -> x1, Pallas kernels: none -> 1.63 us  [place_edges(): pl.pallas_call(functools.partial(place_edges_kernel, slots=slots, rows=ro...]
    unnamed x18 -> x20, local copies, waits for them, and re-layouts: 1 us -> 2.33 us
    broadcast_in_dim x1 -> x0, local copies, waits for them, and re-layouts: 0.77 us -> none  [local(): skew = jnp.broadcast_to(skew_list[:, None], (rows, LANES))]
  transfers between devices with their start and end apart: 7 -> 7, of which waited for: 3 -> 2; matrix products, arithmetic and copies ran while one was open for 1% -> 0% of each run, Pallas kernels for 10% -> 6%
where the time goes in v5:
time: 63.8 us; the launch traced here: 63.5 us
  Pallas kernels  36.8 us (58%)
  starting transfers between devices  13 us (20%)
  waiting for transfers between devices  11.3 us (18%)
  local copies, waits for them, and re-layouts  2.33 us (4%)
    pallas_call x1, Pallas kernels, relax(): pl.pallas_call(functools.partial(relax_kernel, pairs=pairs, rows=rows, ti...  24.9 us
    ppermute x7, starting transfers between devices, moved(): lax.ppermute(value, axis, [(i, (i + steps) % count) for i in range(count)])  13 us
    ppermute x7, waiting for transfers between devices, moved(): lax.ppermute(value, axis, [(i, (i + steps) % count) for i in range(count)])  11.3 us
    pallas_call x1, Pallas kernels, pack_cols(): pl.pallas_call(functools.partial(cols_kernel, pairs=pairs, tiles=tiles, b...  4.43 us
    pallas_call x1, Pallas kernels, pack_rows(): pl.pallas_call(functools.partial(rows_kernel, pairs=pairs, tiles=tiles),...  3.41 us
    pallas_call x1, Pallas kernels, place_cycle(): pl.pallas_call(functools.partial(place_kernel, slots=len(rotor) + 2, rows...  2.39 us
    unnamed x20, local copies, waits for them, and re-layouts  2.33 us
    pallas_call x1, Pallas kernels, place_edges(): pl.pallas_call(functools.partial(place_edges_kernel, slots=slots, rows=ro...  1.63 us
  transfers between devices with their start and end apart: 7, of which 2 were waited for; matrix products, arithmetic and copies ran while one was open for 0% of the time, Pallas kernels for 6%

profile of v5, /device:TPU:0, one launch (start us, length us, event | category | flops | bytes accessed | tf_op | source)
XLA Modules:
  0.0 63.5 jit_solution(16979381292477275467)
XLA Ops:
  0.0 4.4 %pack_cols.1 = (bf16[8,10,16,128]{3,2,1,0:T(8,128)(2,1)}, bf16[8,10,16,128]{3,2,1,0:T(8,128)(2,1)}) custom-call(f32[16,128,1024]{2,1,0:T(8,128)} %u_ref.1, f32[16,128,1024]{2,1,0:T(8,128)} %u_ref.1, bf16[16,128,1024]{2,1,0:T(8,128)(2,1)} %s_ref.1, bf16[16,128,1024]{2,1,0:T(8,128)(2,1)} %s_ref.1, bf16[16,128,1024]{2,1,0:T(8,128)(2,1)} %j_ref.1, ...), custom_call_target="tpu_custom_call" | custom-call | bytes 16777216 | tf_op jit(solution)/shard_map/pack_cols/pallas_call | solution.py:141
  4.4 0.0 copy-start.9
  4.4 0.0 copy-start.6
  4.4 0.0 copy-start.2
  4.5 3.4 %pack_rows.1 = (bf16[2,8,16,1024]{3,2,1,0:T(8,128)(2,1)}, bf16[2,8,16,1024]{3,2,1,0:T(8,128)(2,1)}) custom-call(f32[16,128,1024]{2,1,0:T(8,128)} %u_ref.1, f32[16,128,1024]{2,1,0:T(8,128)} %u_ref.1, bf16[16,128,1024]{2,1,0:T(8,128)(2,1)} %s_ref.1, bf16[16,128,1024]{2,1,0:T(8,128)(2,1)} %s_ref.1, bf16[16,128,1024]{2,1,0:T(8,128)(2,1)} %j_ref.1, ...), custom_call_target="tpu_custom_call" | custom-call | bytes 12582912 | tf_op jit(solution)/shard_map/pack_rows/pallas_call | solution.py:122
  7.9 0.5 collective-permute-start.5
  8.3 4.0 %collective-permute-start.6 = (bf16[2,8,16,1024]{3,2,1,0:T(8,128)(2,1)}, bf16[2,8,16,1024]{3,2,1,0:T(8,128)(2,1)S(1)}, u32[]{:S(2)}, u32[]{:S(2)}) collective-permute-start(bf16[2,8,16,1024]{3,2,1,0:T(8,128)(2,1)} %get-tuple-element.16), channel_id=1, source_target_pairs={{0,7},{1,0},{2,1},{3,2},{4,3},{5,4},{6,5},{7,6},{8,15},{9,8},{10,9... | collective-permute-start | bytes 1572872 | tf_op jit(solution)/shard_map/ppermute | solution.py:423
  12.4 0.0 copy-done.9
  12.4 2.0 %collective-permute-start.1 = (bf16[8,10,16,128]{3,2,1,0:T(8,128)(2,1)S(1)}, bf16[8,10,16,128]{3,2,1,0:T(8,128)(2,1)S(1)}, u32[]{:S(2)}, u32[]{:S(2)}) collective-permute-start(bf16[8,10,16,128]{3,2,1,0:T(8,128)(2,1)S(1)} %copy-done.9), channel_id=1, source_target_pairs={{0,8},{8,16},{16,24},{24,0},{1,9},{9,17},{17,25},{25,1},{2,10},{10... | collective-permute-start | bytes 983048 | tf_op jit(solution)/shard_map/ppermute | solution.py:423
  14.4 0.0 copy-done.6
  14.4 1.0 %collective-permute-start.2 = (bf16[8,10,16,128]{3,2,1,0:T(8,128)(2,1)S(1)}, bf16[8,10,16,128]{3,2,1,0:T(8,128)(2,1)S(1)}, u32[]{:S(2)}, u32[]{:S(2)}) collective-permute-start(bf16[8,10,16,128]{3,2,1,0:T(8,128)(2,1)S(1)} %copy-done.6), channel_id=1, source_target_pairs={{0,24},{8,0},{16,8},{24,16},{1,25},{9,1},{17,9},{25,17},{2,26},{10... | collective-permute-start | bytes 983048 | tf_op jit(solution)/shard_map/ppermute | solution.py:423
  15.4 0.0 copy-done.2
  15.4 1.9 %collective-permute-start = (bf16[128,1024]{1,0:T(8,128)(2,1)S(1)}, bf16[128,1024]{1,0:T(8,128)(2,1)S(1)}, u32[]{:S(2)}, u32[]{:S(2)}) collective-permute-start(bf16[128,1024]{1,0:T(8,128)(2,1)S(1)} %copy-done.2), channel_id=1, source_target_pairs={{0,16},{8,24},{16,0},{24,8},{1,17},{9,25},{17,1},{25,9},{2,18},{10... | collective-permute-start | bytes 786440 | tf_op jit(solution)/shard_map/ppermute | solution.py:423
  17.3 9.8 %collective-permute-done.refs_1_.refs_5_ = bf16[128,1024]{1,0:T(8,128)(2,1)S(1)} collective-permute-done((bf16[128,1024]{1,0:T(8,128)(2,1)S(1)}, bf16[128,1024]{1,0:T(8,128)(2,1)S(1)}, u32[]{:S(2)}, u32[]{:S(2)}) %collective-permute-start) | collective-permute-done | bytes 262176 | tf_op jit(solution)/shard_map/ppermute | solution.py:423
  27.2 0.0 copy-start.3
  27.2 0.0 collective-permute-done.1.refs_2_.refs_6_.from_left
  27.2 0.0 copy-start
  27.2 1.5 %collective-permute-done.2.refs_3_.refs_7_.from_right = bf16[8,10,16,128]{3,2,1,0:T(8,128)(2,1)S(1)} collective-permute-done((bf16[8,10,16,128]{3,2,1,0:T(8,128)(2,1)S(1)}, bf16[8,10,16,128]{3,2,1,0:T(8,128)(2,1)S(1)}, u32[]{:S(2)}, u32[]{:S(2)}) %collective-permute-start.2) | collective-permute-done | bytes 327712 | tf_op jit(solution)/shard_map/ppermute | solution.py:423
  28.7 0.0 copy-done.3
  28.7 0.0 copy-done
  28.7 0.0 copy-start.1
  28.7 0.7 %copy-done.1 = bf16[8,10,16,128]{3,2,1,0:T(8,128)(2,1)} copy-done((bf16[8,10,16,128]{3,2,1,0:T(8,128)(2,1)}, bf16[8,10,16,128]{3,2,1,0:T(8,128)(2,1)S(1)}, u32[]{:S(2)}) %copy-start.1) | copy-done | bytes 327704
  29.4 1.6 %place_edges.1 = (bf16[13,16,128]{2,1,0:T(8,128)(2,1)}, bf16[13,16,128]{2,1,0:T(8,128)(2,1)}) custom-call(s32[128]{0:T(128)} %skew.3, bf16[128,1024]{1,0:T(8,128)(2,1)} %refs_0_.3, bf16[128,1024]{1,0:T(8,128)(2,1)} %copy-done.3, bf16[8,10,16,128]{3,2,1,0:T(8,128)(2,1)} %copy-done, bf16[8,10,16,128]{3,2,1,0:T(8,128)(2,1)} %copy-done.1, ...), custom_call_target="tpu_custom_call" | custom-call | bytes 1048576 | tf_op jit(solution)/shard_map/place_edges/pallas_call | solution.py:202
  31.0 0.0 collective-permute-start.3
  31.0 3.5 %collective-permute-start.4 = (bf16[13,16,128]{2,1,0:T(8,128)(2,1)}, bf16[13,16,128]{2,1,0:T(8,128)(2,1)S(1)}, u32[]{:S(2)}, u32[]{:S(2)}) collective-permute-start(bf16[13,16,128]{2,1,0:T(8,128)(2,1)} %get-tuple-element.13.refs_4_), channel_id=1, source_target_pairs={{0,7},{1,0},{2,1},{3,2},{4,3},{5,4},{6,5},{7,6},{8,15},{9,8},{10,9... | collective-permute-start | bytes 159752 | tf_op jit(solution)/shard_map/ppermute | solution.py:423
  34.6 2.4 %place_cycle.1.placed = bf16[9,128,128]{2,1,0:T(8,128)(2,1)} custom-call(s32[128]{0:T(128)} %skew.3, bf16[128,1024]{1,0:T(8,128)(2,1)} %refs_0_.3, bf16[128,1024]{1,0:T(8,128)(2,1)} %copy-done.3, bf16[8,10,16,128]{3,2,1,0:T(8,128)(2,1)} %copy-done, bf16[8,10,16,128]{3,2,1,0:T(8,128)(2,1)} %copy-done.1, bf16[13,16,128]{2,1,0:T(8,128)(2,1)} %get-tuple-element.13.refs_4_), custom_call_target="tpu_custom_call" | custom-call | bytes 4194304 | tf_op jit(solution)/shard_map/place_cycle/pallas_call | solution.py:232
  37.0 0.0 collective-permute-done.3.small_prev
  37.0 0.0 copy-start.7
  37.0 0.0 collective-permute-done.4.small_next
  37.0 0.0 copy-start.8
  37.0 0.0 collective-permute-done.5.from_prev
  37.0 0.0 copy-start.4
  37.0 0.0 collective-permute-done.6.from_next
  37.0 0.6 copy-done.7
  37.6 0.0 copy-done.8
  37.6 0.2 copy-done.4
  37.8 0.0 copy-start.5
  37.8 0.8 %copy-done.5 = bf16[2,8,16,1024]{3,2,1,0:T(8,128)(2,1)} copy-done((bf16[2,8,16,1024]{3,2,1,0:T(8,128)(2,1)}, bf16[2,8,16,1024]{3,2,1,0:T(8,128)(2,1)S(1)}, u32[]{:S(2)}) %copy-start.5) | copy-done | bytes 524312
  38.6 24.9 %relax.1 = f32[16,128,1024]{2,1,0:T(8,128)} custom-call(bf16[9,128,128]{2,1,0:T(8,128)(2,1)} %place_cycle.1.placed, bf16[13,16,128]{2,1,0:T(8,128)(2,1)} %copy-done.7, bf16[13,16,128]{2,1,0:T(8,128)(2,1)} %copy-done.8, bf16[8,10,16,128]{3,2,1,0:T(8,128)(2,1)} %copy-done, bf16[8,10,16,128]{3,2,1,0:T(8,128)(2,1)} %copy-done.1, ...), custom_call_target="tpu_custom_call" | custom-call | tf_op jit(solution)/shard_map/relax/pallas_call | solution.py:409
Async XLA Ops:
  4.4 7.9 %copy-start.9 = (bf16[8,10,16,128]{3,2,1,0:T(8,128)(2,1)S(1)}, bf16[8,10,16,128]{3,2,1,0:T(8,128)(2,1)}, u32[]{:S(2)}) copy-start(bf16[8,10,16,128]{3,2,1,0:T(8,128)(2,1)} %get-tuple-element.11) | copy-start | bytes 983044
  4.4 9.9 %copy-start.6 = (bf16[8,10,16,128]{3,2,1,0:T(8,128)(2,1)S(1)}, bf16[8,10,16,128]{3,2,1,0:T(8,128)(2,1)}, u32[]{:S(2)}) copy-start(bf16[8,10,16,128]{3,2,1,0:T(8,128)(2,1)} %get-tuple-element.12.after) | copy-start | bytes 983044
  4.4 10.9 %copy-start.2 = (bf16[128,1024]{1,0:T(8,128)(2,1)S(1)}, bf16[128,1024]{1,0:T(8,128)(2,1)}, u32[]{:S(2)}) copy-start(bf16[128,1024]{1,0:T(8,128)(2,1)} %refs_0_.3) | copy-start | bytes 786436
  7.9 29.1 %collective-permute-start.5 = (bf16[2,8,16,1024]{3,2,1,0:T(8,128)(2,1)}, bf16[2,8,16,1024]{3,2,1,0:T(8,128)(2,1)S(1)}, u32[]{:S(2)}, u32[]{:S(2)}) collective-permute-start(bf16[2,8,16,1024]{3,2,1,0:T(8,128)(2,1)} %get-tuple-element.15), channel_id=1, source_target_pairs={{0,1},{1,2},{2,3},{3,4},{4,5},{5,6},{6,7},{7,0},{8,9},{9,10},{10,1... | collective-permute-start | bytes 1572872 | tf_op jit(solution)/shard_map/ppermute | solution.py:423
  8.3 28.7 %collective-permute-start.6 = (bf16[2,8,16,1024]{3,2,1,0:T(8,128)(2,1)}, bf16[2,8,16,1024]{3,2,1,0:T(8,128)(2,1)S(1)}, u32[]{:S(2)}, u32[]{:S(2)}) collective-permute-start(bf16[2,8,16,1024]{3,2,1,0:T(8,128)(2,1)} %get-tuple-element.16), channel_id=1, source_target_pairs={{0,7},{1,0},{2,1},{3,2},{4,3},{5,4},{6,5},{7,6},{8,15},{9,8},{10,9... | collective-permute-start | bytes 1572872 | tf_op jit(solution)/shard_map/ppermute | solution.py:423
  12.4 14.8 %collective-permute-start.1 = (bf16[8,10,16,128]{3,2,1,0:T(8,128)(2,1)S(1)}, bf16[8,10,16,128]{3,2,1,0:T(8,128)(2,1)S(1)}, u32[]{:S(2)}, u32[]{:S(2)}) collective-permute-start(bf16[8,10,16,128]{3,2,1,0:T(8,128)(2,1)S(1)} %copy-done.9), channel_id=1, source_target_pairs={{0,8},{8,16},{16,24},{24,0},{1,9},{9,17},{17,25},{25,1},{2,10},{10... | collective-permute-start | bytes 983048 | tf_op jit(solution)/shard_map/ppermute | solution.py:423
  14.4 14.3 %collective-permute-start.2 = (bf16[8,10,16,128]{3,2,1,0:T(8,128)(2,1)S(1)}, bf16[8,10,16,128]{3,2,1,0:T(8,128)(2,1)S(1)}, u32[]{:S(2)}, u32[]{:S(2)}) collective-permute-start(bf16[8,10,16,128]{3,2,1,0:T(8,128)(2,1)S(1)} %copy-done.6), channel_id=1, source_target_pairs={{0,24},{8,0},{16,8},{24,16},{1,25},{9,1},{17,9},{25,17},{2,26},{10... | collective-permute-start | bytes 983048 | tf_op jit(solution)/shard_map/ppermute | solution.py:423
  15.4 11.8 %collective-permute-start = (bf16[128,1024]{1,0:T(8,128)(2,1)S(1)}, bf16[128,1024]{1,0:T(8,128)(2,1)S(1)}, u32[]{:S(2)}, u32[]{:S(2)}) collective-permute-start(bf16[128,1024]{1,0:T(8,128)(2,1)S(1)} %copy-done.2), channel_id=1, source_target_pairs={{0,16},{8,24},{16,0},{24,8},{1,17},{9,25},{17,1},{25,9},{2,18},{10... | collective-permute-start | bytes 786440 | tf_op jit(solution)/shard_map/ppermute | solution.py:423
  27.2 1.5 %copy-start.3 = (bf16[128,1024]{1,0:T(8,128)(2,1)}, bf16[128,1024]{1,0:T(8,128)(2,1)S(1)}, u32[]{:S(2)}) copy-start(bf16[128,1024]{1,0:T(8,128)(2,1)S(1)} %collective-permute-done.refs_1_.refs_5_) | copy-start | bytes 786436
  27.2 1.5 %copy-start = (bf16[8,10,16,128]{3,2,1,0:T(8,128)(2,1)}, bf16[8,10,16,128]{3,2,1,0:T(8,128)(2,1)S(1)}, u32[]{:S(2)}) copy-start(bf16[8,10,16,128]{3,2,1,0:T(8,128)(2,1)S(1)} %collective-permute-done.1.refs_2_.refs_6_.from_left) | copy-start | bytes 983044
  28.7 0.7 %copy-start.1 = (bf16[8,10,16,128]{3,2,1,0:T(8,128)(2,1)}, bf16[8,10,16,128]{3,2,1,0:T(8,128)(2,1)S(1)}, u32[]{:S(2)}) copy-start(bf16[8,10,16,128]{3,2,1,0:T(8,128)(2,1)S(1)} %collective-permute-done.2.refs_3_.refs_7_.from_right) | copy-start | bytes 983044
  31.0 5.9 %collective-permute-start.3 = (bf16[13,16,128]{2,1,0:T(8,128)(2,1)}, bf16[13,16,128]{2,1,0:T(8,128)(2,1)S(1)}, u32[]{:S(2)}, u32[]{:S(2)}) collective-permute-start(bf16[13,16,128]{2,1,0:T(8,128)(2,1)} %get-tuple-element.14), channel_id=1, source_target_pairs={{0,1},{1,2},{2,3},{3,4},{4,5},{5,6},{6,7},{7,0},{8,9},{9,10},{10,1... | collective-permute-start | bytes 159752 | tf_op jit(solution)/shard_map/ppermute | solution.py:423
  31.0 5.9 %collective-permute-start.4 = (bf16[13,16,128]{2,1,0:T(8,128)(2,1)}, bf16[13,16,128]{2,1,0:T(8,128)(2,1)S(1)}, u32[]{:S(2)}, u32[]{:S(2)}) collective-permute-start(bf16[13,16,128]{2,1,0:T(8,128)(2,1)} %get-tuple-element.13.refs_4_), channel_id=1, source_target_pairs={{0,7},{1,0},{2,1},{3,2},{4,3},{5,4},{6,5},{7,6},{8,15},{9,8},{10,9... | collective-permute-start | bytes 159752 | tf_op jit(solution)/shard_map/ppermute | solution.py:423
  37.0 0.6 copy-start.7
  37.0 0.6 copy-start.8
  37.0 0.8 %copy-start.4 = (bf16[2,8,16,1024]{3,2,1,0:T(8,128)(2,1)}, bf16[2,8,16,1024]{3,2,1,0:T(8,128)(2,1)S(1)}, u32[]{:S(2)}) copy-start(bf16[2,8,16,1024]{3,2,1,0:T(8,128)(2,1)S(1)} %collective-permute-done.5.from_prev) | copy-start | bytes 1572868
  37.8 0.8 %copy-start.5 = (bf16[2,8,16,1024]{3,2,1,0:T(8,128)(2,1)}, bf16[2,8,16,1024]{3,2,1,0:T(8,128)(2,1)S(1)}, u32[]{:S(2)}) copy-start(bf16[2,8,16,1024]{3,2,1,0:T(8,128)(2,1)S(1)} %collective-permute-done.6.from_next) | copy-start | bytes 1572868

commit v6 on v5

v6 whole, which is shorter than its diff:
```python
import functools

import jax
import jax.numpy as jnp
from jax import lax
from jax.experimental import pallas as pl
from jax.experimental.pallas import tpu as pltpu
from jax.sharding import PartitionSpec as P

LANES = 128
EDGE = 8
LAG = 4
VMEM_BYTES = 60 * 1024 * 1024


def checker(rows):
    sub = lax.broadcasted_iota(jnp.int32, (rows, LANES), 0)
    lane = lax.broadcasted_iota(jnp.int32, (rows, LANES), 1)
    return ((sub + lane) & 1) == 0


def f32(value):
    return value.astype(jnp.float32)


def split_high_low(value):
    high = f32(value.astype(jnp.bfloat16))
    return high, value - high


def rows_kernel(u_top, u_bot, s_top, s_bot, j_top, j_bot, after, to_prev, to_next, *, pairs, tiles):
    even8 = checker(8)
    sub = lax.broadcasted_iota(jnp.int32, (8, LANES), 0)
    field_rows = sub < 5

    def pair_rows(m, _):
        for c in range(tiles):
            cols = slice(c * LANES, (c + 1) * LANES)
            for u_ref, s_ref, j_ref, half, out_ref in (
                (u_top, s_top, j_top, 0, to_prev),
                (u_bot, s_bot, j_bot, 8, to_next),
            ):
                eo = []
                for ref in (u_ref, s_ref, j_ref):
                    first = f32(ref[2 * m, :, cols])
                    second = f32(ref[2 * m + 1, :, cols])
                    if first.shape[0] == 16:
                        first = first[half : half + 8]
                        second = second[half : half + 8]
                    eo.append((first, second))
                for colour in (0, 1):
                    pick = [
                        jnp.where(even8, a, b) if colour == 0 else jnp.where(even8, b, a)
                        for a, b in eo
                    ]
                    high, low = split_high_low(pick[0])
                    sig, cur = pick[1], pick[2]
                    if half == 0:
                        sig = pltpu.roll(sig, 5, 0)
                        cur = pltpu.roll(cur, 5, 0)
                    else:
                        high = pltpu.roll(high, 5, 0)
                        low = pltpu.roll(low, 5, 0)
                    both = jnp.concatenate(
                        [jnp.where(field_rows, high, sig), jnp.where(field_rows, low, cur)], 0
                    )
                    out_ref[colour, m, :, cols] = both.astype(jnp.bfloat16)
        return 0

    lax.fori_loop(0, pairs, pair_rows, 0)


def cols_kernel(
    u_left, u_right, s_left, s_right, j_left, j_right, to_left, to_right, *, pairs, blocks
):
    even16 = checker(16)
    slot = lax.broadcasted_iota(jnp.int32, (8, LANES), 1) // 4
    slots = LANES // 4
    for q in range(blocks):
        rows = slice(16 * q, 16 * q + 16)
        for refs, out_ref, near_at, far_at in (
            ((u_left, s_left, j_left), to_left, 1, 2),
            ((u_right, s_right, j_right), to_right, 0, 1),
        ):
            packed = []
            for ref in refs:
                total = jnp.zeros((8, LANES), jnp.float32)
                for m in range(pairs):
                    first = f32(ref[2 * m, rows, :])
                    second = f32(ref[2 * m + 1, rows, :])
                    red = jnp.where(even16, first, second)
                    black = jnp.where(even16, second, first)
                    for w in (0, 1):
                        g = m + pairs * w
                        near = pltpu.roll(red[8 * w : 8 * w + 8], (8 * g + 4) % LANES, 1)
                        far = pltpu.roll(black[8 * w : 8 * w + 8], (8 * g + 8) % LANES, 1)
                        total = jnp.where(slot == (2 * g + near_at) % slots, near, total)
                        total = jnp.where(slot == (2 * g + far_at) % slots, far, total)
                packed.append(total)
            high, low = split_high_low(packed[0])
            out_ref[q, 0] = jnp.concatenate([high, low], 0).astype(jnp.bfloat16)
            out_ref[q, 1] = jnp.concatenate([packed[1], packed[2]], 0).astype(jnp.bfloat16)


def whole_at(shape, index):
    return pl.BlockSpec(shape, lambda i: index)


def pack_rows(field, sigma, current, after):
    layers, rows, cols = field.shape
    pairs, tiles = layers // 2, cols // LANES

    def row_specs(height):
        shape = (layers, height, cols)
        return [whole_at(shape, (0, 0, 0)), whole_at(shape, (0, rows // height - 1, 0))]

    shape = (2, pairs, 16, cols)
    return pl.pallas_call(
        functools.partial(rows_kernel, pairs=pairs, tiles=tiles),
        grid=(1,),
        in_specs=row_specs(8) + row_specs(16) * 2 + [pl.BlockSpec(memory_space=pl.ANY)],
        out_specs=[whole_at(shape, (0,) * 4)] * 2,
        out_shape=[jax.ShapeDtypeStruct(shape, jnp.bfloat16)] * 2,
        compiler_params=pltpu.CompilerParams(vmem_limit_bytes=VMEM_BYTES),
        cost_estimate=pl.CostEstimate(flops=0, bytes_accessed=12 << 20, transcendentals=0),
        name="pack_rows",
    )(field, field, sigma, sigma, current, current, after)


def pack_cols(field, sigma, current):
    layers, rows, cols = field.shape
    pairs, tiles, blocks = layers // 2, cols // LANES, rows // 16
    part = 2
    shape = (layers, 16 * part, LANES)
    col_specs = [pl.BlockSpec(shape, lambda i: (0, i, 0)), pl.BlockSpec(shape, lambda i: (0, i, tiles - 1))]
    out_spec = pl.BlockSpec((part, 2, 16, LANES), lambda i: (i, 0, 0, 0))
    return pl.pallas_call(
        functools.partial(cols_kernel, pairs=pairs, blocks=part),
        grid=(blocks // part,),
        in_specs=col_specs * 3,
        out_specs=[out_spec] * 2,
        out_shape=[jax.ShapeDtypeStruct((blocks, 2, 16, LANES), jnp.bfloat16)] * 2,
        compiler_params=pltpu.CompilerParams(vmem_limit_bytes=VMEM_BYTES),
        cost_estimate=pl.CostEstimate(flops=0, bytes_accessed=16 << 20, transcendentals=0),
        name="pack_cols",
    )(field, field, sigma, sigma, current, current)


def small_kernel(skew, r_top, r_bot, l_near, l_far, e_near, e_far, small_prev, small_next, *, rows, tiles):
    sub = lax.broadcasted_iota(jnp.int32, (16, LANES), 0)
    for out_ref, r_ref, left, right, first in (
        (small_prev, r_top, l_near, e_near, 0),
        (small_next, r_bot, l_far, e_far, rows - 16),
    ):
        for i in (0, 1):
            out_ref[i] = left[0, i]
            out_ref[2 + i] = right[0, i]
        for c in range(tiles):
            out_ref[4 + c] = r_ref[:, c * LANES : (c + 1) * LANES]
        out_ref[4 + tiles] = f32(turns(skew, first, sub)).astype(jnp.bfloat16)


def turns(skew, row, sub):
    turn = jnp.zeros(sub.shape, jnp.int32)
    for i in range(16):
        turn = jnp.where(sub == i, skew[row + i], turn)
    return turn


def pack_small(rotor_cycle, skew_list, from_left, from_right):
    rows, cols = rotor_cycle.shape
    tiles, blocks = cols // LANES, rows // 16
    ends = (0, blocks - 1)
    side = [whole_at((1, 2, 16, LANES), (i, 0, 0, 0)) for i in ends]
    out = (tiles + 5, 16, LANES)
    return pl.pallas_call(
        functools.partial(small_kernel, rows=rows, tiles=tiles),
        grid=(1,),
        in_specs=[pl.BlockSpec(memory_space=pltpu.SMEM)] + [whole_at((16, cols), (i, 0)) for i in ends] + side * 2,
        out_specs=[whole_at(out, (0,) * 3)] * 2,
        out_shape=[jax.ShapeDtypeStruct(out, jnp.bfloat16)] * 2,
        compiler_params=pltpu.CompilerParams(vmem_limit_bytes=VMEM_BYTES),
        name="pack_small",
    )(skew_list, rotor_cycle, rotor_cycle, from_left, from_left, from_right, from_right)


def rotor_kernel(rotor, small_prev, small_next, out_ref, *, blocks, tiles):
    for c in range(tiles):
        for b in range(blocks):
            out_ref[b, c] = rotor[16 * b : 16 * b + 16, c * LANES : (c + 1) * LANES]
        out_ref[blocks, c] = small_prev[4 + c]
        out_ref[blocks + 1, c] = small_next[4 + c]


def pack_rotor(rotor_cycle, small_prev, small_next):
    rows, cols = rotor_cycle.shape
    tiles, blocks = cols // LANES, rows // 16
    small = whole_at((tiles + 5, 16, LANES), (0, 0, 0))
    out = (blocks + 2, tiles, 16, LANES)
    return pl.pallas_call(
        functools.partial(rotor_kernel, blocks=blocks, tiles=tiles),
        grid=(1,),
        in_specs=[whole_at((rows, cols), (0, 0)), small, small],
        out_specs=whole_at(out, (0,) * 4),
        out_shape=jax.ShapeDtypeStruct(out, jnp.bfloat16),
        compiler_params=pltpu.CompilerParams(vmem_limit_bytes=VMEM_BYTES),
        name="pack_rotor",
    )(rotor_cycle, small_prev, small_next)


def place_block(turn, rotor, b, slots, tiles):
    lane16 = lax.broadcasted_iota(jnp.int32, (16, LANES), 1)
    panels = slots * tiles
    bits = (panels - 1).bit_length()
    want = [(panels - tiles - 1 + p) % panels for p in range(tiles + 2)]
    needs = [set(want)]
    for bit in range(bits):
        needs.append(needs[-1] | {(q - (1 << bit)) % panels for q in needs[-1]})
    cur = {q: f32(rotor[slots - 1 - q // tiles][b, q % tiles]) for q in sorted(needs[bits])}
    for bit in reversed(range(bits)):
        on = ((turn >> bit) & 1) == 1
        cur = {q: jnp.where(on, cur[(q - (1 << bit)) % panels], cur[q]) for q in sorted(needs[bit])}
    placed = [cur[want[p + 1]] for p in range(tiles)]
    return placed + [jnp.where(lane16 < LANES // 2, cur[want[tiles + 1]], cur[want[0]])]


def make_steps(ins, out_ref, scratch, pairs, rows, tiles):
    small_prev, small_next, from_left, from_right, from_prev, from_next, u_ref, s_ref, j_ref = ins
    red_a, red_b, black_a, black_b, sig_r, sig_b, cur_r, cur_b, side = scratch
    blocks = rows // 16
    even8 = checker(8)
    even16 = checker(16)
    lane = lax.broadcasted_iota(jnp.int32, (8, LANES), 1)
    lane_first = lane == 0
    lane_last = lane == LANES - 1
    left_slot = (lane & 7) < 4

    def decode(q, left, right):
        left0, left1, right0, right1 = f32(left[0]), f32(left[1]), f32(right[0]), f32(right[1])
        items = (
            (left0[:8] + left0[8:], right0[:8] + right0[8:], 1.0),
            (left1[:8], right1[:8], 1.0 / 48.0),
            (left1[8:], right1[8:], 0.25),
        )
        for item, (a, b, scale) in enumerate(items):
            side[0, item, q] = jnp.where(left_slot, a, b) * scale
            side[1, item, q] = jnp.where(left_slot, b, a) * scale

    def start():
        for q in range(blocks):
            decode(q, from_left[q], from_right[q])
        decode(blocks, small_prev[0:2], small_prev[2:4])
        decode(blocks + 1, small_next[0:2], small_next[2:4])

    def load(m, with_field):
        fields = ((red_a, sig_r, cur_r), (black_a, sig_b, cur_b))
        for colour in (0, 1):
            u_dst, s_dst, j_dst = fields[colour]
            for c in range(tiles):
                cols = slice(c * LANES, (c + 1) * LANES)
                both = f32(from_prev[colour, 0, :, cols])
                if with_field:
                    u_dst[m + 1, c, pl.ds(EDGE - 5, 8), :] = both[:8] + both[8:]
                s_dst[m, c, pl.ds(0, 8), :] = both[:8] * (1.0 / 48.0)
                j_dst[m, c, pl.ds(0, 8), :] = both[8:] * 0.25
                both = f32(from_next[colour, 0, :, cols])
                if with_field:
                    u_dst[m + 1, c, pl.ds(EDGE + rows, 8), :] = both[:8] + both[8:]
                s_dst[m, c, pl.ds(EDGE + rows - 5, 8), :] = both[:8] * (1.0 / 48.0)
                j_dst[m, c, pl.ds(EDGE + rows - 5, 8), :] = both[8:] * 0.25

        def own_rows(q, _):
            at = pl.ds(pl.multiple_of(16 * q, 16), 16)
            to = pl.ds(pl.multiple_of(16 * q + EDGE, 8), 16)
            for c in range(tiles):
                cols = slice(c * LANES, (c + 1) * LANES)
                if with_field:
                    a, b = u_ref[0, at, cols], u_ref[1, at, cols]
                    red_a[m + 1, c, to, :] = jnp.where(even16, a, b)
                    black_a[m + 1, c, to, :] = jnp.where(even16, b, a)
                a, b = f32(s_ref[0, at, cols]) * (1.0 / 48.0), f32(s_ref[1, at, cols]) * (1.0 / 48.0)
                sig_r[m, c, to, :] = jnp.where(even16, a, b)
                sig_b[m, c, to, :] = jnp.where(even16, b, a)
                a, b = f32(j_ref[0, at, cols]) * 0.25, f32(j_ref[1, at, cols]) * 0.25
                cur_r[m, c, to, :] = jnp.where(even16, a, b)
                cur_b[m, c, to, :] = jnp.where(even16, b, a)
            return 0

        lax.fori_loop(0, blocks, own_rows, 0)

        for colour in (0, 1):
            u_dst, s_dst, j_dst = fields[colour]
            for item, (dst, plane) in enumerate(((u_dst, m + 1), (s_dst, m), (j_dst, m))):
                if item == 0 and not with_field:
                    continue
                for w in (0, 1):
                    turn = lax.rem(2 * LANES + 124 - 4 * colour - 8 * (m + pairs * w), LANES)
                    for q in range(blocks):
                        dst[plane, tiles, pl.ds(EDGE + 16 * q + 8 * w, 8), :] = pltpu.roll(side[colour, item, q], turn, 1)
                    if w == 1:
                        dst[plane, tiles, pl.ds(0, 8), :] = pltpu.roll(side[colour, item, blocks], turn, 1)
                    else:
                        dst[plane, tiles, pl.ds(EDGE + rows, 8), :] = pltpu.roll(side[colour, item, blocks + 1], turn, 1)

    def half_step(m, colour, own, other, sig, cur, start, count, outputs, write):
        def row_tile(at):
            centre = [other[m + 1, c, pl.ds(at, 8), :] for c in range(tiles + 1)]
            ahead = [pltpu.roll(x, 1, 1) for x in centre]
            back = [pltpu.roll(x, LANES - 1, 1) for x in centre]
            for c in range(outputs):
                left = jnp.where(lane_first, ahead[c - 1], ahead[c])
                right = jnp.where(lane_last, back[(c + 1) % (tiles + 1)], back[c])
                below = other[m, c, pl.ds(at, 8), :]
                above = other[m + 2, c, pl.ds(at, 8), :]
                outer = jnp.where(even8, below, above) if colour == 0 else jnp.where(even8, above, below)
                near = other[m + 1, c, pl.ds(at + 1, 8), :] - other[m + 1, c, pl.ds(at - 1, 8), :]
                far = own[m + 1, c, pl.ds(at + 2, 8), :] - own[m + 1, c, pl.ds(at - 2, 8), :]
                total = (left + right) + (centre[c] + outer)
                new = cur[m, c, pl.ds(at, 8), :] + 0.25 * total - sig[m, c, pl.ds(at, 8), :] * (8.0 * near - far)
                write(m, c, at, new)

        for r in range(count):
            row_tile(start + 8 * r)

    def keep(buf):
        def write(m, c, at, new):
            buf[m + 1, c, pl.ds(at, 8), :] = new

        return write

    def emit(m, c, at, new):
        red = red_a[m + 1, c, pl.ds(at, 8), :]
        cols = slice(c * LANES, (c + 1) * LANES)
        to = pl.ds(pl.multiple_of(at - EDGE, 8), 8)
        out_ref[0, to, cols] = jnp.where(even8, red, new)
        out_ref[1, to, cols] = jnp.where(even8, new, red)

    wide = (EDGE - 4, rows // 8 + 1, tiles + 1)
    last = (EDGE, rows // 8, tiles)

    def step(number, m):
        own, other, sig, cur, where, write = (
            (red_a, black_a, sig_r, cur_r, wide, keep(red_b)),
            (black_a, red_b, sig_b, cur_b, wide, keep(black_b)),
            (red_b, black_b, sig_r, cur_r, wide, keep(red_a)),
            (black_b, red_a, sig_b, cur_b, last, emit),
        )[number - 1]
        half_step(m, (number - 1) % 2, own, other, sig, cur, *where, write)

    return start, load, step


def upper_kernel(*refs, pairs, rows, tiles):
    ins, out_ref, saved, scratch, sem = refs[:9], refs[9], refs[10:13], refs[13:22], refs[22]
    g = pl.program_id(0)
    start, load, step = make_steps(ins, out_ref, scratch, pairs, rows, tiles)
    red_a, red_b, black_a, black_b = scratch[:4]
    copies = [
        pltpu.make_async_copy(buf.at[pl.ds(first, 2)], to, sem.at[i])
        for i, (buf, first, to) in enumerate(zip((red_b, black_b, red_a), (2, 3, 4), saved))
    ]

    @pl.when(g == 0)
    def first():
        start()
        zero = jnp.zeros((8, LANES), jnp.float32)
        for buf in (red_a, red_b, black_a, black_b):
            for c in range(tiles + 1):
                for r in range(rows // 8 + 2):
                    buf[pairs + 1, c, pl.ds(8 * r, 8), :] = zero

    load(pairs - 1 - g, True)
    for number in (1, 2, 3, 4):

        @pl.when(g >= number)
        def run(number=number):
            step(number, pairs - 1 - g + number)

        if number < 4:

            @pl.when(g == pairs - 1)
            def save(number=number):
                copies[number - 1].start()

    @pl.when(g == pairs - 1)
    def finish():
        for copy in copies:
            copy.wait()


def lower_kernel(*refs, slots, pairs, rows, tiles):
    saved, skew, rotor, refs = refs[1:4], refs[4], refs[5 : 5 + slots], refs[5 + slots :]
    ins, out_ref, scratch, sem = refs[:9], refs[9], refs[10:19], refs[19]
    small_prev, small_next = ins[:2]
    g = pl.program_id(0)
    blocks = rows // 16
    start, load, step = make_steps(ins, out_ref, scratch, pairs, rows, tiles)
    red_a, red_b, black_a, black_b = scratch[:4]
    copies = [
        pltpu.make_async_copy(of, buf.at[pl.ds(first, 2)], sem.at[i])
        for i, (buf, first, of) in enumerate(zip((red_b, black_b, red_a), (2, 3, 4), saved))
    ]

    @pl.when(g == 0)
    def first():
        for copy in copies:
            copy.start()
        start()
        sub16 = lax.broadcasted_iota(jnp.int32, (16, LANES), 0)

        def fill(values, spots):
            for c, value in enumerate(values):
                for buf in (red_a, red_b, black_a, black_b):
                    for half, to in spots:
                        buf[0, c, to, :] = value[8 * half : 8 * half + 8]

        def placed_rows(b, _):
            spots = [(half, pl.ds(pl.multiple_of(16 * b + EDGE + 8 * half, 8), 8)) for half in (0, 1)]
            fill(place_block(turns(skew, 16 * b, sub16), rotor, b, slots, tiles), spots)
            return 0

        lax.fori_loop(0, blocks, placed_rows, 0)
        for i, (small, spot) in enumerate(((small_prev, (1, pl.ds(0, 8))), (small_next, (0, pl.ds(EDGE + rows, 8))))):
            turn = f32(small[4 + tiles]).astype(jnp.int32)
            fill(place_block(turn, rotor, blocks + i, slots, tiles), [spot])

    @pl.when(g < 2)
    def load_all():
        load(g, True)

    @pl.when((g >= 2) & (g < LAG))
    def load_coefficients():
        load(g, False)

    def several(number, count):
        def body(i, _):
            step(number, count - 1 - i)
            return 0

        lax.fori_loop(0, count, body, 0)

    @pl.when(g == 1)
    def early():
        for copy in copies:
            copy.wait()
        several(1, 1)
        several(2, 2)

    @pl.when(g == 2)
    def middle():
        several(3, 3)

    @pl.when(g >= 3)
    def late():
        step(4, 6 - g)


def relax(rotor, skew_list, small_prev, small_next, from_left, from_right, from_prev, from_next, field, sigma, current):
    layers, rows, cols = field.shape
    pairs, tiles, slots = layers // 2, cols // LANES, len(rotor)
    plane = (tiles + 1, rows + 2 * EDGE, LANES)
    anywhere = pl.BlockSpec(memory_space=pl.ANY)

    def whole(array):
        zeros = (0,) * array.ndim
        return pl.BlockSpec(array.shape, lambda g: zeros)

    def specs(field_at, rest_at):
        halo = pl.BlockSpec((2, 1, 16, cols), lambda g: (0, rest_at(g), 0, 0))
        rest = pl.BlockSpec((2, rows, cols), lambda g: (rest_at(g), 0, 0))
        mine = pl.BlockSpec((2, rows, cols), lambda g: (field_at(g), 0, 0))
        return [whole(a) for a in ins[:4]] + [halo, halo, mine, rest, rest]

    def scratch(states, coefs):
        return (
            [pltpu.VMEM((states, *plane), jnp.float32)] * 4
            + [pltpu.VMEM((coefs, *plane), jnp.float32)] * 4
            + [pltpu.VMEM((2, 3, rows // 16 + 2, 8, LANES), jnp.float32), pltpu.SemaphoreType.DMA((3,))]
        )

    ins = [small_prev, small_next, from_left, from_right, from_prev, from_next, field, sigma, current]
    params = pltpu.CompilerParams(vmem_limit_bytes=VMEM_BYTES)
    result = jax.ShapeDtypeStruct(field.shape, jnp.float32)
    kept = jax.ShapeDtypeStruct((2, *plane), jnp.float32)
    cost = pl.CostEstimate(flops=0, bytes_accessed=64 << 20, transcendentals=0)

    def down(g):
        return pairs - 1 - g

    out, *saved = pl.pallas_call(
        functools.partial(upper_kernel, pairs=pairs, rows=rows, tiles=tiles),
        grid=(pairs,),
        in_specs=specs(down, down),
        out_specs=[pl.BlockSpec((2, rows, cols), lambda g: (jnp.minimum(pairs - 1, pairs + LAG - 1 - g), 0, 0))]
        + [anywhere] * 3,
        out_shape=[result, kept, kept, kept],
        scratch_shapes=scratch(pairs + 2, pairs),
        compiler_params=params,
        cost_estimate=cost,
        name="upper",
    )(*ins)
    return pl.pallas_call(
        functools.partial(lower_kernel, slots=slots, pairs=pairs, rows=rows, tiles=tiles),
        grid=(2 * LAG - 1,),
        in_specs=[anywhere] * 4
        + [pl.BlockSpec(memory_space=pltpu.SMEM)]
        + [whole(a) for a in rotor]
        + specs(lambda g: jnp.minimum(g, 1), lambda g: jnp.minimum(g, LAG - 1)),
        out_specs=pl.BlockSpec((2, rows, cols), lambda g: (jnp.minimum(LAG - 1, 2 * LAG - 2 - g), 0, 0)),
        out_shape=result,
        scratch_shapes=scratch(LAG + 2, LAG),
        input_output_aliases={0: 0},
        compiler_params=params,
        name="lower",
    )(out, *saved, skew_list, *rotor, *ins)


def moved(value, axis, steps):
    count = lax.axis_size(axis)
    return lax.ppermute(value, axis, [(i, (i + steps) % count) for i in range(count)])


def local(field, sigma, current, rotor_cycle, skew_list):
    to_left, to_right = pack_cols(field, sigma, current)
    from_left, from_right = moved(to_right, "az", 1), moved(to_left, "az", -1)
    to_prev, to_next = pack_rows(field, sigma, current, to_left)
    from_prev, from_next = moved(to_next, "ta", 1), moved(to_prev, "ta", -1)
    small_to_prev, small_to_next = pack_small(rotor_cycle, skew_list, from_left, from_right)
    small_prev, small_next = moved(small_to_next, "ta", 1), moved(small_to_prev, "ta", -1)
    rotor = pack_rotor(rotor_cycle, small_prev, small_next)
    rotor = [rotor] + [moved(rotor, "az", s) for s in range(1, lax.axis_size("az"))]
    return relax(
        rotor, skew_list, small_prev, small_next, from_left, from_right, from_prev, from_next, field, sigma, current
    )


def solution(mesh):
    placed = (P(None, "ta", "az"), P(None, "ta", "az"), P(None, "ta", "az"), P("ta", "az"), P("ta"))
    return jax.shard_map(
        local, mesh=mesh, in_specs=placed, out_specs=P(None, "ta", "az"), check_vma=False
    )
```

time: 63.8 us -> 70.6 us (1.11)
  Pallas kernels: 36.8 us -> 45.3 us
  waiting for transfers between devices: 11.3 us -> 5.72 us
  local copies, waits for them, and re-layouts: 2.33 us -> 4.37 us
  starting transfers between devices: 13 us -> 14.7 us
    pallas_call x4 -> x5, Pallas kernels: 33.4 us -> 41.9 us  [the longest x1 21.5 us: relax(): pl.pallas_call(functools.partial(upper_kernel, pairs=pairs, rows=rows, ti...]
    ppermute x7 -> x9, waiting for transfers between devices: 11.3 us -> 5.72 us  [moved(): lax.ppermute(value, axis, [(i, (i + steps) % count) for i in range(count)])]
    unnamed x20 -> x22, local copies, waits for them, and re-layouts: 2.33 us -> 4.37 us
    ppermute x7 -> x9, starting transfers between devices: 13 us -> 14.7 us  [moved(): lax.ppermute(value, axis, [(i, (i + steps) % count) for i in range(count)])]
  transfers between devices with their start and end apart: 7 -> 9, of which waited for: 2 -> 3; matrix products, arithmetic and copies ran while one was open for 0% -> 0% of each run, Pallas kernels for 6% -> 35%
where the time goes in v6:
time: 70.6 us; the launch traced here: 70.2 us
  Pallas kernels  45.3 us (64%)
  starting transfers between devices  14.7 us (21%)
  waiting for transfers between devices  5.72 us (8%)
  local copies, waits for them, and re-layouts  4.37 us (6%)
    pallas_call x1, Pallas kernels, relax(): pl.pallas_call(functools.partial(upper_kernel, pairs=pairs, rows=rows, ti...  21.5 us
    ppermute x9, starting transfers between devices, moved(): lax.ppermute(value, axis, [(i, (i + steps) % count) for i in range(count)])  14.7 us
    pallas_call x1, Pallas kernels, relax(): pl.pallas_call(functools.partial(lower_kernel, slots=slots, pairs=pairs,...  12.8 us
    ppermute x9, waiting for transfers between devices, moved(): lax.ppermute(value, axis, [(i, (i + steps) % count) for i in range(count)])  5.72 us
    unnamed x22, local copies, waits for them, and re-layouts  4.37 us
    pallas_call x1, Pallas kernels, pack_cols(): pl.pallas_call(functools.partial(cols_kernel, pairs=pairs, blocks=part),...  4.37 us
    pallas_call x1, Pallas kernels, pack_rows(): pl.pallas_call(functools.partial(rows_kernel, pairs=pairs, tiles=tiles),...  3.38 us
    pallas_call x1, Pallas kernels, pack_rotor(): pl.pallas_call(functools.partial(rotor_kernel, blocks=blocks, tiles=tiles...  1.78 us
  transfers between devices with their start and end apart: 9, of which 3 were waited for; matrix products, arithmetic and copies ran while one was open for 0% of the time, Pallas kernels for 35%

profile of v6, /device:TPU:0, one launch (start us, length us, event | category | flops | bytes accessed | tf_op | source)
XLA Modules:
  0.0 70.2 jit_solution(14023654975697569809)
XLA Ops:
  0.0 4.4 %pack_cols.1 = (bf16[8,2,16,128]{3,2,1,0:T(8,128)(2,1)}, bf16[8,2,16,128]{3,2,1,0:T(8,128)(2,1)}) custom-call(f32[16,128,1024]{2,1,0:T(8,128)} %refs_15_.1, f32[16,128,1024]{2,1,0:T(8,128)} %refs_15_.1, bf16[16,128,1024]{2,1,0:T(8,128)(2,1)} %refs_16_.1, bf16[16,128,1024]{2,1,0:T(8,128)(2,1)} %refs_16_.1, bf16[16,128,1024]{2,1,0:T(8,128)(2,1)} %refs_17_.1, ...), custom_call_target="tpu_custom_call" | custom-call | bytes 16777216 | tf_op jit(solution)/shard_map/pack_cols/pallas_call | solution.py:137
  4.4 0.0 copy-start.10
  4.4 0.0 copy-start.9
  4.4 3.4 %pack_rows.1 = (bf16[2,8,16,1024]{3,2,1,0:T(8,128)(2,1)}, bf16[2,8,16,1024]{3,2,1,0:T(8,128)(2,1)}) custom-call(f32[16,128,1024]{2,1,0:T(8,128)} %refs_15_.1, f32[16,128,1024]{2,1,0:T(8,128)} %refs_15_.1, bf16[16,128,1024]{2,1,0:T(8,128)(2,1)} %refs_16_.1, bf16[16,128,1024]{2,1,0:T(8,128)(2,1)} %refs_16_.1, bf16[16,128,1024]{2,1,0:T(8,128)(2,1)} %refs_17_.1, ...), custom_call_target="tpu_custom_call" | custom-call | bytes 12582912 | tf_op jit(solution)/shard_map/pack_rows/pallas_call | solution.py:118
  7.8 0.5 collective-permute-start.4
  8.2 4.0 %collective-permute-start.5 = (bf16[2,8,16,1024]{3,2,1,0:T(8,128)(2,1)}, bf16[2,8,16,1024]{3,2,1,0:T(8,128)(2,1)S(1)}, u32[]{:S(2)}, u32[]{:S(2)}) collective-permute-start(bf16[2,8,16,1024]{3,2,1,0:T(8,128)(2,1)} %get-tuple-element.20), channel_id=1, source_target_pairs={{0,7},{1,0},{2,1},{3,2},{4,3},{5,4},{6,5},{7,6},{8,15},{9,8},{10,9... | collective-permute-start | bytes 1572872 | tf_op jit(solution)/shard_map/ppermute | solution.py:520
  12.3 0.0 copy-done.10
  12.3 2.0 %collective-permute-start = (bf16[8,2,16,128]{3,2,1,0:T(8,128)(2,1)S(1)}, bf16[8,2,16,128]{3,2,1,0:T(8,128)(2,1)S(1)}, u32[]{:S(2)}, u32[]{:S(2)}) collective-permute-start(bf16[8,2,16,128]{3,2,1,0:T(8,128)(2,1)S(1)} %copy-done.10), channel_id=1, source_target_pairs={{0,8},{8,16},{16,24},{24,0},{1,9},{9,17},{17,25},{25,1},{2,10},{10... | collective-permute-start | bytes 196616 | tf_op jit(solution)/shard_map/ppermute | solution.py:520
  14.3 0.0 copy-done.9
  14.3 1.0 %collective-permute-start.1 = (bf16[8,2,16,128]{3,2,1,0:T(8,128)(2,1)S(1)}, bf16[8,2,16,128]{3,2,1,0:T(8,128)(2,1)S(1)}, u32[]{:S(2)}, u32[]{:S(2)}) collective-permute-start(bf16[8,2,16,128]{3,2,1,0:T(8,128)(2,1)S(1)} %copy-done.9), channel_id=1, source_target_pairs={{0,24},{8,0},{16,8},{24,16},{1,25},{9,1},{17,9},{25,17},{2,26},{10... | collective-permute-start | bytes 196616 | tf_op jit(solution)/shard_map/ppermute | solution.py:520
  15.3 2.2 %collective-permute-done.l_near.l_far.refs_2_.refs_11_ = bf16[8,2,16,128]{3,2,1,0:T(8,128)(2,1)S(1)} collective-permute-done((bf16[8,2,16,128]{3,2,1,0:T(8,128)(2,1)S(1)}, bf16[8,2,16,128]{3,2,1,0:T(8,128)(2,1)S(1)}, u32[]{:S(2)}, u32[]{:S(2)}) %collective-permute-start) | collective-permute-done | bytes 65568 | tf_op jit(solution)/shard_map/ppermute | solution.py:520
  17.5 0.0 copy-start.2
  17.5 1.2 %collective-permute-done.1.e_near.e_far.refs_3_.refs_12_ = bf16[8,2,16,128]{3,2,1,0:T(8,128)(2,1)S(1)} collective-permute-done((bf16[8,2,16,128]{3,2,1,0:T(8,128)(2,1)S(1)}, bf16[8,2,16,128]{3,2,1,0:T(8,128)(2,1)S(1)}, u32[]{:S(2)}, u32[]{:S(2)}) %collective-permute-start.1) | collective-permute-done | bytes 65568 | tf_op jit(solution)/shard_map/ppermute | solution.py:520
  18.7 0.0 copy-done.2
  18.7 0.0 copy-start.3
  18.7 0.6 copy-done.3
  19.3 1.5 %pack_small.1 = (bf16[13,16,128]{2,1,0:T(8,128)(2,1)}, bf16[13,16,128]{2,1,0:T(8,128)(2,1)}) custom-call(s32[128]{0:T(128)} %refs_4_.1, bf16[128,1024]{1,0:T(8,128)(2,1)} %rotor.1, bf16[128,1024]{1,0:T(8,128)(2,1)} %rotor.1, bf16[8,2,16,128]{3,2,1,0:T(8,128)(2,1)} %copy-done.2, bf16[8,2,16,128]{3,2,1,0:T(8,128)(2,1)} %copy-done.2, ...), custom_call_target="tpu_custom_call" | custom-call | tf_op jit(solution)/shard_map/pack_small/pallas_call | solution.py:176
  20.8 0.0 collective-permute-start.2
  20.8 3.5 %collective-permute-start.3 = (bf16[13,16,128]{2,1,0:T(8,128)(2,1)}, bf16[13,16,128]{2,1,0:T(8,128)(2,1)S(1)}, u32[]{:S(2)}, u32[]{:S(2)}) collective-permute-start(bf16[13,16,128]{2,1,0:T(8,128)(2,1)} %get-tuple-element.18), channel_id=1, source_target_pairs={{0,7},{1,0},{2,1},{3,2},{4,3},{5,4},{6,5},{7,6},{8,15},{9,8},{10,9... | collective-permute-start | bytes 159752 | tf_op jit(solution)/shard_map/ppermute | solution.py:520
  24.3 2.3 %collective-permute-done.2.refs_0_.small_prev.refs_9_ = bf16[13,16,128]{2,1,0:T(8,128)(2,1)S(1)} collective-permute-done((bf16[13,16,128]{2,1,0:T(8,128)(2,1)}, bf16[13,16,128]{2,1,0:T(8,128)(2,1)S(1)}, u32[]{:S(2)}, u32[]{:S(2)}) %collective-permute-start.2) | collective-permute-done | bytes 53280 | tf_op jit(solution)/shard_map/ppermute | solution.py:520
  26.6 0.0 copy-start.4
  26.6 0.0 collective-permute-done.3.refs_1_.small_next.refs_10_
  26.6 0.6 copy-done.4
  27.2 0.0 copy-start.5
  27.2 0.6 copy-done.5
  27.9 1.8 %pack_rotor.1.refs_5_ = bf16[10,8,16,128]{3,2,1,0:T(8,128)(2,1)} custom-call(bf16[128,1024]{1,0:T(8,128)(2,1)} %rotor.1, bf16[13,16,128]{2,1,0:T(8,128)(2,1)} %copy-done.4, bf16[13,16,128]{2,1,0:T(8,128)(2,1)} %copy-done.5), custom_call_target="tpu_custom_call" | custom-call | tf_op jit(solution)/shard_map/pack_rotor/pallas_call | solution.py:200
  29.6 2.1 %collective-permute-start.8 = (bf16[10,8,16,128]{3,2,1,0:T(8,128)(2,1)}, bf16[10,8,16,128]{3,2,1,0:T(8,128)(2,1)S(1)}, u32[]{:S(2)}, u32[]{:S(2)}) collective-permute-start(bf16[10,8,16,128]{3,2,1,0:T(8,128)(2,1)} %pack_rotor.1.refs_5_), channel_id=1, source_target_pairs={{0,24},{8,0},{16,8},{24,16},{1,25},{9,1},{17,9},{25,17},{2,26},{10... | collective-permute-start | bytes 983048 | tf_op jit(solution)/shard_map/ppermute | solution.py:520
  31.7 1.6 %collective-permute-start.7 = (bf16[10,8,16,128]{3,2,1,0:T(8,128)(2,1)}, bf16[10,8,16,128]{3,2,1,0:T(8,128)(2,1)S(1)}, u32[]{:S(2)}, u32[]{:S(2)}) collective-permute-start(bf16[10,8,16,128]{3,2,1,0:T(8,128)(2,1)} %pack_rotor.1.refs_5_), channel_id=1, source_target_pairs={{0,16},{8,24},{16,0},{24,8},{1,17},{9,25},{17,1},{25,9},{2,18},{10... | collective-permute-start | bytes 983048 | tf_op jit(solution)/shard_map/ppermute | solution.py:520
  33.3 0.0 collective-permute-start.6
  33.3 0.0 collective-permute-done.4.refs_4_.refs_13_
  33.3 0.0 copy-start
  33.3 0.0 collective-permute-done.5.refs_5_.refs_14_
  33.4 0.8 %copy-done = bf16[2,8,16,1024]{3,2,1,0:T(8,128)(2,1)} copy-done((bf16[2,8,16,1024]{3,2,1,0:T(8,128)(2,1)}, bf16[2,8,16,1024]{3,2,1,0:T(8,128)(2,1)S(1)}, u32[]{:S(2)}) %copy-start) | copy-done | bytes 524312
  34.1 0.0 copy-start.1
  34.1 0.8 %copy-done.1 = bf16[2,8,16,1024]{3,2,1,0:T(8,128)(2,1)} copy-done((bf16[2,8,16,1024]{3,2,1,0:T(8,128)(2,1)}, bf16[2,8,16,1024]{3,2,1,0:T(8,128)(2,1)S(1)}, u32[]{:S(2)}) %copy-start.1) | copy-done | bytes 524312
  34.9 21.5 %upper.1 = (f32[16,128,1024]{2,1,0:T(8,128)}, f32[2,9,144,128]{3,2,1,0:T(8,128)}, f32[2,9,144,128]{3,2,1,0:T(8,128)}, f32[2,9,144,128]{3,2,1,0:T(8,128)}) custom-call(bf16[13,16,128]{2,1,0:T(8,128)(2,1)} %copy-done.4, bf16[13,16,128]{2,1,0:T(8,128)(2,1)} %copy-done.5, bf16[8,2,16,128]{3,2,1,0:T(8,128)(2,1)} %copy-done.2, bf16[8,2,16,128]{3,2,1,0:T(8,128)(2,1)} %copy-done.3, ...), custom_call_target="tpu_custom_call" | custom-call | bytes 67108864 | tf_op jit(solution)/shard_map/upper/pallas_call | solution.py:490
  56.4 0.0 collective-permute-done.8.refs_8_
  56.4 0.0 copy-start.6
  56.4 0.0 collective-permute-done.7.refs_7_
  56.4 0.0 copy-start.7
  56.4 0.0 collective-permute-done.6.refs_6_
  56.5 0.0 copy-start.8
  56.5 0.7 copy-done.6
  57.1 0.1 copy-done.7
  57.3 0.1 copy-done.8
  57.4 12.8 %lower.1 = f32[16,128,1024]{2,1,0:T(8,128)} custom-call(f32[16,128,1024]{2,1,0:T(8,128)} %get-tuple-element.21.refs_0_, f32[2,9,144,128]{3,2,1,0:T(8,128)} %get-tuple-element.22.refs_1_, f32[2,9,144,128]{3,2,1,0:T(8,128)} %get-tuple-element.23.refs_2_, f32[2,9,144,128]{3,2,1,0:T(8,128)} %get-tuple-element.24.refs_3_, ...), custom_call_target="tpu_custom_call", output_to_operand_aliasing={{}: (0, {})} | custom-call | tf_op jit(solution)/shard_map/lower/pallas_call | solution.py:502
Async XLA Ops:
  4.4 7.9 %copy-start.10 = (bf16[8,2,16,128]{3,2,1,0:T(8,128)(2,1)S(1)}, bf16[8,2,16,128]{3,2,1,0:T(8,128)(2,1)}, u32[]{:S(2)}) copy-start(bf16[8,2,16,128]{3,2,1,0:T(8,128)(2,1)} %get-tuple-element.15) | copy-start | bytes 196612
  4.4 9.9 %copy-start.9 = (bf16[8,2,16,128]{3,2,1,0:T(8,128)(2,1)S(1)}, bf16[8,2,16,128]{3,2,1,0:T(8,128)(2,1)}, u32[]{:S(2)}) copy-start(bf16[8,2,16,128]{3,2,1,0:T(8,128)(2,1)} %get-tuple-element.16.after) | copy-start | bytes 196612
  7.8 25.6 %collective-permute-start.4 = (bf16[2,8,16,1024]{3,2,1,0:T(8,128)(2,1)}, bf16[2,8,16,1024]{3,2,1,0:T(8,128)(2,1)S(1)}, u32[]{:S(2)}, u32[]{:S(2)}) collective-permute-start(bf16[2,8,16,1024]{3,2,1,0:T(8,128)(2,1)} %get-tuple-element.19), channel_id=1, source_target_pairs={{0,1},{1,2},{2,3},{3,4},{4,5},{5,6},{6,7},{7,0},{8,9},{9,10},{10,1... | collective-permute-start | bytes 1572872 | tf_op jit(solution)/shard_map/ppermute | solution.py:520
  8.2 25.1 %collective-permute-start.5 = (bf16[2,8,16,1024]{3,2,1,0:T(8,128)(2,1)}, bf16[2,8,16,1024]{3,2,1,0:T(8,128)(2,1)S(1)}, u32[]{:S(2)}, u32[]{:S(2)}) collective-permute-start(bf16[2,8,16,1024]{3,2,1,0:T(8,128)(2,1)} %get-tuple-element.20), channel_id=1, source_target_pairs={{0,7},{1,0},{2,1},{3,2},{4,3},{5,4},{6,5},{7,6},{8,15},{9,8},{10,9... | collective-permute-start | bytes 1572872 | tf_op jit(solution)/shard_map/ppermute | solution.py:520
  12.3 5.2 %collective-permute-start = (bf16[8,2,16,128]{3,2,1,0:T(8,128)(2,1)S(1)}, bf16[8,2,16,128]{3,2,1,0:T(8,128)(2,1)S(1)}, u32[]{:S(2)}, u32[]{:S(2)}) collective-permute-start(bf16[8,2,16,128]{3,2,1,0:T(8,128)(2,1)S(1)} %copy-done.10), channel_id=1, source_target_pairs={{0,8},{8,16},{16,24},{24,0},{1,9},{9,17},{17,25},{25,1},{2,10},{10... | collective-permute-start | bytes 196616 | tf_op jit(solution)/shard_map/ppermute | solution.py:520
  14.3 4.4 %collective-permute-start.1 = (bf16[8,2,16,128]{3,2,1,0:T(8,128)(2,1)S(1)}, bf16[8,2,16,128]{3,2,1,0:T(8,128)(2,1)S(1)}, u32[]{:S(2)}, u32[]{:S(2)}) collective-permute-start(bf16[8,2,16,128]{3,2,1,0:T(8,128)(2,1)S(1)} %copy-done.9), channel_id=1, source_target_pairs={{0,24},{8,0},{16,8},{24,16},{1,25},{9,1},{17,9},{25,17},{2,26},{10... | collective-permute-start | bytes 196616 | tf_op jit(solution)/shard_map/ppermute | solution.py:520
  17.5 1.2 %copy-start.2 = (bf16[8,2,16,128]{3,2,1,0:T(8,128)(2,1)}, bf16[8,2,16,128]{3,2,1,0:T(8,128)(2,1)S(1)}, u32[]{:S(2)}) copy-start(bf16[8,2,16,128]{3,2,1,0:T(8,128)(2,1)S(1)} %collective-permute-done.l_near.l_far.refs_2_.refs_11_) | copy-start | bytes 196612
  18.7 0.6 copy-start.3
  20.8 5.8 %collective-permute-start.2 = (bf16[13,16,128]{2,1,0:T(8,128)(2,1)}, bf16[13,16,128]{2,1,0:T(8,128)(2,1)S(1)}, u32[]{:S(2)}, u32[]{:S(2)}) collective-permute-start(bf16[13,16,128]{2,1,0:T(8,128)(2,1)} %get-tuple-element.17), channel_id=1, source_target_pairs={{0,1},{1,2},{2,3},{3,4},{4,5},{5,6},{6,7},{7,0},{8,9},{9,10},{10,1... | collective-permute-start | bytes 159752 | tf_op jit(solution)/shard_map/ppermute | solution.py:520
  20.8 5.8 %collective-permute-start.3 = (bf16[13,16,128]{2,1,0:T(8,128)(2,1)}, bf16[13,16,128]{2,1,0:T(8,128)(2,1)S(1)}, u32[]{:S(2)}, u32[]{:S(2)}) collective-permute-start(bf16[13,16,128]{2,1,0:T(8,128)(2,1)} %get-tuple-element.18), channel_id=1, source_target_pairs={{0,7},{1,0},{2,1},{3,2},{4,3},{5,4},{6,5},{7,6},{8,15},{9,8},{10,9... | collective-permute-start | bytes 159752 | tf_op jit(solution)/shard_map/ppermute | solution.py:520
  26.6 0.6 copy-start.4
  27.2 0.6 copy-start.5
  29.6 26.8 %collective-permute-start.8 = (bf16[10,8,16,128]{3,2,1,0:T(8,128)(2,1)}, bf16[10,8,16,128]{3,2,1,0:T(8,128)(2,1)S(1)}, u32[]{:S(2)}, u32[]{:S(2)}) collective-permute-start(bf16[10,8,16,128]{3,2,1,0:T(8,128)(2,1)} %pack_rotor.1.refs_5_), channel_id=1, source_target_pairs={{0,24},{8,0},{16,8},{24,16},{1,25},{9,1},{17,9},{25,17},{2,26},{10... | collective-permute-start | bytes 983048 | tf_op jit(solution)/shard_map/ppermute | solution.py:520
  31.7 24.7 %collective-permute-start.7 = (bf16[10,8,16,128]{3,2,1,0:T(8,128)(2,1)}, bf16[10,8,16,128]{3,2,1,0:T(8,128)(2,1)S(1)}, u32[]{:S(2)}, u32[]{:S(2)}) collective-permute-start(bf16[10,8,16,128]{3,2,1,0:T(8,128)(2,1)} %pack_rotor.1.refs_5_), channel_id=1, source_target_pairs={{0,16},{8,24},{16,0},{24,8},{1,17},{9,25},{17,1},{25,9},{2,18},{10... | collective-permute-start | bytes 983048 | tf_op jit(solution)/shard_map/ppermute | solution.py:520
  33.3 23.1 %collective-permute-start.6 = (bf16[10,8,16,128]{3,2,1,0:T(8,128)(2,1)}, bf16[10,8,16,128]{3,2,1,0:T(8,128)(2,1)S(1)}, u32[]{:S(2)}, u32[]{:S(2)}) collective-permute-start(bf16[10,8,16,128]{3,2,1,0:T(8,128)(2,1)} %pack_rotor.1.refs_5_), channel_id=1, source_target_pairs={{0,8},{8,16},{16,24},{24,0},{1,9},{9,17},{17,25},{25,1},{2,10},{10... | collective-permute-start | bytes 983048 | tf_op jit(solution)/shard_map/ppermute | solution.py:520
  33.3 0.8 %copy-start = (bf16[2,8,16,1024]{3,2,1,0:T(8,128)(2,1)}, bf16[2,8,16,1024]{3,2,1,0:T(8,128)(2,1)S(1)}, u32[]{:S(2)}) copy-start(bf16[2,8,16,1024]{3,2,1,0:T(8,128)(2,1)S(1)} %collective-permute-done.4.refs_4_.refs_13_) | copy-start | bytes 1572868
  34.1 0.8 %copy-start.1 = (bf16[2,8,16,1024]{3,2,1,0:T(8,128)(2,1)}, bf16[2,8,16,1024]{3,2,1,0:T(8,128)(2,1)S(1)}, u32[]{:S(2)}) copy-start(bf16[2,8,16,1024]{3,2,1,0:T(8,128)(2,1)S(1)} %collective-permute-done.5.refs_5_.refs_14_) | copy-start | bytes 1572868
  56.4 0.7 %copy-start.6 = (bf16[10,8,16,128]{3,2,1,0:T(8,128)(2,1)}, bf16[10,8,16,128]{3,2,1,0:T(8,128)(2,1)S(1)}, u32[]{:S(2)}) copy-start(bf16[10,8,16,128]{3,2,1,0:T(8,128)(2,1)S(1)} %collective-permute-done.8.refs_8_) | copy-start | bytes 983044
  56.4 0.8 %copy-start.7 = (bf16[10,8,16,128]{3,2,1,0:T(8,128)(2,1)}, bf16[10,8,16,128]{3,2,1,0:T(8,128)(2,1)S(1)}, u32[]{:S(2)}) copy-start(bf16[10,8,16,128]{3,2,1,0:T(8,128)(2,1)S(1)} %collective-permute-done.7.refs_7_) | copy-start | bytes 983044
  56.5 0.9 %copy-start.8 = (bf16[10,8,16,128]{3,2,1,0:T(8,128)(2,1)}, bf16[10,8,16,128]{3,2,1,0:T(8,128)(2,1)S(1)}, u32[]{:S(2)}) copy-start(bf16[10,8,16,128]{3,2,1,0:T(8,128)(2,1)S(1)} %collective-permute-done.6.refs_6_) | copy-start | bytes 983044

commit v7 on v5

--- a/solution.py
+++ b/solution.py
@@ -10,6 +10,7 @@
 LANES = 128
 EDGE = 8
 LAG = 4
+DEPTH = 4
 VMEM_BYTES = 60 * 1024 * 1024
 
 
@@ -245,7 +246,7 @@
 
 def relax_kernel(placed, small_prev, small_next, from_left, from_right, from_prev, from_next,
      u_ref, s_ref, j_ref, out_ref,
-     red_a, red_b, black_a, black_b, sig_r, sig_b, cur_r, cur_b, side, *, pairs, rows, tiles):
+     red_a, red_b, black_a, black_b, sig_r, sig_b, cur_r, cur_b, side, u_buf, s_buf, j_buf, sem, *, pairs, rows, tiles):
     g = pl.program_id(0)
     blocks = rows // 16
     even8 = checker(8)
@@ -254,8 +255,20 @@
     lane_first = lane == 0
     lane_last = lane == LANES - 1
 
+    def fetch(m):
+        slot = lax.rem(m, DEPTH)
+        return [
+            pltpu.make_async_copy(ref.at[2 * m + half], buf.at[slot, half], sem.at[slot, i, half])
+            for i, (ref, buf) in enumerate(((u_ref, u_buf), (s_ref, s_buf), (j_ref, j_buf)))
+            for half in (0, 1)
+        ]
+
     @pl.when(g == 0)
     def prologue():
+        for m in range(min(DEPTH, pairs)):
+            for copy in fetch(m):
+                copy.start()
+
         def fill(value, c, spots):
             zero = jnp.zeros((8, LANES), jnp.float32)
             for buf in (red_a, red_b, black_a, black_b):
@@ -296,6 +309,7 @@
     @pl.when(g < pairs)
     def load():
         m = g
+        slot = lax.rem(m, DEPTH)
         fields = ((red_a, sig_r, cur_r), (black_a, sig_b, cur_b))
         for colour in (0, 1):
             u_dst, s_dst, j_dst = fields[colour]
@@ -310,23 +324,31 @@
                 s_dst[m, c, pl.ds(EDGE + rows - 5, 8), :] = both[:8] * (1.0 / 48.0)
                 j_dst[m, c, pl.ds(EDGE + rows - 5, 8), :] = both[8:] * 0.25
 
+        for copy in fetch(m):
+            copy.wait()
+
         def own_rows(q, _):
             at = pl.ds(pl.multiple_of(16 * q, 16), 16)
             to = pl.ds(pl.multiple_of(16 * q + EDGE, 8), 16)
             for c in range(tiles):
                 cols = slice(c * LANES, (c + 1) * LANES)
-                a, b = u_ref[0, at, cols], u_ref[1, at, cols]
+                a, b = u_buf[slot, 0, at, cols], u_buf[slot, 1, at, cols]
                 red_a[m + 1, c, to, :] = jnp.where(even16, a, b)
                 black_a[m + 1, c, to, :] = jnp.where(even16, b, a)
-                a, b = f32(s_ref[0, at, cols]) * (1.0 / 48.0), f32(s_ref[1, at, cols]) * (1.0 / 48.0)
+                a, b = f32(s_buf[slot, 0, at, cols]) * (1.0 / 48.0), f32(s_buf[slot, 1, at, cols]) * (1.0 / 48.0)
                 sig_r[m, c, to, :] = jnp.where(even16, a, b)
                 sig_b[m, c, to, :] = jnp.where(even16, b, a)
-                a, b = f32(j_ref[0, at, cols]) * 0.25, f32(j_ref[1, at, cols]) * 0.25
+                a, b = f32(j_buf[slot, 0, at, cols]) * 0.25, f32(j_buf[slot, 1, at, cols]) * 0.25
                 cur_r[m, c, to, :] = jnp.where(even16, a, b)
                 cur_b[m, c, to, :] = jnp.where(even16, b, a)
             return 0
 
         lax.fori_loop(0, blocks, own_rows, 0)
+
+        @pl.when(m + DEPTH < pairs)
+        def fetch_more():
+            for copy in fetch(m + DEPTH):
+                copy.start()
 
         for colour in (0, 1):
             u_dst, s_dst, j_dst = fields[colour]
@@ -401,7 +423,7 @@
         return jnp.minimum(g, pairs - 1)
 
     halo = pl.BlockSpec((2, 1, 16, cols), lambda g: (0, coming(g), 0, 0))
-    block = pl.BlockSpec((2, rows, cols), lambda g: (coming(g), 0, 0))
+    block = pl.BlockSpec(memory_space=pl.ANY)
     fixed = [placed, small_prev, small_next]
     side = pl.BlockSpec((rows // 16, 2, 16, LANES), lambda g: (0, 0, 0, 0))
     state = pltpu.VMEM((pairs + 2, tiles + 1, ext, LANES), jnp.float32)
@@ -412,7 +434,13 @@
         in_specs=[whole(a) for a in fixed] + [side, side, halo, halo, block, block, block],
         out_specs=pl.BlockSpec((2, rows, cols), lambda g: (jnp.maximum(g - LAG, 0), 0, 0)),
         out_shape=jax.ShapeDtypeStruct(field.shape, jnp.float32),
-        scratch_shapes=[state] * 4 + [coef] * 4 + [pltpu.VMEM((2, 3, rows // 16 + 2, 8, LANES), jnp.float32)],
+        scratch_shapes=[state] * 4 + [coef] * 4 + [
+            pltpu.VMEM((2, 3, rows // 16 + 2, 8, LANES), jnp.float32),
+            pltpu.VMEM((DEPTH, 2, rows, cols), jnp.float32),
+            pltpu.VMEM((DEPTH, 2, rows, cols), jnp.bfloat16),
+            pltpu.VMEM((DEPTH, 2, rows, cols), jnp.bfloat16),
+            pltpu.SemaphoreType.DMA((DEPTH, 3, 2)),
+        ],
         compiler_params=pltpu.CompilerParams(vmem_limit_bytes=VMEM_BYTES),
         name="relax",
     )(*fixed, from_left, from_right, from_prev, from_next, field, sigma, current)

time: 63.8 us -> 65 us (1.019)
  Pallas kernels: 36.8 us -> 38 us
    pallas_call x1, Pallas kernels: 24.9 us -> 26.1 us  [relax(): pl.pallas_call(functools.partial(relax_kernel, pairs=pairs, rows=rows, ti...]
where the time goes in v7:
time: 65 us; the launch traced here: 64.7 us
  Pallas kernels  38 us (58%)
  starting transfers between devices  13 us (20%)
  waiting for transfers between devices  11.3 us (17%)
  local copies, waits for them, and re-layouts  2.33 us (4%)
    pallas_call x1, Pallas kernels, relax(): pl.pallas_call(functools.partial(relax_kernel, pairs=pairs, rows=rows, ti...  26.1 us
    ppermute x7, starting transfers between devices, moved(): lax.ppermute(value, axis, [(i, (i + steps) % count) for i in range(count)])  13 us
    ppermute x7, waiting for transfers between devices, moved(): lax.ppermute(value, axis, [(i, (i + steps) % count) for i in range(count)])  11.3 us
    pallas_call x1, Pallas kernels, pack_cols(): pl.pallas_call(functools.partial(cols_kernel, pairs=pairs, tiles=tiles, b...  4.43 us
    pallas_call x1, Pallas kernels, pack_rows(): pl.pallas_call(functools.partial(rows_kernel, pairs=pairs, tiles=tiles),...  3.41 us
    pallas_call x1, Pallas kernels, place_cycle(): pl.pallas_call(functools.partial(place_kernel, slots=len(rotor) + 2, rows...  2.39 us
    unnamed x20, local copies, waits for them, and re-layouts  2.33 us
    pallas_call x1, Pallas kernels, place_edges(): pl.pallas_call(functools.partial(place_edges_kernel, slots=slots, rows=ro...  1.63 us
  transfers between devices with their start and end apart: 7, of which 2 were waited for; matrix products, arithmetic and copies ran while one was open for 0% of the time, Pallas kernels for 6%

profile of v7, /device:TPU:0, one launch (start us, length us, event | category | flops | bytes accessed | tf_op | source)
XLA Modules:
  0.0 64.7 jit_solution(16718149253900710376)
XLA Ops:
  0.0 4.4 %pack_cols.1 = (bf16[8,10,16,128]{3,2,1,0:T(8,128)(2,1)}, bf16[8,10,16,128]{3,2,1,0:T(8,128)(2,1)}) custom-call(f32[16,128,1024]{2,1,0:T(8,128)} %u_ref.1, f32[16,128,1024]{2,1,0:T(8,128)} %u_ref.1, bf16[16,128,1024]{2,1,0:T(8,128)(2,1)} %s_ref.1, bf16[16,128,1024]{2,1,0:T(8,128)(2,1)} %s_ref.1, bf16[16,128,1024]{2,1,0:T(8,128)(2,1)} %j_ref.1, ...), custom_call_target="tpu_custom_call" | custom-call | bytes 16777216 | tf_op jit(solution)/shard_map/pack_cols/pallas_call | solution.py:142
  4.4 0.0 copy-start.9
  4.4 0.0 copy-start.6
  4.4 0.0 copy-start.2
  4.5 3.4 %pack_rows.1 = (bf16[2,8,16,1024]{3,2,1,0:T(8,128)(2,1)}, bf16[2,8,16,1024]{3,2,1,0:T(8,128)(2,1)}) custom-call(f32[16,128,1024]{2,1,0:T(8,128)} %u_ref.1, f32[16,128,1024]{2,1,0:T(8,128)} %u_ref.1, bf16[16,128,1024]{2,1,0:T(8,128)(2,1)} %s_ref.1, bf16[16,128,1024]{2,1,0:T(8,128)(2,1)} %s_ref.1, bf16[16,128,1024]{2,1,0:T(8,128)(2,1)} %j_ref.1, ...), custom_call_target="tpu_custom_call" | custom-call | bytes 12582912 | tf_op jit(solution)/shard_map/pack_rows/pallas_call | solution.py:123
  7.9 0.5 collective-permute-start.5
  8.3 4.0 %collective-permute-start.6 = (bf16[2,8,16,1024]{3,2,1,0:T(8,128)(2,1)}, bf16[2,8,16,1024]{3,2,1,0:T(8,128)(2,1)S(1)}, u32[]{:S(2)}, u32[]{:S(2)}) collective-permute-start(bf16[2,8,16,1024]{3,2,1,0:T(8,128)(2,1)} %get-tuple-element.16), channel_id=1, source_target_pairs={{0,7},{1,0},{2,1},{3,2},{4,3},{5,4},{6,5},{7,6},{8,15},{9,8},{10,9... | collective-permute-start | bytes 1572872 | tf_op jit(solution)/shard_map/ppermute | solution.py:451
  12.4 0.0 copy-done.9
  12.4 2.0 %collective-permute-start.1 = (bf16[8,10,16,128]{3,2,1,0:T(8,128)(2,1)S(1)}, bf16[8,10,16,128]{3,2,1,0:T(8,128)(2,1)S(1)}, u32[]{:S(2)}, u32[]{:S(2)}) collective-permute-start(bf16[8,10,16,128]{3,2,1,0:T(8,128)(2,1)S(1)} %copy-done.9), channel_id=1, source_target_pairs={{0,8},{8,16},{16,24},{24,0},{1,9},{9,17},{17,25},{25,1},{2,10},{10... | collective-permute-start | bytes 983048 | tf_op jit(solution)/shard_map/ppermute | solution.py:451
  14.4 0.0 copy-done.6
  14.4 1.0 %collective-permute-start.2 = (bf16[8,10,16,128]{3,2,1,0:T(8,128)(2,1)S(1)}, bf16[8,10,16,128]{3,2,1,0:T(8,128)(2,1)S(1)}, u32[]{:S(2)}, u32[]{:S(2)}) collective-permute-start(bf16[8,10,16,128]{3,2,1,0:T(8,128)(2,1)S(1)} %copy-done.6), channel_id=1, source_target_pairs={{0,24},{8,0},{16,8},{24,16},{1,25},{9,1},{17,9},{25,17},{2,26},{10... | collective-permute-start | bytes 983048 | tf_op jit(solution)/shard_map/ppermute | solution.py:451
  15.4 0.0 copy-done.2
  15.4 1.9 %collective-permute-start = (bf16[128,1024]{1,0:T(8,128)(2,1)S(1)}, bf16[128,1024]{1,0:T(8,128)(2,1)S(1)}, u32[]{:S(2)}, u32[]{:S(2)}) collective-permute-start(bf16[128,1024]{1,0:T(8,128)(2,1)S(1)} %copy-done.2), channel_id=1, source_target_pairs={{0,16},{8,24},{16,0},{24,8},{1,17},{9,25},{17,1},{25,9},{2,18},{10... | collective-permute-start | bytes 786440 | tf_op jit(solution)/shard_map/ppermute | solution.py:451
  17.3 9.8 %collective-permute-done.refs_1_.refs_5_ = bf16[128,1024]{1,0:T(8,128)(2,1)S(1)} collective-permute-done((bf16[128,1024]{1,0:T(8,128)(2,1)S(1)}, bf16[128,1024]{1,0:T(8,128)(2,1)S(1)}, u32[]{:S(2)}, u32[]{:S(2)}) %collective-permute-start) | collective-permute-done | bytes 262176 | tf_op jit(solution)/shard_map/ppermute | solution.py:451
  27.2 0.0 copy-start.3
  27.2 0.0 collective-permute-done.1.refs_2_.refs_6_.from_left
  27.2 0.0 copy-start
  27.2 1.5 %collective-permute-done.2.refs_3_.refs_7_.from_right = bf16[8,10,16,128]{3,2,1,0:T(8,128)(2,1)S(1)} collective-permute-done((bf16[8,10,16,128]{3,2,1,0:T(8,128)(2,1)S(1)}, bf16[8,10,16,128]{3,2,1,0:T(8,128)(2,1)S(1)}, u32[]{:S(2)}, u32[]{:S(2)}) %collective-permute-start.2) | collective-permute-done | bytes 327712 | tf_op jit(solution)/shard_map/ppermute | solution.py:451
  28.7 0.0 copy-done.3
  28.7 0.0 copy-done
  28.7 0.0 copy-start.1
  28.7 0.7 %copy-done.1 = bf16[8,10,16,128]{3,2,1,0:T(8,128)(2,1)} copy-done((bf16[8,10,16,128]{3,2,1,0:T(8,128)(2,1)}, bf16[8,10,16,128]{3,2,1,0:T(8,128)(2,1)S(1)}, u32[]{:S(2)}) %copy-start.1) | copy-done | bytes 327704
  29.4 1.6 %place_edges.1 = (bf16[13,16,128]{2,1,0:T(8,128)(2,1)}, bf16[13,16,128]{2,1,0:T(8,128)(2,1)}) custom-call(s32[128]{0:T(128)} %skew.3, bf16[128,1024]{1,0:T(8,128)(2,1)} %refs_0_.3, bf16[128,1024]{1,0:T(8,128)(2,1)} %copy-done.3, bf16[8,10,16,128]{3,2,1,0:T(8,128)(2,1)} %copy-done, bf16[8,10,16,128]{3,2,1,0:T(8,128)(2,1)} %copy-done.1, ...), custom_call_target="tpu_custom_call" | custom-call | bytes 1048576 | tf_op jit(solution)/shard_map/place_edges/pallas_call | solution.py:203
  31.0 0.0 collective-permute-start.3
  31.0 3.5 %collective-permute-start.4 = (bf16[13,16,128]{2,1,0:T(8,128)(2,1)}, bf16[13,16,128]{2,1,0:T(8,128)(2,1)S(1)}, u32[]{:S(2)}, u32[]{:S(2)}) collective-permute-start(bf16[13,16,128]{2,1,0:T(8,128)(2,1)} %get-tuple-element.13.refs_4_), channel_id=1, source_target_pairs={{0,7},{1,0},{2,1},{3,2},{4,3},{5,4},{6,5},{7,6},{8,15},{9,8},{10,9... | collective-permute-start | bytes 159752 | tf_op jit(solution)/shard_map/ppermute | solution.py:451
  34.6 2.4 %place_cycle.1.placed = bf16[9,128,128]{2,1,0:T(8,128)(2,1)} custom-call(s32[128]{0:T(128)} %skew.3, bf16[128,1024]{1,0:T(8,128)(2,1)} %refs_0_.3, bf16[128,1024]{1,0:T(8,128)(2,1)} %copy-done.3, bf16[8,10,16,128]{3,2,1,0:T(8,128)(2,1)} %copy-done, bf16[8,10,16,128]{3,2,1,0:T(8,128)(2,1)} %copy-done.1, bf16[13,16,128]{2,1,0:T(8,128)(2,1)} %get-tuple-element.13.refs_4_), custom_call_target="tpu_custom_call" | custom-call | bytes 4194304 | tf_op jit(solution)/shard_map/place_cycle/pallas_call | solution.py:233
  37.0 0.0 collective-permute-done.3.small_prev
  37.0 0.0 copy-start.7
  37.0 0.0 collective-permute-done.4.small_next
  37.0 0.0 copy-start.8
  37.0 0.0 collective-permute-done.5.from_prev
  37.0 0.0 copy-start.4
  37.0 0.0 collective-permute-done.6.from_next
  37.0 0.6 copy-done.7
  37.6 0.0 copy-done.8
  37.6 0.2 copy-done.4
  37.8 0.0 copy-start.5
  37.8 0.8 %copy-done.5 = bf16[2,8,16,1024]{3,2,1,0:T(8,128)(2,1)} copy-done((bf16[2,8,16,1024]{3,2,1,0:T(8,128)(2,1)}, bf16[2,8,16,1024]{3,2,1,0:T(8,128)(2,1)S(1)}, u32[]{:S(2)}) %copy-start.5) | copy-done | bytes 524312
  38.6 26.1 %relax.1 = f32[16,128,1024]{2,1,0:T(8,128)} custom-call(bf16[9,128,128]{2,1,0:T(8,128)(2,1)} %place_cycle.1.placed, bf16[13,16,128]{2,1,0:T(8,128)(2,1)} %copy-done.7, bf16[13,16,128]{2,1,0:T(8,128)(2,1)} %copy-done.8, bf16[8,10,16,128]{3,2,1,0:T(8,128)(2,1)} %copy-done, bf16[8,10,16,128]{3,2,1,0:T(8,128)(2,1)} %copy-done.1, ...), custom_call_target="tpu_custom_call" | custom-call | tf_op jit(solution)/shard_map/relax/pallas_call | solution.py:431
Async XLA Ops:
  4.4 7.9 %copy-start.9 = (bf16[8,10,16,128]{3,2,1,0:T(8,128)(2,1)S(1)}, bf16[8,10,16,128]{3,2,1,0:T(8,128)(2,1)}, u32[]{:S(2)}) copy-start(bf16[8,10,16,128]{3,2,1,0:T(8,128)(2,1)} %get-tuple-element.11) | copy-start | bytes 983044
  4.4 9.9 %copy-start.6 = (bf16[8,10,16,128]{3,2,1,0:T(8,128)(2,1)S(1)}, bf16[8,10,16,128]{3,2,1,0:T(8,128)(2,1)}, u32[]{:S(2)}) copy-start(bf16[8,10,16,128]{3,2,1,0:T(8,128)(2,1)} %get-tuple-element.12.after) | copy-start | bytes 983044
  4.4 10.9 %copy-start.2 = (bf16[128,1024]{1,0:T(8,128)(2,1)S(1)}, bf16[128,1024]{1,0:T(8,128)(2,1)}, u32[]{:S(2)}) copy-start(bf16[128,1024]{1,0:T(8,128)(2,1)} %refs_0_.3) | copy-start | bytes 786436
  7.9 29.1 %collective-permute-start.5 = (bf16[2,8,16,1024]{3,2,1,0:T(8,128)(2,1)}, bf16[2,8,16,1024]{3,2,1,0:T(8,128)(2,1)S(1)}, u32[]{:S(2)}, u32[]{:S(2)}) collective-permute-start(bf16[2,8,16,1024]{3,2,1,0:T(8,128)(2,1)} %get-tuple-element.15), channel_id=1, source_target_pairs={{0,1},{1,2},{2,3},{3,4},{4,5},{5,6},{6,7},{7,0},{8,9},{9,10},{10,1... | collective-permute-start | bytes 1572872 | tf_op jit(solution)/shard_map/ppermute | solution.py:451
  8.3 28.7 %collective-permute-start.6 = (bf16[2,8,16,1024]{3,2,1,0:T(8,128)(2,1)}, bf16[2,8,16,1024]{3,2,1,0:T(8,128)(2,1)S(1)}, u32[]{:S(2)}, u32[]{:S(2)}) collective-permute-start(bf16[2,8,16,1024]{3,2,1,0:T(8,128)(2,1)} %get-tuple-element.16), channel_id=1, source_target_pairs={{0,7},{1,0},{2,1},{3,2},{4,3},{5,4},{6,5},{7,6},{8,15},{9,8},{10,9... | collective-permute-start | bytes 1572872 | tf_op jit(solution)/shard_map/ppermute | solution.py:451
  12.4 14.8 %collective-permute-start.1 = (bf16[8,10,16,128]{3,2,1,0:T(8,128)(2,1)S(1)}, bf16[8,10,16,128]{3,2,1,0:T(8,128)(2,1)S(1)}, u32[]{:S(2)}, u32[]{:S(2)}) collective-permute-start(bf16[8,10,16,128]{3,2,1,0:T(8,128)(2,1)S(1)} %copy-done.9), channel_id=1, source_target_pairs={{0,8},{8,16},{16,24},{24,0},{1,9},{9,17},{17,25},{25,1},{2,10},{10... | collective-permute-start | bytes 983048 | tf_op jit(solution)/shard_map/ppermute | solution.py:451
  14.4 14.3 %collective-permute-start.2 = (bf16[8,10,16,128]{3,2,1,0:T(8,128)(2,1)S(1)}, bf16[8,10,16,128]{3,2,1,0:T(8,128)(2,1)S(1)}, u32[]{:S(2)}, u32[]{:S(2)}) collective-permute-start(bf16[8,10,16,128]{3,2,1,0:T(8,128)(2,1)S(1)} %copy-done.6), channel_id=1, source_target_pairs={{0,24},{8,0},{16,8},{24,16},{1,25},{9,1},{17,9},{25,17},{2,26},{10... | collective-permute-start | bytes 983048 | tf_op jit(solution)/shard_map/ppermute | solution.py:451
  15.4 11.8 %collective-permute-start = (bf16[128,1024]{1,0:T(8,128)(2,1)S(1)}, bf16[128,1024]{1,0:T(8,128)(2,1)S(1)}, u32[]{:S(2)}, u32[]{:S(2)}) collective-permute-start(bf16[128,1024]{1,0:T(8,128)(2,1)S(1)} %copy-done.2), channel_id=1, source_target_pairs={{0,16},{8,24},{16,0},{24,8},{1,17},{9,25},{17,1},{25,9},{2,18},{10... | collective-permute-start | bytes 786440 | tf_op jit(solution)/shard_map/ppermute | solution.py:451
  27.2 1.5 %copy-start.3 = (bf16[128,1024]{1,0:T(8,128)(2,1)}, bf16[128,1024]{1,0:T(8,128)(2,1)S(1)}, u32[]{:S(2)}) copy-start(bf16[128,1024]{1,0:T(8,128)(2,1)S(1)} %collective-permute-done.refs_1_.refs_5_) | copy-start | bytes 786436
  27.2 1.5 %copy-start = (bf16[8,10,16,128]{3,2,1,0:T(8,128)(2,1)}, bf16[8,10,16,128]{3,2,1,0:T(8,128)(2,1)S(1)}, u32[]{:S(2)}) copy-start(bf16[8,10,16,128]{3,2,1,0:T(8,128)(2,1)S(1)} %collective-permute-done.1.refs_2_.refs_6_.from_left) | copy-start | bytes 983044
  28.7 0.7 %copy-start.1 = (bf16[8,10,16,128]{3,2,1,0:T(8,128)(2,1)}, bf16[8,10,16,128]{3,2,1,0:T(8,128)(2,1)S(1)}, u32[]{:S(2)}) copy-start(bf16[8,10,16,128]{3,2,1,0:T(8,128)(2,1)S(1)} %collective-permute-done.2.refs_3_.refs_7_.from_right) | copy-start | bytes 983044
  31.0 5.9 %collective-permute-start.3 = (bf16[13,16,128]{2,1,0:T(8,128)(2,1)}, bf16[13,16,128]{2,1,0:T(8,128)(2,1)S(1)}, u32[]{:S(2)}, u32[]{:S(2)}) collective-permute-start(bf16[13,16,128]{2,1,0:T(8,128)(2,1)} %get-tuple-element.14), channel_id=1, source_target_pairs={{0,1},{1,2},{2,3},{3,4},{4,5},{5,6},{6,7},{7,0},{8,9},{9,10},{10,1... | collective-permute-start | bytes 159752 | tf_op jit(solution)/shard_map/ppermute | solution.py:451
  31.0 5.9 %collective-permute-start.4 = (bf16[13,16,128]{2,1,0:T(8,128)(2,1)}, bf16[13,16,128]{2,1,0:T(8,128)(2,1)S(1)}, u32[]{:S(2)}, u32[]{:S(2)}) collective-permute-start(bf16[13,16,128]{2,1,0:T(8,128)(2,1)} %get-tuple-element.13.refs_4_), channel_id=1, source_target_pairs={{0,7},{1,0},{2,1},{3,2},{4,3},{5,4},{6,5},{7,6},{8,15},{9,8},{10,9... | collective-permute-start | bytes 159752 | tf_op jit(solution)/shard_map/ppermute | solution.py:451
  37.0 0.6 copy-start.7
  37.0 0.6 copy-start.8
  37.0 0.8 %copy-start.4 = (bf16[2,8,16,1024]{3,2,1,0:T(8,128)(2,1)}, bf16[2,8,16,1024]{3,2,1,0:T(8,128)(2,1)S(1)}, u32[]{:S(2)}) copy-start(bf16[2,8,16,1024]{3,2,1,0:T(8,128)(2,1)S(1)} %collective-permute-done.5.from_prev) | copy-start | bytes 1572868
  37.8 0.8 %copy-start.5 = (bf16[2,8,16,1024]{3,2,1,0:T(8,128)(2,1)}, bf16[2,8,16,1024]{3,2,1,0:T(8,128)(2,1)S(1)}, u32[]{:S(2)}) copy-start(bf16[2,8,16,1024]{3,2,1,0:T(8,128)(2,1)S(1)} %collective-permute-done.6.from_next) | copy-start | bytes 1572868

commit v8 on v5

--- a/solution.py
+++ b/solution.py
@@ -293,6 +293,18 @@
         decode(blocks, small_prev[0:2], small_prev[2:4])
         decode(blocks + 1, small_next[0:2], small_next[2:4])
 
+        fields = ((red_a, sig_r, cur_r), (black_a, sig_b, cur_b))
+        for m in range(pairs):
+            for colour in (0, 1):
+                for item, dst in enumerate(fields[colour]):
+                    plane = m + 1 if item == 0 else m
+                    for w in (0, 1):
+                        turn = (2 * LANES + 124 - 4 * colour - 8 * (m + pairs * w)) % LANES
+                        for q in range(blocks):
+                            dst[plane, tiles, pl.ds(EDGE + 16 * q + 8 * w, 8), :] = pltpu.roll(side[colour, item, q], turn, 1)
+                        end, at = (blocks, 0) if w == 1 else (blocks + 1, EDGE + rows)
+                        dst[plane, tiles, pl.ds(at, 8), :] = pltpu.roll(side[colour, item, end], turn, 1)
+
     @pl.when(g < pairs)
     def load():
         m = g
@@ -328,18 +340,6 @@
 
         lax.fori_loop(0, blocks, own_rows, 0)
 
-        for colour in (0, 1):
-            u_dst, s_dst, j_dst = fields[colour]
-            for item, (dst, plane) in enumerate(((u_dst, m + 1), (s_dst, m), (j_dst, m))):
-                for w in (0, 1):
-                    turn = lax.rem(2 * LANES + 124 - 4 * colour - 8 * (m + pairs * w), LANES)
-                    for q in range(blocks):
-                        dst[plane, tiles, pl.ds(EDGE + 16 * q + 8 * w, 8), :] = pltpu.roll(side[colour, item, q], turn, 1)
-                    if w == 1:
-                        dst[plane, tiles, pl.ds(0, 8), :] = pltpu.roll(side[colour, item, blocks], turn, 1)
-                    else:
-                        dst[plane, tiles, pl.ds(EDGE + rows, 8), :] = pltpu.roll(side[colour, item, blocks + 1], turn, 1)
-
     def half_step(m, colour, own, other, sig, cur, start, count, outputs, write):
         def row_tile(at):
             centre = [other[m + 1, c, pl.ds(at, 8), :] for c in range(tiles + 1)]

time: 63.8 us -> 63.5 us (level)
  no operation moved by 1% of the time
where the time goes in v8:
time: 63.5 us; the launch traced here: 63.1 us
  Pallas kernels  36.4 us (57%)
  starting transfers between devices  13 us (20%)
  waiting for transfers between devices  11.3 us (18%)
  local copies, waits for them, and re-layouts  2.33 us (4%)
    pallas_call x1, Pallas kernels, relax(): pl.pallas_call(functools.partial(relax_kernel, pairs=pairs, rows=rows, ti...  24.5 us
    ppermute x7, starting transfers between devices, moved(): lax.ppermute(value, axis, [(i, (i + steps) % count) for i in range(count)])  13 us
    ppermute x7, waiting for transfers between devices, moved(): lax.ppermute(value, axis, [(i, (i + steps) % count) for i in range(count)])  11.3 us
    pallas_call x1, Pallas kernels, pack_cols(): pl.pallas_call(functools.partial(cols_kernel, pairs=pairs, tiles=tiles, b...  4.43 us
    pallas_call x1, Pallas kernels, pack_rows(): pl.pallas_call(functools.partial(rows_kernel, pairs=pairs, tiles=tiles),...  3.41 us
    pallas_call x1, Pallas kernels, place_cycle(): pl.pallas_call(functools.partial(place_kernel, slots=len(rotor) + 2, rows...  2.39 us
    unnamed x20, local copies, waits for them, and re-layouts  2.33 us
    pallas_call x1, Pallas kernels, place_edges(): pl.pallas_call(functools.partial(place_edges_kernel, slots=slots, rows=ro...  1.63 us
  transfers between devices with their start and end apart: 7, of which 2 were waited for; matrix products, arithmetic and copies ran while one was open for 0% of the time, Pallas kernels for 6%

profile of v8, /device:TPU:0, one launch (start us, length us, event | category | flops | bytes accessed | tf_op | source)
XLA Modules:
  0.0 63.1 jit_solution(13635456536585163280)
XLA Ops:
  0.0 4.4 %pack_cols.1 = (bf16[8,10,16,128]{3,2,1,0:T(8,128)(2,1)}, bf16[8,10,16,128]{3,2,1,0:T(8,128)(2,1)}) custom-call(f32[16,128,1024]{2,1,0:T(8,128)} %u_ref.1, f32[16,128,1024]{2,1,0:T(8,128)} %u_ref.1, bf16[16,128,1024]{2,1,0:T(8,128)(2,1)} %s_ref.1, bf16[16,128,1024]{2,1,0:T(8,128)(2,1)} %s_ref.1, bf16[16,128,1024]{2,1,0:T(8,128)(2,1)} %j_ref.1, ...), custom_call_target="tpu_custom_call" | custom-call | bytes 16777216 | tf_op jit(solution)/shard_map/pack_cols/pallas_call | solution.py:141
  4.4 0.0 copy-start.9
  4.4 0.0 copy-start.6
  4.4 0.0 copy-start.2
  4.5 3.4 %pack_rows.1 = (bf16[2,8,16,1024]{3,2,1,0:T(8,128)(2,1)}, bf16[2,8,16,1024]{3,2,1,0:T(8,128)(2,1)}) custom-call(f32[16,128,1024]{2,1,0:T(8,128)} %u_ref.1, f32[16,128,1024]{2,1,0:T(8,128)} %u_ref.1, bf16[16,128,1024]{2,1,0:T(8,128)(2,1)} %s_ref.1, bf16[16,128,1024]{2,1,0:T(8,128)(2,1)} %s_ref.1, bf16[16,128,1024]{2,1,0:T(8,128)(2,1)} %j_ref.1, ...), custom_call_target="tpu_custom_call" | custom-call | bytes 12582912 | tf_op jit(solution)/shard_map/pack_rows/pallas_call | solution.py:122
  7.9 0.5 collective-permute-start.5
  8.3 4.0 %collective-permute-start.6 = (bf16[2,8,16,1024]{3,2,1,0:T(8,128)(2,1)}, bf16[2,8,16,1024]{3,2,1,0:T(8,128)(2,1)S(1)}, u32[]{:S(2)}, u32[]{:S(2)}) collective-permute-start(bf16[2,8,16,1024]{3,2,1,0:T(8,128)(2,1)} %get-tuple-element.16), channel_id=1, source_target_pairs={{0,7},{1,0},{2,1},{3,2},{4,3},{5,4},{6,5},{7,6},{8,15},{9,8},{10,9... | collective-permute-start | bytes 1572872 | tf_op jit(solution)/shard_map/ppermute | solution.py:423
  12.4 0.0 copy-done.9
  12.4 2.0 %collective-permute-start.1 = (bf16[8,10,16,128]{3,2,1,0:T(8,128)(2,1)S(1)}, bf16[8,10,16,128]{3,2,1,0:T(8,128)(2,1)S(1)}, u32[]{:S(2)}, u32[]{:S(2)}) collective-permute-start(bf16[8,10,16,128]{3,2,1,0:T(8,128)(2,1)S(1)} %copy-done.9), channel_id=1, source_target_pairs={{0,8},{8,16},{16,24},{24,0},{1,9},{9,17},{17,25},{25,1},{2,10},{10... | collective-permute-start | bytes 983048 | tf_op jit(solution)/shard_map/ppermute | solution.py:423
  14.4 0.0 copy-done.6
  14.4 1.0 %collective-permute-start.2 = (bf16[8,10,16,128]{3,2,1,0:T(8,128)(2,1)S(1)}, bf16[8,10,16,128]{3,2,1,0:T(8,128)(2,1)S(1)}, u32[]{:S(2)}, u32[]{:S(2)}) collective-permute-start(bf16[8,10,16,128]{3,2,1,0:T(8,128)(2,1)S(1)} %copy-done.6), channel_id=1, source_target_pairs={{0,24},{8,0},{16,8},{24,16},{1,25},{9,1},{17,9},{25,17},{2,26},{10... | collective-permute-start | bytes 983048 | tf_op jit(solution)/shard_map/ppermute | solution.py:423
  15.4 0.0 copy-done.2
  15.4 1.9 %collective-permute-start = (bf16[128,1024]{1,0:T(8,128)(2,1)S(1)}, bf16[128,1024]{1,0:T(8,128)(2,1)S(1)}, u32[]{:S(2)}, u32[]{:S(2)}) collective-permute-start(bf16[128,1024]{1,0:T(8,128)(2,1)S(1)} %copy-done.2), channel_id=1, source_target_pairs={{0,16},{8,24},{16,0},{24,8},{1,17},{9,25},{17,1},{25,9},{2,18},{10... | collective-permute-start | bytes 786440 | tf_op jit(solution)/shard_map/ppermute | solution.py:423
  17.3 9.8 %collective-permute-done.refs_1_.refs_5_ = bf16[128,1024]{1,0:T(8,128)(2,1)S(1)} collective-permute-done((bf16[128,1024]{1,0:T(8,128)(2,1)S(1)}, bf16[128,1024]{1,0:T(8,128)(2,1)S(1)}, u32[]{:S(2)}, u32[]{:S(2)}) %collective-permute-start) | collective-permute-done | bytes 262176 | tf_op jit(solution)/shard_map/ppermute | solution.py:423
  27.2 0.0 copy-start.3
  27.2 0.0 collective-permute-done.1.refs_2_.refs_6_.from_left
  27.2 0.0 copy-start
  27.2 1.5 %collective-permute-done.2.refs_3_.refs_7_.from_right = bf16[8,10,16,128]{3,2,1,0:T(8,128)(2,1)S(1)} collective-permute-done((bf16[8,10,16,128]{3,2,1,0:T(8,128)(2,1)S(1)}, bf16[8,10,16,128]{3,2,1,0:T(8,128)(2,1)S(1)}, u32[]{:S(2)}, u32[]{:S(2)}) %collective-permute-start.2) | collective-permute-done | bytes 327712 | tf_op jit(solution)/shard_map/ppermute | solution.py:423
  28.7 0.0 copy-done.3
  28.7 0.0 copy-done
  28.7 0.0 copy-start.1
  28.7 0.7 %copy-done.1 = bf16[8,10,16,128]{3,2,1,0:T(8,128)(2,1)} copy-done((bf16[8,10,16,128]{3,2,1,0:T(8,128)(2,1)}, bf16[8,10,16,128]{3,2,1,0:T(8,128)(2,1)S(1)}, u32[]{:S(2)}) %copy-start.1) | copy-done | bytes 327704
  29.4 1.6 %place_edges.1 = (bf16[13,16,128]{2,1,0:T(8,128)(2,1)}, bf16[13,16,128]{2,1,0:T(8,128)(2,1)}) custom-call(s32[128]{0:T(128)} %skew.3, bf16[128,1024]{1,0:T(8,128)(2,1)} %refs_0_.3, bf16[128,1024]{1,0:T(8,128)(2,1)} %copy-done.3, bf16[8,10,16,128]{3,2,1,0:T(8,128)(2,1)} %copy-done, bf16[8,10,16,128]{3,2,1,0:T(8,128)(2,1)} %copy-done.1, ...), custom_call_target="tpu_custom_call" | custom-call | bytes 1048576 | tf_op jit(solution)/shard_map/place_edges/pallas_call | solution.py:202
  31.0 0.0 collective-permute-start.3
  31.0 3.5 %collective-permute-start.4 = (bf16[13,16,128]{2,1,0:T(8,128)(2,1)}, bf16[13,16,128]{2,1,0:T(8,128)(2,1)S(1)}, u32[]{:S(2)}, u32[]{:S(2)}) collective-permute-start(bf16[13,16,128]{2,1,0:T(8,128)(2,1)} %get-tuple-element.13.refs_4_), channel_id=1, source_target_pairs={{0,7},{1,0},{2,1},{3,2},{4,3},{5,4},{6,5},{7,6},{8,15},{9,8},{10,9... | collective-permute-start | bytes 159752 | tf_op jit(solution)/shard_map/ppermute | solution.py:423
  34.6 2.4 %place_cycle.1.placed = bf16[9,128,128]{2,1,0:T(8,128)(2,1)} custom-call(s32[128]{0:T(128)} %skew.3, bf16[128,1024]{1,0:T(8,128)(2,1)} %refs_0_.3, bf16[128,1024]{1,0:T(8,128)(2,1)} %copy-done.3, bf16[8,10,16,128]{3,2,1,0:T(8,128)(2,1)} %copy-done, bf16[8,10,16,128]{3,2,1,0:T(8,128)(2,1)} %copy-done.1, bf16[13,16,128]{2,1,0:T(8,128)(2,1)} %get-tuple-element.13.refs_4_), custom_call_target="tpu_custom_call" | custom-call | bytes 4194304 | tf_op jit(solution)/shard_map/place_cycle/pallas_call | solution.py:232
  37.0 0.0 collective-permute-done.3.small_prev
  37.0 0.0 copy-start.7
  37.0 0.0 collective-permute-done.4.small_next
  37.0 0.0 copy-start.8
  37.0 0.0 collective-permute-done.5.from_prev
  37.0 0.0 copy-start.4
  37.0 0.0 collective-permute-done.6.from_next
  37.0 0.6 copy-done.7
  37.6 0.0 copy-done.8
  37.6 0.2 copy-done.4
  37.8 0.0 copy-start.5
  37.8 0.8 %copy-done.5 = bf16[2,8,16,1024]{3,2,1,0:T(8,128)(2,1)} copy-done((bf16[2,8,16,1024]{3,2,1,0:T(8,128)(2,1)}, bf16[2,8,16,1024]{3,2,1,0:T(8,128)(2,1)S(1)}, u32[]{:S(2)}) %copy-start.5) | copy-done | bytes 524312
  38.6 24.5 %relax.1 = f32[16,128,1024]{2,1,0:T(8,128)} custom-call(bf16[9,128,128]{2,1,0:T(8,128)(2,1)} %place_cycle.1.placed, bf16[13,16,128]{2,1,0:T(8,128)(2,1)} %copy-done.7, bf16[13,16,128]{2,1,0:T(8,128)(2,1)} %copy-done.8, bf16[8,10,16,128]{3,2,1,0:T(8,128)(2,1)} %copy-done, bf16[8,10,16,128]{3,2,1,0:T(8,128)(2,1)} %copy-done.1, ...), custom_call_target="tpu_custom_call" | custom-call | tf_op jit(solution)/shard_map/relax/pallas_call | solution.py:409
Async XLA Ops:
  4.4 7.9 %copy-start.9 = (bf16[8,10,16,128]{3,2,1,0:T(8,128)(2,1)S(1)}, bf16[8,10,16,128]{3,2,1,0:T(8,128)(2,1)}, u32[]{:S(2)}) copy-start(bf16[8,10,16,128]{3,2,1,0:T(8,128)(2,1)} %get-tuple-element.11) | copy-start | bytes 983044
  4.4 9.9 %copy-start.6 = (bf16[8,10,16,128]{3,2,1,0:T(8,128)(2,1)S(1)}, bf16[8,10,16,128]{3,2,1,0:T(8,128)(2,1)}, u32[]{:S(2)}) copy-start(bf16[8,10,16,128]{3,2,1,0:T(8,128)(2,1)} %get-tuple-element.12.after) | copy-start | bytes 983044
  4.4 10.9 %copy-start.2 = (bf16[128,1024]{1,0:T(8,128)(2,1)S(1)}, bf16[128,1024]{1,0:T(8,128)(2,1)}, u32[]{:S(2)}) copy-start(bf16[128,1024]{1,0:T(8,128)(2,1)} %refs_0_.3) | copy-start | bytes 786436
  7.9 29.1 %collective-permute-start.5 = (bf16[2,8,16,1024]{3,2,1,0:T(8,128)(2,1)}, bf16[2,8,16,1024]{3,2,1,0:T(8,128)(2,1)S(1)}, u32[]{:S(2)}, u32[]{:S(2)}) collective-permute-start(bf16[2,8,16,1024]{3,2,1,0:T(8,128)(2,1)} %get-tuple-element.15), channel_id=1, source_target_pairs={{0,1},{1,2},{2,3},{3,4},{4,5},{5,6},{6,7},{7,0},{8,9},{9,10},{10,1... | collective-permute-start | bytes 1572872 | tf_op jit(solution)/shard_map/ppermute | solution.py:423
  8.3 28.7 %collective-permute-start.6 = (bf16[2,8,16,1024]{3,2,1,0:T(8,128)(2,1)}, bf16[2,8,16,1024]{3,2,1,0:T(8,128)(2,1)S(1)}, u32[]{:S(2)}, u32[]{:S(2)}) collective-permute-start(bf16[2,8,16,1024]{3,2,1,0:T(8,128)(2,1)} %get-tuple-element.16), channel_id=1, source_target_pairs={{0,7},{1,0},{2,1},{3,2},{4,3},{5,4},{6,5},{7,6},{8,15},{9,8},{10,9... | collective-permute-start | bytes 1572872 | tf_op jit(solution)/shard_map/ppermute | solution.py:423
  12.4 14.8 %collective-permute-start.1 = (bf16[8,10,16,128]{3,2,1,0:T(8,128)(2,1)S(1)}, bf16[8,10,16,128]{3,2,1,0:T(8,128)(2,1)S(1)}, u32[]{:S(2)}, u32[]{:S(2)}) collective-permute-start(bf16[8,10,16,128]{3,2,1,0:T(8,128)(2,1)S(1)} %copy-done.9), channel_id=1, source_target_pairs={{0,8},{8,16},{16,24},{24,0},{1,9},{9,17},{17,25},{25,1},{2,10},{10... | collective-permute-start | bytes 983048 | tf_op jit(solution)/shard_map/ppermute | solution.py:423
  14.4 14.3 %collective-permute-start.2 = (bf16[8,10,16,128]{3,2,1,0:T(8,128)(2,1)S(1)}, bf16[8,10,16,128]{3,2,1,0:T(8,128)(2,1)S(1)}, u32[]{:S(2)}, u32[]{:S(2)}) collective-permute-start(bf16[8,10,16,128]{3,2,1,0:T(8,128)(2,1)S(1)} %copy-done.6), channel_id=1, source_target_pairs={{0,24},{8,0},{16,8},{24,16},{1,25},{9,1},{17,9},{25,17},{2,26},{10... | collective-permute-start | bytes 983048 | tf_op jit(solution)/shard_map/ppermute | solution.py:423
  15.4 11.8 %collective-permute-start = (bf16[128,1024]{1,0:T(8,128)(2,1)S(1)}, bf16[128,1024]{1,0:T(8,128)(2,1)S(1)}, u32[]{:S(2)}, u32[]{:S(2)}) collective-permute-start(bf16[128,1024]{1,0:T(8,128)(2,1)S(1)} %copy-done.2), channel_id=1, source_target_pairs={{0,16},{8,24},{16,0},{24,8},{1,17},{9,25},{17,1},{25,9},{2,18},{10... | collective-permute-start | bytes 786440 | tf_op jit(solution)/shard_map/ppermute | solution.py:423
  27.2 1.5 %copy-start.3 = (bf16[128,1024]{1,0:T(8,128)(2,1)}, bf16[128,1024]{1,0:T(8,128)(2,1)S(1)}, u32[]{:S(2)}) copy-start(bf16[128,1024]{1,0:T(8,128)(2,1)S(1)} %collective-permute-done.refs_1_.refs_5_) | copy-start | bytes 786436
  27.2 1.5 %copy-start = (bf16[8,10,16,128]{3,2,1,0:T(8,128)(2,1)}, bf16[8,10,16,128]{3,2,1,0:T(8,128)(2,1)S(1)}, u32[]{:S(2)}) copy-start(bf16[8,10,16,128]{3,2,1,0:T(8,128)(2,1)S(1)} %collective-permute-done.1.refs_2_.refs_6_.from_left) | copy-start | bytes 983044
  28.7 0.7 %copy-start.1 = (bf16[8,10,16,128]{3,2,1,0:T(8,128)(2,1)}, bf16[8,10,16,128]{3,2,1,0:T(8,128)(2,1)S(1)}, u32[]{:S(2)}) copy-start(bf16[8,10,16,128]{3,2,1,0:T(8,128)(2,1)S(1)} %collective-permute-done.2.refs_3_.refs_7_.from_right) | copy-start | bytes 983044
  31.0 5.9 %collective-permute-start.3 = (bf16[13,16,128]{2,1,0:T(8,128)(2,1)}, bf16[13,16,128]{2,1,0:T(8,128)(2,1)S(1)}, u32[]{:S(2)}, u32[]{:S(2)}) collective-permute-start(bf16[13,16,128]{2,1,0:T(8,128)(2,1)} %get-tuple-element.14), channel_id=1, source_target_pairs={{0,1},{1,2},{2,3},{3,4},{4,5},{5,6},{6,7},{7,0},{8,9},{9,10},{10,1... | collective-permute-start | bytes 159752 | tf_op jit(solution)/shard_map/ppermute | solution.py:423
  31.0 5.9 %collective-permute-start.4 = (bf16[13,16,128]{2,1,0:T(8,128)(2,1)}, bf16[13,16,128]{2,1,0:T(8,128)(2,1)S(1)}, u32[]{:S(2)}, u32[]{:S(2)}) collective-permute-start(bf16[13,16,128]{2,1,0:T(8,128)(2,1)} %get-tuple-element.13.refs_4_), channel_id=1, source_target_pairs={{0,7},{1,0},{2,1},{3,2},{4,3},{5,4},{6,5},{7,6},{8,15},{9,8},{10,9... | collective-permute-start | bytes 159752 | tf_op jit(solution)/shard_map/ppermute | solution.py:423
  37.0 0.6 copy-start.7
  37.0 0.6 copy-start.8
  37.0 0.8 %copy-start.4 = (bf16[2,8,16,1024]{3,2,1,0:T(8,128)(2,1)}, bf16[2,8,16,1024]{3,2,1,0:T(8,128)(2,1)S(1)}, u32[]{:S(2)}) copy-start(bf16[2,8,16,1024]{3,2,1,0:T(8,128)(2,1)S(1)} %collective-permute-done.5.from_prev) | copy-start | bytes 1572868
  37.8 0.8 %copy-start.5 = (bf16[2,8,16,1024]{3,2,1,0:T(8,128)(2,1)}, bf16[2,8,16,1024]{3,2,1,0:T(8,128)(2,1)S(1)}, u32[]{:S(2)}) copy-start(bf16[2,8,16,1024]{3,2,1,0:T(8,128)(2,1)S(1)} %collective-permute-done.6.from_next) | copy-start | bytes 1572868
